TPU v7x, 32 devices: a whole 2x2x4 slice. The times are simulated.
32 devices in a mesh: dp: 4 (over x, core), fsdp: 8 (over z, y).
Axes of the slice: x: 2, y: 2, z: 4, core: 2. Of those that a mesh axis runs over, the one named last changes fastest.
Arguments:
- tokens: bfloat16 [8192, 2048], P(('dp', 'fsdp')), may hold values from -6 to 6
- cotangent: bfloat16 [8192, 2048], P(('dp', 'fsdp')), may hold values from -6 to 6
- w_in: bfloat16 [2048, 12288], P(('dp', 'fsdp')), may hold values from -0.125 to 0.125
- w_out: bfloat16 [4096, 2048], P(('dp', 'fsdp')), may hold values from -0.1875 to 0.1875
- w_up: bfloat16 [2048, 4096], P(('dp', 'fsdp')), may hold values from -0.125 to 0.125
- w_down: bfloat16 [4096, 2048], P(('dp', 'fsdp')), may hold values from -0.125 to 0.125
- ln1_gain: bfloat16 [2048], P(('dp', 'fsdp')), may hold values from 0.099609375 to 1.8984375
- ln1_bias: bfloat16 [2048], P(('dp', 'fsdp')), may hold values from -1.5 to 1.5
- group_gain: bfloat16 [4096], P(('dp', 'fsdp')), may hold values from 0.099609375 to 1.8984375
- ln2_gain: bfloat16 [2048], P(('dp', 'fsdp')), may hold values from 0.099609375 to 1.8984375
- ln2_bias: bfloat16 [2048], P(('dp', 'fsdp')), may hold values from -1.5 to 1.5
- seq_lens: int32 [64], replicated, may hold values from 0 to 256, as said below
- seq_owner: int32 [64], replicated, may hold values from 0 to 31, as said below
- seq_offset: int32 [64], replicated, may hold values from 0 to 256, as said below
Outputs:
- output: bfloat16 [8192, 2048], P(('dp', 'fsdp'))
- d_tokens: bfloat16 [8192, 2048], P(('dp', 'fsdp'))
- d_w_in: float32 [2048, 12288], P(('dp', 'fsdp'))
- d_w_out: float32 [4096, 2048], P(('dp', 'fsdp'))
- d_w_up: float32 [2048, 4096], P(('dp', 'fsdp'))
- d_w_down: float32 [4096, 2048], P(('dp', 'fsdp'))
- d_ln1_gain: float32 [2048], P(('dp', 'fsdp'))
- d_ln1_bias: float32 [2048], P(('dp', 'fsdp'))
- d_group_gain: float32 [4096], P(('dp', 'fsdp'))
- d_ln2_gain: float32 [2048], P(('dp', 'fsdp'))
- d_ln2_bias: float32 [2048], P(('dp', 'fsdp'))
Inputs may be any that keep to these rules, and one draw needn't show every extreme that they name: `seq_lens`: length 0 marks an unused entry; every other entry is one whole sequence of 128 to 256 tokens, and some sequence has exactly 256. Each device is named by exactly 2 entries, one or both used, and its used sequences lie end to end from position 0 of its buffer. `seq_owner`: the device, as an index over dp+fsdp, whose buffer holds the entry. `seq_offset`: where the entry begins in its device's buffer; an unused entry begins where that device's used positions end.
All inputs are finite; a program needn't handle non-finite values.
Results may differ from a plain program's by a relative error of at most 0.014.
Values may be sent and summed in bfloat16 or wider, within the bound.
A program may use at most 448 MiB of HBM per device.

v0:
```python
import jax
import jax.numpy as jnp
from jax import lax
from jax.sharding import PartitionSpec as P

HEADS = 8
QKH = 256
VH = 512


EPSILON = 1e-05
GROUP_EPSILON = 0.1


def layer_norm(values, gain_vec, bias_vec):
    center = values - jnp.mean(values, axis=-1, keepdims=True)
    spread = jnp.mean(center * center, axis=-1, keepdims=True)
    return center * lax.rsqrt(spread + EPSILON) * gain_vec + bias_vec


def layout(seq_lens, seq_owner, seq_offset, device_id, buffer_len):
    positions = jnp.arange(buffer_len, dtype=jnp.int32)[:, None]
    inside = (
        (seq_owner[None, :] == device_id)
        & (seq_lens[None, :] > 0)
        & (positions >= seq_offset[None, :])
        & (positions < seq_offset[None, :] + seq_lens[None, :])
    )
    number = jnp.arange(seq_lens.shape[0], dtype=jnp.int32)[None, :] + 1
    seq_ident = jnp.sum(jnp.where(inside, number, 0), axis=1) - 1
    starts = jnp.sum(jnp.where(inside, seq_offset[None, :], 0), axis=1)
    places = jnp.where(seq_ident >= 0, positions[:, 0] - starts, 0)
    return (seq_ident, places)


def rotation(places, head_size):
    half_size = head_size // 2
    pair_index = jnp.arange(half_size, dtype=jnp.float32) / half_size
    inverse_freq = 10000.0 ** (-pair_index)
    zeta_base = (pair_index + 0.4) / 1.4
    offsets = places.astype(jnp.float32)[:, None]
    angles = offsets * inverse_freq[None, :]
    growth = zeta_base[None, :] ** (offsets / 512.0)
    return (jnp.cos(angles), jnp.sin(angles), growth)


def rotate_xpos(vectors, cosine, sine_tab, scaling):
    half_size = vectors.shape[-1] // 2
    first_half = vectors[..., :half_size]
    second_half = vectors[..., half_size:]
    cos_tab = cosine[:, None, :]
    sin_tab = sine_tab[:, None, :]
    scale_tab = scaling[:, None, :]
    return jnp.concatenate(
        [
            (first_half * cos_tab - second_half * sin_tab) * scale_tab,
            (second_half * cos_tab + first_half * sin_tab) * scale_tab,
        ],
        axis=-1,
    )


def decay_mask(seq_ident, head_count):
    positions = jnp.arange(seq_ident.shape[0], dtype=jnp.int32)
    distance = positions[:, None] - positions[None, :]
    linked = (
        (distance >= 0) & (seq_ident[:, None] == seq_ident[None, :]) & (seq_ident[:, None] >= 0)
    )
    log_rates = jnp.log1p(-(2.0 ** (-5.0 - jnp.arange(head_count, dtype=jnp.float32))))
    powers = jnp.maximum(distance, 0).astype(jnp.float32)
    return jnp.where(linked[None], jnp.exp(log_rates[:, None, None] * powers[None]), 0.0)


def mixer_tail(mixed_out, gate_part, group_vec):
    center = mixed_out - jnp.mean(mixed_out, axis=-1, keepdims=True)
    spread = jnp.mean(center * center, axis=-1, keepdims=True)
    normal = (
        center
        * lax.rsqrt(spread + GROUP_EPSILON)
        * group_vec.reshape(mixed_out.shape[1], mixed_out.shape[2])
    )
    return jax.nn.silu(gate_part) * normal.reshape(mixed_out.shape[0], -1)


def exact_gelu(values):
    return jax.nn.gelu(values, approximate=False)


def inner_rows(left_mat, right_mat):
    return lax.dot_general(
        left_mat, right_mat, (((0,), (0,)), ((), ())), preferred_element_type=jnp.float32
    )


def times_transposed(left_mat, right_mat):
    return lax.dot_general(
        left_mat, right_mat, (((1,), (1,)), ((), ())), preferred_element_type=jnp.float32
    )


def local(
    tokens,
    cotangent,
    w_in,
    w_out,
    w_up,
    w_down,
    ln1_gain,
    ln1_bias,
    group_gain,
    ln2_gain,
    ln2_bias,
    seq_lens,
    seq_owner,
    seq_offset,
):
    row_count = tokens.shape[0]
    key_width = HEADS * QKH
    value_width = HEADS * VH
    seq_ident, places = layout(
        seq_lens, seq_owner, seq_offset, lax.axis_index(("dp", "fsdp")), row_count
    )
    valid_rows = (seq_ident >= 0).astype(jnp.float32)[:, None]
    full_in, full_out, gain_one, bias_one, gain_group = (
        lax.all_gather(w_in, ("dp", "fsdp"), axis=0, tiled=True),
        lax.all_gather(w_out, ("dp", "fsdp"), axis=0, tiled=True),
        lax.all_gather(ln1_gain, ("dp", "fsdp"), axis=0, tiled=True),
        lax.all_gather(ln1_bias, ("dp", "fsdp"), axis=0, tiled=True),
        lax.all_gather(group_gain, ("dp", "fsdp"), axis=0, tiled=True),
    )
    tok_rows = tokens.astype(jnp.float32)
    normed, pull_one = jax.vjp(
        layer_norm, tok_rows, gain_one.astype(jnp.float32), bias_one.astype(jnp.float32)
    )
    normed_low = normed.astype(jnp.bfloat16)
    project = jnp.dot(normed_low, full_in, preferred_element_type=jnp.float32)
    cosine, sine_tab, growth = rotation(places, QKH)

    def rotate_query(raw_part):
        return rotate_xpos(
            raw_part.reshape(row_count, HEADS, QKH), cosine, sine_tab, growth
        ) * QKH ** (-0.5)

    def rotate_keys(raw_part):
        return rotate_xpos(raw_part.reshape(row_count, HEADS, QKH), cosine, sine_tab, 1.0 / growth)

    query_rot, pull_query = jax.vjp(rotate_query, project[:, :key_width])
    key_rot, pull_keys = jax.vjp(rotate_keys, project[:, key_width : 2 * key_width])
    query_low = query_rot.astype(jnp.bfloat16)
    key_low = key_rot.astype(jnp.bfloat16)
    value_low = (
        project[:, 2 * key_width : 2 * key_width + value_width]
        .reshape(row_count, HEADS, VH)
        .astype(jnp.bfloat16)
    )
    gate_part = project[:, 2 * key_width + value_width :]
    decay_table = decay_mask(seq_ident, HEADS)
    raw_scores = jnp.einsum("thd,shd->hts", query_low, key_low, preferred_element_type=jnp.float32)
    masked_low = (raw_scores * decay_table).astype(jnp.bfloat16)
    mixed_out = jnp.einsum(
        "hts,shv->thv", masked_low, value_low, preferred_element_type=jnp.float32
    )
    gated_out, pull_tail = jax.vjp(mixer_tail, mixed_out, gate_part, gain_group.astype(jnp.float32))
    gated_low = gated_out.astype(jnp.bfloat16)
    hidden = tok_rows + jnp.dot(gated_low, full_out, preferred_element_type=jnp.float32)
    full_up, full_down, gain_two, bias_two = (
        lax.all_gather(w_up, ("dp", "fsdp"), axis=0, tiled=True),
        lax.all_gather(w_down, ("dp", "fsdp"), axis=0, tiled=True),
        lax.all_gather(ln2_gain, ("dp", "fsdp"), axis=0, tiled=True),
        lax.all_gather(ln2_bias, ("dp", "fsdp"), axis=0, tiled=True),
    )
    normed_two, pull_two = jax.vjp(
        layer_norm, hidden, gain_two.astype(jnp.float32), bias_two.astype(jnp.float32)
    )
    two_low = normed_two.astype(jnp.bfloat16)
    upper_part = jnp.dot(two_low, full_up, preferred_element_type=jnp.float32)
    active, pull_gelu = jax.vjp(exact_gelu, upper_part)
    active_low = active.astype(jnp.bfloat16)
    down_part = jnp.dot(active_low, full_down, preferred_element_type=jnp.float32)
    output = ((hidden + down_part) * valid_rows).astype(jnp.bfloat16)
    seed_grad = cotangent.astype(jnp.float32) * valid_rows
    seed_low = seed_grad.astype(jnp.bfloat16)
    back_up, back_down = (
        lax.all_gather(w_up, ("dp", "fsdp"), axis=0, tiled=True),
        lax.all_gather(w_down, ("dp", "fsdp"), axis=0, tiled=True),
    )
    d_active = times_transposed(seed_low, back_down)
    (d_upper,) = pull_gelu(d_active)
    upper_low = d_upper.astype(jnp.bfloat16)
    d_two = times_transposed(upper_low, back_up)
    d_hidden_norm, d_gain_two, d_bias_two = pull_two(d_two)
    d_hidden = seed_grad + d_hidden_norm
    branch_low = d_hidden.astype(jnp.bfloat16)
    grad_up, grad_down = (
        lax.psum_scatter(
            inner_rows(two_low, upper_low), ("dp", "fsdp"), scatter_dimension=0, tiled=True
        ),
        lax.psum_scatter(
            inner_rows(active_low, seed_low), ("dp", "fsdp"), scatter_dimension=0, tiled=True
        ),
    )
    back_in, back_out = (
        lax.all_gather(w_in, ("dp", "fsdp"), axis=0, tiled=True),
        lax.all_gather(w_out, ("dp", "fsdp"), axis=0, tiled=True),
    )
    d_gated = times_transposed(branch_low, back_out)
    d_mixed, d_gate, d_gain_group = pull_tail(d_gated)
    mixed_low = d_mixed.astype(jnp.bfloat16)
    d_values = jnp.einsum("hts,thv->shv", masked_low, mixed_low, preferred_element_type=jnp.float32)
    d_masked = jnp.einsum("thv,shv->hts", mixed_low, value_low, preferred_element_type=jnp.float32)
    scores_low = (d_masked * decay_table).astype(jnp.bfloat16)
    d_query_rot = jnp.einsum(
        "hts,shd->thd", scores_low, key_low, preferred_element_type=jnp.float32
    )
    d_key_rot = jnp.einsum(
        "hts,thd->shd", scores_low, query_low, preferred_element_type=jnp.float32
    )
    (d_query,) = pull_query(d_query_rot)
    (d_keys,) = pull_keys(d_key_rot)
    project_low = jnp.concatenate(
        [d_query, d_keys, d_values.reshape(row_count, value_width), d_gate], axis=1
    ).astype(jnp.bfloat16)
    d_normed = times_transposed(project_low, back_in)
    d_rows, d_gain_one, d_bias_one = pull_one(d_normed)
    d_tokens = (d_hidden + d_rows).astype(jnp.bfloat16)
    grad_in, grad_out, grad_gain_one, grad_bias_one, grad_group, grad_gain_two, grad_bias_two = (
        lax.psum_scatter(
            inner_rows(normed_low, project_low), ("dp", "fsdp"), scatter_dimension=0, tiled=True
        ),
        lax.psum_scatter(
            inner_rows(gated_low, branch_low), ("dp", "fsdp"), scatter_dimension=0, tiled=True
        ),
        lax.psum_scatter(d_gain_one, ("dp", "fsdp"), scatter_dimension=0, tiled=True),
        lax.psum_scatter(d_bias_one, ("dp", "fsdp"), scatter_dimension=0, tiled=True),
        lax.psum_scatter(d_gain_group, ("dp", "fsdp"), scatter_dimension=0, tiled=True),
        lax.psum_scatter(d_gain_two, ("dp", "fsdp"), scatter_dimension=0, tiled=True),
        lax.psum_scatter(d_bias_two, ("dp", "fsdp"), scatter_dimension=0, tiled=True),
    )
    return (
        output,
        d_tokens,
        grad_in,
        grad_out,
        grad_up,
        grad_down,
        grad_gain_one,
        grad_bias_one,
        grad_group,
        grad_gain_two,
        grad_bias_two,
    )


def solution(mesh):
    placed = (
        P(("dp", "fsdp"), None),
        P(("dp", "fsdp"), None),
        P(("dp", "fsdp"), None),
        P(("dp", "fsdp"), None),
        P(("dp", "fsdp"), None),
        P(("dp", "fsdp"), None),
        P(("dp", "fsdp")),
        P(("dp", "fsdp")),
        P(("dp", "fsdp")),
        P(("dp", "fsdp")),
        P(("dp", "fsdp")),
        P(),
        P(),
        P(),
    )
    return jax.shard_map(
        local,
        mesh=mesh,
        in_specs=placed,
        out_specs=(
            P(("dp", "fsdp"), None),
            P(("dp", "fsdp"), None),
            P(("dp", "fsdp"), None),
            P(("dp", "fsdp"), None),
            P(("dp", "fsdp"), None),
            P(("dp", "fsdp"), None),
            P(("dp", "fsdp")),
            P(("dp", "fsdp")),
            P(("dp", "fsdp")),
            P(("dp", "fsdp")),
            P(("dp", "fsdp")),
        ),
        check_vma=False,
    )
```

profile of v0, /device:TPU:1, one launch (start us, length us, event | category | flops | bytes accessed | tf_op | source)
XLA Modules:
  0.0 3651.5 jit_solution(3395002578691650220)
XLA Ops:
  13.4 44.3 %all-reduce.14 = (bf16[2048]{0:T(1024)(128)(2,1)S(1)}, bf16[2048]{0:T(1024)(128)(2,1)S(1)}, bf16[2048]{0:T(1024)(128)(2,1)S(1)}, bf16[2048]{0:T(1024)(128)(2,1)S(1)}) all-reduce(bf16[2048]{0:T(1024)(128)(2,1)S(1)} %dynamic-update-slice.1, bf16[2048]{0:T(1024)(128)(2,1)S(1)} %dynamic-update-slice, ...), channel_id=1, replica_groups=mesh['dp'=4,'fsdp'=8] {'dp','fsdp'}, use_global_device_ids=true, to_apply=%add.5 | all-reduce | flops 8192 | bytes 32768
  57.8 60.6 %all-gather = bf16[32,1,128]{2,1,0:T(2,128)(2,1)S(1)} all-gather(bf16[1,1,128]{2,1,0:T(2,128)(2,1)} %bitcast.82), channel_id=1, replica_groups=mesh['dp'=4,'fsdp'=8] {'dp','fsdp'}, dimensions={0}, use_global_device_ids=true | all-gather | bytes 8448 | tf_op jit(solution)/shard_map/all_gather | solution.py:129
  122.9 167.1 %all-gather.6.cloned.1.call-done = bf16[2048,12288]{1,0:T(8,128)(2,1)} async-done(((bf16[64,12288]{1,0:T(8,128)(2,1)}), bf16[2048,12288]{1,0:T(8,128)(2,1)}) %all-gather.6.cloned.1.call-update) | async-done | bytes 50331664 | tf_op jit(solution)/shard_map/all_gather | solution.py:125
  290.1 25.4 fusion.65
  318.0 3.5 fusion.74
  327.4 2.8 multiply_multiply_fusion.5
  330.2 5.7 copy.81
  335.9 6.1 multiply_convert_fusion.1
  342.1 64.2 %all-gather.8.cloned.1.call-done = bf16[4096,2048]{1,0:T(8,128)(2,1)} async-done(((bf16[128,2048]{1,0:T(8,128)(2,1)}), bf16[4096,2048]{1,0:T(8,128)(2,1)}) %all-gather.8.cloned.1.call-update) | async-done | bytes 16777232 | tf_op jit(solution)/shard_map/all_gather | solution.py:126
  406.2 9.3 fusion.77
  416.0 106.4 %all-gather.10.cloned.1.call-done = bf16[2048,4096]{1,0:T(8,128)(2,1)} async-done(((bf16[64,4096]{1,0:T(8,128)(2,1)}), bf16[2048,4096]{1,0:T(8,128)(2,1)}) %all-gather.10.cloned.1.call-update) | async-done | bytes 16777232 | tf_op jit(solution)/shard_map/all_gather | solution.py:167
  522.4 10.3 fusion.69
  532.7 105.8 %all-gather.12.cloned.1.call-done = bf16[4096,2048]{1,0:T(8,128)(2,1)} async-done(((bf16[128,2048]{1,0:T(8,128)(2,1)}), bf16[4096,2048]{1,0:T(8,128)(2,1)}) %all-gather.12.cloned.1.call-update) | async-done | bytes 16777232 | tf_op jit(solution)/shard_map/all_gather | solution.py:168
  638.4 19.0 add_convert_fusion.1
  657.4 13.4 multiply_reduce_fusion.3
  675.0 13.2 fusion.78
  688.2 15.2 fusion.68
  704.6 21.0 fusion.39
  725.6 13.4 fusion.38
  739.1 5.6 copy.83
  744.7 5.9 multiply_reduce_fusion
  757.1 2.9 copy.82
  760.1 4.1 multiply_convert_fusion.2
  768.5 38.1 %fusion.34 = f32[2048,12288]{1,0:T(8,128)} fusion(bf16[256,4096]{1,0:T(8,128)(2,1)} %get-tuple-element.40, bf16[256,4096]{1,0:T(8,128)(2,1)S(1)} %copy.82, bf16[256,2048]{1,0:T(8,128)(2,1)} %bitcast.76, bf16[256,2048]{1,0:T(8,128)(2,1)} %bitcast.78, bf16[256,2048]{1,0:T(8,128)(2,1)S(1)} %copy-done.4, f32[2048]{0:T(1024)S(1)} %copy-done.35, ...), kind=kOutput, calls=%fused_computation.78 | convolution fusion | flops 12913213440 | bytes 108021760 | tf_op jit(solution)/shard_map/dot_general | solution.py:90
  806.6 23.9 fusion.70
  833.1 51.3 %all-reduce.13 = (f32[2048]{0:T(1024)S(1)}, f32[2048]{0:T(1024)S(1)}, f32[4096]{0:T(1024)S(1)}, f32[2048]{0:T(1024)S(1)}, f32[2048]{0:T(1024)S(1)}) all-reduce(f32[2048]{0:T(1024)S(1)} %get-tuple-element.15, f32[2048]{0:T(1024)S(1)} %get-tuple-element.18, ...), channel_id=6, replica_groups=mesh['dp'=4,'fsdp'=8] {'dp','fsdp'}, use_global_device_ids=true, to_apply=%region_19.20.clone | all-reduce | flops 12288 | bytes 98304
  887.4 4.6 add_convert_fusion.2
  892.0 16.9 fusion.15
  908.9 484.6 %reduce-scatter.7.cloned.1.call-done = f32[128,2048]{1,0:T(8,128)} async-done(((f32[4096,2048]{1,0:T(8,128)}), f32[128,2048]{1,0:T(8,128)}) %reduce-scatter.7.cloned.1.call-update) | async-done | bytes 1048592 | tf_op jit(solution)/shard_map/reduce_scatter | solution.py:230
  1393.4 708.7 %reduce-scatter.9.cloned.1.call-done = f32[64,4096]{1,0:T(8,128)} async-done(((f32[2048,4096]{1,0:T(8,128)}), f32[64,4096]{1,0:T(8,128)}) %reduce-scatter.9.cloned.1.call-update) | async-done | bytes 1048592 | tf_op jit(solution)/shard_map/reduce_scatter | solution.py:195
  2102.1 708.8 %reduce-scatter.11.cloned.1.call-done = f32[128,2048]{1,0:T(8,128)} async-done(((f32[4096,2048]{1,0:T(8,128)}), f32[128,2048]{1,0:T(8,128)}) %reduce-scatter.11.cloned.1.call-update) | async-done | bytes 1048592 | tf_op jit(solution)/shard_map/reduce_scatter | solution.py:198
  2810.9 833.6 %reduce-scatter.5.cloned.1.call-done = f32[64,12288]{1,0:T(8,128)} async-done(((f32[2048,12288]{1,0:T(8,128)}), f32[64,12288]{1,0:T(8,128)}) %reduce-scatter.5.cloned.1.call-update) | async-done | bytes 3145744 | tf_op jit(solution)/shard_map/reduce_scatter | solution.py:227
  (207 shorter events, 40.6 us)
Async XLA Ops:
  7.2 113.6 %copy-start.3 = (bf16[256,2048]{1,0:T(8,128)(2,1)S(1)}, bf16[256,2048]{1,0:T(8,128)(2,1)}, u32[]{:S(2)}) copy-start(bf16[256,2048]{1,0:T(8,128)(2,1)} %param.14) | copy-start | bytes 3145732
  7.2 282.9 %all-gather.6.cloned.1.call-start = ((), (), s32[]{:S(2)}) async-start(), calls=%async_computation.4 | async-start | bytes 51904512 | tf_op jit(solution)/shard_map/all_gather | solution.py:125
  7.9 398.3 %all-gather.8.cloned.1.call-start = ((), (), s32[]{:S(2)}) async-start(), calls=%async_computation.5 | async-start | bytes 17301504 | tf_op jit(solution)/shard_map/all_gather | solution.py:126
  8.7 513.7 %all-gather.10.cloned.1.call-start = ((), (), s32[]{:S(2)}) async-start(), calls=%async_computation.6 | async-start | bytes 17301504 | tf_op jit(solution)/shard_map/all_gather | solution.py:167
  9.4 629.0 %all-gather.12.cloned.1.call-start = ((), (), s32[]{:S(2)}) async-start(), calls=%async_computation.7 | async-start | bytes 17301504 | tf_op jit(solution)/shard_map/all_gather | solution.py:168
  10.0 1383.4 %reduce-scatter.7.cloned.1.call-start = ((), (), s32[]{:S(2)}) async-start(), calls=%async_computation.9 | async-start | bytes 34603008 | tf_op jit(solution)/shard_map/reduce_scatter | solution.py:230
  57.8 257.7 %copy-start.34 = (f32[2048]{0:T(1024)}, f32[2048]{0:T(1024)S(1)}, u32[]{:S(2)}) copy-start(f32[2048]{0:T(1024)S(1)} %convert_element_type.92) | copy-start | bytes 24580
  57.8 257.7 %copy-start.32 = (f32[2048]{0:T(1024)}, f32[2048]{0:T(1024)S(1)}, u32[]{:S(2)}) copy-start(f32[2048]{0:T(1024)S(1)} %convert_element_type.91) | copy-start | bytes 24580
  118.5 208.9 %copy-start.40 = (f32[8,512]{1,0:T(8,128)}, f32[8,512]{1,0:T(8,128)S(1)}, u32[]{:S(2)}) copy-start(f32[8,512]{1,0:T(8,128)S(1)} %reshape.376) | copy-start | bytes 49156
  119.2 205.5 %copy-start.58 = (f32[8]{0:T(128)}, f32[8]{0:T(128)S(1)}, u32[]{:S(2)}) copy-start(f32[8]{0:T(128)S(1)} %negate_log-plus-one_fusion) | copy-start | bytes 100
  120.8 204.0 %copy-start.42 = (f32[256,256]{1,0:T(8,128)}, f32[256,256]{1,0:T(8,128)S(1)}, u32[]{:S(2)}) copy-start(f32[256,256]{1,0:T(8,128)S(1)} %maximum_convert_fusion) | copy-start | bytes 786436
  121.0 194.5 %copy-start.36 = (f32[256]{0:T(256)}, f32[256]{0:T(256)S(1)}, u32[]{:S(2)}) copy-start(f32[256]{0:T(256)S(1)} %broadcast_multiply_fusion.3) | copy-start | bytes 3076
  121.5 194.0 %copy-start.38 = (f32[256]{0:T(256)}, f32[256]{0:T(256)S(1)}, u32[]{:S(2)}) copy-start(f32[256]{0:T(256)S(1)} %fusion.53) | copy-start | bytes 3076
  122.0 202.7 %copy-start.50 = (pred[256,256]{1,0:T(8,128)(4,1)}, pred[256,256]{1,0:T(8,128)(4,1)S(1)}, u32[]{:S(2)}) copy-start(pred[256,256]{1,0:T(8,128)(4,1)S(1)} %fusion.47) | copy-start | bytes 196612
  122.9 200.9 %copy-start.24 = (f32[256,128]{1,0:T(8,128)}, f32[256,128]{1,0:T(8,128)S(1)}, u32[]{:S(2)}) copy-start(f32[256,128]{1,0:T(8,128)S(1)} %get-tuple-element.59) | copy-start | bytes 393220
  122.9 200.9 %copy-start.26 = (f32[256,128]{1,0:T(8,128)}, f32[256,128]{1,0:T(8,128)S(1)}, u32[]{:S(2)}) copy-start(f32[256,128]{1,0:T(8,128)S(1)} %get-tuple-element.60) | copy-start | bytes 393220
  122.9 200.9 %copy-start.28 = (f32[256,128]{1,0:T(8,128)}, f32[256,128]{1,0:T(8,128)S(1)}, u32[]{:S(2)}) copy-start(f32[256,128]{1,0:T(8,128)S(1)} %get-tuple-element.69) | copy-start | bytes 393220
  122.9 200.9 %copy-start.30 = (f32[256,128]{1,0:T(8,128)}, f32[256,128]{1,0:T(8,128)S(1)}, u32[]{:S(2)}) copy-start(f32[256,128]{1,0:T(8,128)S(1)} %get-tuple-element.70) | copy-start | bytes 393220
  318.0 8.0 copy-start.10
  415.6 272.6 %copy-start.5 = (f32[256,2048]{1,0:T(8,128)}, f32[256,2048]{1,0:T(8,128)S(1)}, u32[]{:S(2)}) copy-start(f32[256,2048]{1,0:T(8,128)S(1)} %get-tuple-element.66) | copy-start | bytes 6291460
  416.0 222.4 %copy-start.15 = (bf16[256,2048]{1,0:T(8,128)(2,1)S(1)}, bf16[256,2048]{1,0:T(8,128)(2,1)}, u32[]{:S(2)}) copy-start(bf16[256,2048]{1,0:T(8,128)(2,1)} %param.15) | copy-start | bytes 3145732
  673.2 14.9 copy-start.54
  688.1 1414.0 %reduce-scatter.9.cloned.1.call-start = ((), (), s32[]{:S(2)}) async-start(), calls=%async_computation.10 | async-start | bytes 34603008 | tf_op jit(solution)/shard_map/reduce_scatter | solution.py:195
  703.4 2107.5 %reduce-scatter.11.cloned.1.call-start = ((), (), s32[]{:S(2)}) async-start(), calls=%async_computation.11 | async-start | bytes 34603008 | tf_op jit(solution)/shard_map/reduce_scatter | solution.py:198
  725.6 2918.9 %reduce-scatter.5.cloned.1.call-start = ((), (), s32[]{:S(2)}) async-start(), calls=%async_computation.8 | async-start | bytes 103809024 | tf_op jit(solution)/shard_map/reduce_scatter | solution.py:227
  744.7 7.2 copy-start.2
  806.6 23.9 copy-start.53
  806.6 26.5 copy-start.56
  806.6 26.5 copy-start.57
  806.6 80.7 %copy-start.55 = (f32[256]{0:T(256)S(1)}, f32[256]{0:T(256)}, u32[]{:S(2)}) copy-start(f32[256]{0:T(256)} %copy-done.54) | copy-start | bytes 3076
  833.1 58.9 %copy-start.6 = (f32[256,2048]{1,0:T(8,128)S(1)}, f32[256,2048]{1,0:T(8,128)}, u32[]{:S(2)}) copy-start(f32[256,2048]{1,0:T(8,128)} %copy-done.5) | copy-start | bytes 6291460
  884.4 7.6 copy-start.60
  (37 other events, 113.7 us)
Sparse Core Ops, SparseCore 0:
  10.9 279.1 all-gather.5
  293.2 113.0 all-gather.7
  409.3 113.0 all-gather.9
  525.3 113.0 all-gather.11
  688.3 705.1 reduce-scatter.6
  1396.2 705.9 reduce-scatter.8
  2105.0 705.8 reduce-scatter.10
  2817.9 826.5 reduce-scatter.4
where the time goes:
time: 3660 us; the launch traced here: 3650 us
  waiting for transfers between devices  3180 us (87%)
  matrix products  227 us (6%)
  blocking collectives  156 us (4%)
  local copies, waits for them, and re-layouts  37.9 us (1%)
    reduce_scatter x1, waiting for transfers between devices, local(): lax.psum_scatter(inner_rows(normed_low, project_low), ('dp', 'fsdp'), sca...  834 us
    reduce_scatter x1, waiting for transfers between devices, local(): lax.psum_scatter(inner_rows(active_low, seed_low), ('dp', 'fsdp'), scatte...  709 us
    reduce_scatter x1, waiting for transfers between devices, local(): lax.psum_scatter(inner_rows(two_low, upper_low), ('dp', 'fsdp'), scatter_...  709 us
    reduce_scatter x1, waiting for transfers between devices, local(): lax.psum_scatter(inner_rows(gated_low, branch_low), ('dp', 'fsdp'), scatt...  485 us
    all_gather x1, waiting for transfers between devices, local(): lax.all_gather(w_in, ('dp', 'fsdp'), axis=0, tiled=True)  167 us
    all_gather x1, waiting for transfers between devices, local(): lax.all_gather(w_up, ('dp', 'fsdp'), axis=0, tiled=True)  106 us
    all_gather x1, waiting for transfers between devices, local(): lax.all_gather(w_down, ('dp', 'fsdp'), axis=0, tiled=True)  106 us
    unnamed x2, blocking collectives  95.6 us
  transfers between devices with their start and end apart: 8, of which 8 were waited for; matrix products, arithmetic and copies ran while one was open for 7% of the time, Pallas kernels for 0%

commit v1 on v0

v1 whole, which is shorter than its diff:
```python
import functools

import jax
import jax.numpy as jnp
from jax import lax
from jax.experimental import pallas as pl
from jax.experimental.pallas import tpu as pltpu
from jax.sharding import PartitionSpec as P

HEADS = 8
QKH = 256
VH = 512
EPSILON = 1e-05
GROUP_EPSILON = 0.1
GROUP = 4
MESH = pl.DeviceIdType.MESH
ANY = pl.ANY
BF16 = jnp.bfloat16
F32 = jnp.float32
MIB = 1 << 20


def ring_place(index, total):
    half = index // 2
    return jnp.where(index % 2 == 0, half, total - 1 - half)


def ring_index(place, total):
    place = lax.rem(place + 2 * total, total)
    return jnp.where(place < total // 2, 2 * place, 2 * (total - 1 - place) + 1)


def flip(group_index, relation):
    low, high = group_index % 2, group_index // 2
    if relation % 2:
        low = 1 - low
    if relation // 2:
        high = 1 - high
    return 2 * high + low


class Place:
    def __init__(self, total):
        self.total = total
        self.group = lax.axis_index("dp")
        self.inner = lax.axis_index("fsdp")
        self.place = ring_place(self.inner, total)
        self.next = (
            ring_index(self.place + 1, total),
            ring_index(self.place - 1, total),
        )

    def peer(self, relation):
        return (flip(self.group, relation), self.inner)

    def neighbour(self, way):
        return (self.group, self.next[way])

    def behind(self, way, steps):
        return ring_index(self.place - steps if way == 0 else self.place + steps, self.total)


def greet(devices):
    barrier = pltpu.get_barrier_semaphore()
    for device in devices:
        pl.semaphore_signal(barrier, inc=1, device_id=device, device_id_type=MESH)
    pl.semaphore_wait(barrier, len(devices))


def remote(src, dst, send_sem, recv_sem, device):
    return pltpu.make_async_remote_copy(
        src_ref=src,
        dst_ref=dst,
        send_sem=send_sem,
        recv_sem=recv_sem,
        device_id=device,
        device_id_type=MESH,
    )


def column_pieces(width_in):
    key = HEADS * QKH
    value = HEADS * VH
    qk, vv = key // GROUP, value // GROUP
    return (
        (0, qk, 0, qk),
        (key, qk, qk, qk),
        (2 * key, vv, 2 * qk, vv),
        (2 * key + value, vv, 2 * qk + vv, vv),
    )


def gather_kernel(
    total,
    w_in,
    w_up,
    w_out,
    w_down,
    tok,
    cot,
    vec,
    full_in,
    full_up,
    full_out,
    full_down,
    full_tok,
    full_cot,
    full_vec,
    a2a_send,
    a2a_recv,
    own_sem,
    ring_send,
    ring_recv,
):
    at = Place(total)
    me, inner = at.group, at.inner
    peers = [at.peer(r) for r in (1, 2, 3)]
    greet(peers + [at.neighbour(0), at.neighbour(1)])
    up_width = full_up.shape[-1]
    half_out = w_out.shape[0] // 2
    pieces = column_pieces(w_in.shape[1])

    def exchange(relation, slot):
        other = flip(me, relation)
        if slot < 4:
            base, stride, off, width = pieces[slot]
            start = pl.multiple_of(base + other * stride, 128)
            src = w_in.at[:, pl.ds(start, width)]
            dst = full_in.at[me, inner, :, pl.ds(off, width)]
        elif slot == 4:
            src = w_up.at[:, pl.ds(pl.multiple_of(other * up_width, 128), up_width)]
            dst = full_up.at[me, inner]
        elif slot == 5:
            src, dst = vec, full_vec.at[inner, me]
        elif slot == 6:
            src, dst = tok, full_tok.at[me]
        else:
            src, dst = cot, full_cot.at[me]
        if relation == 0:
            return pltpu.make_async_copy(src, dst, own_sem.at[slot])
        return remote(
            src,
            dst,
            a2a_send.at[relation - 1, slot],
            a2a_recv.at[relation - 1, slot],
            at.peer(relation),
        )

    def own_block(which):
        src, dst = ((w_out, full_out), (w_down, full_down))[which]
        rows = src.shape[0]
        return pltpu.make_async_copy(src, dst.at[inner], own_sem.at[8 + which])

    for relation in (1, 0, 2, 3):
        for slot in (0, 1, 2, 3):
            exchange(relation, slot).start()
    for relation in (1, 0, 2, 3):
        for slot in (5, 4):
            exchange(relation, slot).start()
    own_block(0).start()
    own_block(1).start()

    ways = ((0, 2), (1, 3))

    def block(item, way, which):
        if item < 2:
            return full_in.at[flip(me, ways[way][item]), which]
        if item < 4:
            return full_up.at[flip(me, ways[way][item - 2]), which]
        if item == 4:
            return full_vec.at[which]
        part = full_out if item == 5 else full_down
        return part.at[which, pl.ds(way * half_out, half_out)]

    def hop(item, way, step):
        which = at.behind(way, step)
        place = block(item, way, which)
        return remote(
            place, place, ring_send.at[item, way, step], ring_recv.at[item, way, step], at.neighbour(way)
        )

    def active(item, way):
        return not (item == 4 and way == 1)

    def first(item, way):
        if item < 4:
            relation = ways[way][item % 2]
            slots = (0, 1, 2, 3) if item < 2 else (4,)
            for slot in slots:
                copy = exchange(relation, slot)
                if relation == 0:
                    copy.wait()
                else:
                    copy.wait_recv()
        elif item == 4:
            for relation in range(4):
                copy = exchange(relation, 5)
                if relation == 0:
                    copy.wait()
                else:
                    copy.wait_recv()
        elif way == 0:
            own_block(item - 5).wait()
        hop(item, way, 0).start()

    groups = ((0, 1), (4, 5, 2, 3, 6))
    for number, group in enumerate(groups):
        for item in group:
            for way in (0, 1):
                if active(item, way):
                    first(item, way)
        if number == 0:
            for relation in (1, 0, 2, 3):
                for slot in (6, 7):
                    exchange(relation, slot).start()

        def onward(step, carry, group=group):
            for item in group:
                for way in (0, 1):
                    if active(item, way):
                        hop(item, way, step - 1).wait_recv()
                        hop(item, way, step).start()
            return carry

        lax.fori_loop(1, total - 1, onward, 0)

    for group in groups:
        for item in group:
            for way in (0, 1):
                if active(item, way):
                    hop(item, way, total - 2).wait_recv()

    def sent(step, carry):
        for group in groups:
            for item in group:
                for way in (0, 1):
                    if active(item, way):
                        hop(item, way, step).wait_send()
        return carry

    lax.fori_loop(0, total - 1, sent, 0)
    for relation in (1, 2, 3):
        for slot in range(8):
            exchange(relation, slot).wait_send()
            if slot >= 6:
                exchange(relation, slot).wait_recv()
    exchange(0, 6).wait()
    exchange(0, 7).wait()


def gather_all(total, w_in, w_up, w_out, w_down, tok, cot, vec):
    width = w_in.shape[1] // GROUP
    up_width = w_up.shape[1] // GROUP
    shapes = (
        ((GROUP, total, w_in.shape[0], width), BF16),
        ((GROUP, total, w_up.shape[0], up_width), BF16),
        ((total,) + w_out.shape, BF16),
        ((total,) + w_down.shape, BF16),
        ((GROUP,) + tok.shape, BF16),
        ((GROUP,) + cot.shape, BF16),
        ((total, GROUP) + vec.shape, F32),
    )
    return pl.pallas_call(
        functools.partial(gather_kernel, total),
        out_shape=[jax.ShapeDtypeStruct(s, d) for s, d in shapes],
        in_specs=[pl.BlockSpec(memory_space=ANY)] * 7,
        out_specs=[pl.BlockSpec(memory_space=ANY)] * 7,
        scratch_shapes=[
            pltpu.SemaphoreType.DMA((3, 8)),
            pltpu.SemaphoreType.DMA((3, 8)),
            pltpu.SemaphoreType.DMA((10,)),
            pltpu.SemaphoreType.DMA((7, 2, total - 1)),
            pltpu.SemaphoreType.DMA((7, 2, total - 1)),
        ],
        compiler_params=pltpu.CompilerParams(collective_id=0, has_side_effects=True),
        name="gather_weights",
    )(w_in, w_up, w_out, w_down, tok, cot, vec)


def norm_parts(values, epsilon):
    center = values - jnp.mean(values, axis=-1, keepdims=True)
    spread = jnp.mean(center * center, axis=-1, keepdims=True)
    scale = lax.rsqrt(spread + epsilon)
    return center * scale, scale


def exchange_kernel(total, chunks, backward, part, extra, hidden_in, gain, bias, *refs):
    if backward:
        (keep, full, sums, core_in, out_x, in_x, low, own_part, sends, recvs, own_sem) = refs
    else:
        (keep, full, core_in, out_x, in_x, low, own_part, sends, recvs, own_sem) = refs
    at = Place(total)
    me = at.group
    core, across = at.peer(1), at.peer(2)
    rows = low.shape[0] // chunks
    greet([core, across])
    mine, far = me, flip(me, 2)

    def rows_of(c):
        return pl.ds(c * rows, rows)

    def copy(kind, c):
        r = rows_of(c)
        if kind == 0:
            src, dst, dev = part.at[flip(me, 3), r], core_in.at[0, r], core
        elif kind == 1:
            src, dst, dev = part.at[flip(me, 1), r], core_in.at[1, r], core
        elif kind == 2:
            src, dst, dev = out_x.at[r], in_x.at[r], across
        elif kind == 3:
            src, dst, dev = low.at[r], full.at[me, r], across
        elif kind == 4:
            src, dst, dev = low.at[r], full.at[me, r], core
        else:
            src, dst, dev = full.at[far, r], full.at[far, r], core
        return remote(src, dst, sends.at[kind, c], recvs.at[kind, c], dev)

    def load(which, c):
        r = rows_of(c)
        source = far if which == 0 else mine
        return pltpu.make_async_copy(part.at[source, r], own_part.at[which, r], own_sem.at[which, c])

    def store(c):
        r = rows_of(c)
        return pltpu.make_async_copy(low.at[r], full.at[me, r], own_sem.at[2, c])

    for c in range(chunks):
        copy(0, c).start()
        load(0, c).start()
    for c in range(chunks):
        copy(1, c).start()
        load(1, c).start()
    for c in range(chunks):
        r = rows_of(c)
        load(0, c).wait()
        copy(0, c).wait_recv()
        out_x[r, :] = (own_part[0, r, :].astype(F32) + core_in[0, r, :].astype(F32)).astype(BF16)
        copy(2, c).start()
    if backward:
        sums[...] = jnp.zeros_like(sums)
    for c in range(chunks):
        r = rows_of(c)
        load(1, c).wait()
        copy(1, c).wait_recv()
        copy(2, c).wait_recv()
        total_rows = (
            own_part[1, r, :].astype(F32) + core_in[1, r, :].astype(F32) + in_x[r, :].astype(F32)
        )
        if backward:
            normal, scale = norm_parts(hidden_in[r, :], EPSILON)
            with_gain = total_rows * gain[...]
            both = with_gain * normal
            sums[0:1, :] += jnp.sum(total_rows * normal, axis=0, keepdims=True)
            sums[1:2, :] += jnp.sum(total_rows, axis=0, keepdims=True)
            result = extra[r, :].astype(F32) + scale * (
                with_gain
                - jnp.mean(with_gain, axis=-1, keepdims=True)
                - normal * jnp.mean(both, axis=-1, keepdims=True)
            )
            keep[r, :] = result
            low[r, :] = result.astype(BF16)
        else:
            hidden = extra[r, :].astype(F32) + total_rows
            keep[r, :] = hidden
            normal, scale = norm_parts(hidden, EPSILON)
            low[r, :] = (normal * gain[...] + bias[...]).astype(BF16)
        copy(3, c).start()
        copy(4, c).start()
        store(c).start()
    for c in range(chunks):
        copy(3, c).wait_recv()
        copy(5, c).start()
    for c in range(chunks):
        copy(4, c).wait_recv()
        copy(5, c).wait_recv()
        store(c).wait()
        for kind in range(6):
            copy(kind, c).wait_send()


def exchange_rows(total, backward, part, extra, hidden, gain, bias):
    rows, width = extra.shape
    chunks = 4
    vmem = pl.BlockSpec(memory_space=pltpu.VMEM)
    shapes = [jax.ShapeDtypeStruct((rows, width), F32), jax.ShapeDtypeStruct((GROUP, rows, width), BF16)]
    specs = [vmem, pl.BlockSpec(memory_space=ANY)]
    if backward:
        shapes.append(jax.ShapeDtypeStruct((8, width), F32))
        specs.append(vmem)
    return pl.pallas_call(
        functools.partial(exchange_kernel, total, chunks, backward),
        out_shape=shapes,
        in_specs=[pl.BlockSpec(memory_space=ANY)] + [vmem] * 4,
        out_specs=specs,
        scratch_shapes=[
            pltpu.VMEM((2, rows, width), BF16),
            pltpu.VMEM((rows, width), BF16),
            pltpu.VMEM((rows, width), BF16),
            pltpu.VMEM((rows, width), BF16),
            pltpu.VMEM((2, rows, width), BF16),
            pltpu.SemaphoreType.DMA((6, chunks)),
            pltpu.SemaphoreType.DMA((6, chunks)),
            pltpu.SemaphoreType.DMA((3, chunks)),
        ],
        compiler_params=pltpu.CompilerParams(
            collective_id=2 if backward else 1, has_side_effects=True, vmem_limit_bytes=40 * MIB
        ),
        name="exchange_backward" if backward else "exchange_forward",
    )(part, extra, hidden, gain, bias)


class Ring:
    def __init__(self, at, way, source, local, arrived, loads, sends, recvs):
        self.at, self.way, self.source = at, way, source
        self.local, self.arrived = local, arrived
        self.loads, self.sends, self.recvs = loads, sends, recvs

    def load(self, which):
        return pltpu.make_async_copy(self.source(which), self.local.at[which], self.loads.at[which])

    def hop(self, step, first=False):
        src = self.local.at[self.at.behind(self.way, 1)] if first else self.arrived.at[step - 1]
        return remote(
            src, self.arrived.at[step], self.sends.at[step], self.recvs.at[step], self.at.neighbour(self.way)
        )

    def begin(self):
        self.load(self.at.behind(self.way, 1)).wait()
        self.hop(0, True).start()

    def onward(self, step):
        which = self.at.behind(self.way, step + 1)
        self.load(which).wait()
        self.hop(step - 1, True).wait_recv()
        self.arrived[step - 1] = (
            self.arrived[step - 1].astype(F32) + self.local[which].astype(F32)
        ).astype(BF16)
        self.hop(step).start()

    def finish(self):
        last = self.at.total - 2
        self.load(self.at.inner).wait()
        self.hop(last, True).wait_recv()
        return self.arrived[last].astype(F32) + self.local[self.at.inner].astype(F32)

    def sent(self, step):
        self.hop(step, True).wait_send()


def run_rings(rings, total, between=()):
    at = rings[0].at
    for ring in rings:
        ring.load(at.behind(ring.way, 1)).start()

    def loads(step, carry):
        for ring in rings:
            ring.load(at.behind(ring.way, step + 1)).start()
        return carry

    lax.fori_loop(1, total, loads, 0)
    for ring in rings:
        ring.begin()
    marks = dict(between)
    last = 1
    for stop in sorted(marks) + [total - 1]:

        def body(step, carry):
            for ring in rings:
                ring.onward(step)
            return carry

        lax.fori_loop(last, stop, body, 0)
        last = stop
        if stop in marks:
            marks[stop]()


def close_rings(rings, total):
    for ring in rings:
        ring.sent(0)

    def body(step, carry):
        for ring in rings:
            ring.sent(step)
        return carry

    lax.fori_loop(1, total - 1, body, 0)


RELATIONS = ((2, 0), (3, 1))


def reduce_rest_kernel(
    total, g_up, g_out, g_down, o_up, o_out, o_down, l_up, r_up, l_od, r_od, stage, landed,
    loads_up, send_up, recv_up, loads_od, send_od, recv_od, a2a_send, a2a_recv,
):
    at = Place(total)
    me = at.group
    greet([at.peer(r) for r in (1, 2, 3)] + [at.neighbour(0), at.neighbour(1)])
    half = g_out.shape[1] // 2
    rings, kinds = [], []
    for order in (0, 1):
        for way in (0, 1):
            relation = RELATIONS[way][order]
            slot = 2 * way + order
            rings.append(
                Ring(
                    at, way,
                    lambda which, relation=relation: g_up.at[flip(me, relation), which],
                    l_up.at[slot], r_up.at[slot], loads_up.at[slot], send_up.at[slot], recv_up.at[slot],
                )
            )
            kinds.append(("up", relation))
    for number, source in enumerate((g_out, g_down)):
        for way in (0, 1):
            slot = 2 * number + way
            rings.append(
                Ring(
                    at, way,
                    lambda which, source=source, way=way: source.at[which, pl.ds(way * half, half)],
                    l_od.at[slot], r_od.at[slot], loads_od.at[slot], send_od.at[slot], recv_od.at[slot],
                )
            )
            kinds.append((number, way))
    run_rings(rings, total)
    width = o_up.shape[1] // GROUP

    def across(relation):
        return remote(
            stage.at[relation - 1], landed.at[relation - 1],
            a2a_send.at[relation - 1], a2a_recv.at[relation - 1], at.peer(relation),
        )

    for ring, (kind, what) in zip(rings, kinds):
        value = ring.finish()
        if kind == "up":
            if what == 0:
                o_up[:, pl.ds(pl.multiple_of(me * width, 128), width)] = value
            else:
                stage[what - 1] = value.astype(BF16)
                across(what).start()
        else:
            out = (o_out, o_down)[kind]
            out[pl.ds(what * half, half), :] = value
    for relation in (1, 2, 3):
        across(relation).wait_recv()
        o_up[:, pl.ds(pl.multiple_of(flip(me, relation) * width, 128), width)] = landed[
            relation - 1
        ].astype(F32)
    for relation in (1, 2, 3):
        across(relation).wait_send()
    close_rings(rings, total)


def reduce_rest(total, g_up, g_out, g_down):
    rows_up, width_up = g_up.shape[2:]
    rows_out, width_out = g_out.shape[1:]
    half = rows_out // 2
    vmem = pl.BlockSpec(memory_space=pltpu.VMEM)
    dma = pltpu.SemaphoreType.DMA
    return pl.pallas_call(
        functools.partial(reduce_rest_kernel, total),
        out_shape=[
            jax.ShapeDtypeStruct((rows_up, width_up * GROUP), F32),
            jax.ShapeDtypeStruct((rows_out, width_out), F32),
            jax.ShapeDtypeStruct((rows_out, width_out), F32),
        ],
        in_specs=[pl.BlockSpec(memory_space=ANY)] * 3,
        out_specs=[vmem] * 3,
        scratch_shapes=[
            pltpu.VMEM((4, total, rows_up, width_up), BF16),
            pltpu.VMEM((4, total - 1, rows_up, width_up), BF16),
            pltpu.VMEM((4, total, half, width_out), BF16),
            pltpu.VMEM((4, total - 1, half, width_out), BF16),
            pltpu.VMEM((3, rows_up, width_up), BF16),
            pltpu.VMEM((3, rows_up, width_up), BF16),
            dma((4, total)), dma((4, total - 1)), dma((4, total - 1)),
            dma((4, total)), dma((4, total - 1)), dma((4, total - 1)),
            dma((3,)), dma((3,)),
        ],
        compiler_params=pltpu.CompilerParams(
            collective_id=3, has_side_effects=True, vmem_limit_bytes=48 * MIB
        ),
        name="reduce_rest",
    )(g_up, g_out, g_down)


def reduce_in_kernel(
    total, g_in, part, o_in, o_part, local, arrived, stage, landed,
    core_in, own_part, out_x, in_x, loads, ring_send, ring_recv, a2a_send, a2a_recv,
    row_send, row_recv, row_own,
):
    at = Place(total)
    me = at.group
    greet([at.peer(r) for r in (1, 2, 3)] + [at.neighbour(0), at.neighbour(1)])
    rings, relations = [], []
    for order in (0, 1):
        for way in (0, 1):
            relation = RELATIONS[way][order]
            slot = 2 * way + order
            rings.append(
                Ring(
                    at, way,
                    lambda which, relation=relation: g_in.at[flip(me, relation), which],
                    local.at[slot], arrived.at[slot], loads.at[slot], ring_send.at[slot], ring_recv.at[slot],
                )
            )
            relations.append(relation)

    count = part.shape[0]

    def row_copy(kind, n):
        if kind == 0:
            src, dst, dev = part.at[n, flip(me, 3)], core_in.at[n, 0], at.peer(1)
        elif kind == 1:
            src, dst, dev = part.at[n, flip(me, 1)], core_in.at[n, 1], at.peer(1)
        else:
            src, dst, dev = out_x.at[n], in_x.at[n], at.peer(2)
        return remote(src, dst, row_send.at[n, kind], row_recv.at[n, kind], dev)

    def row_load(n, which):
        return pltpu.make_async_copy(
            part.at[n, flip(me, 2) if which == 0 else me], own_part.at[n, which], row_own.at[n, which]
        )

    for n in range(count):
        for kind in (0, 1):
            row_copy(kind, n).start()
            row_load(n, kind).start()

    def send_rows():
        for n in range(count):
            row_load(n, 0).wait()
            row_copy(0, n).wait_recv()
            out_x[n] = (own_part[n, 0].astype(F32) + core_in[n, 0].astype(F32)).astype(BF16)
            row_copy(2, n).start()

    def take_rows():
        for n in range(count):
            row_load(n, 1).wait()
            row_copy(1, n).wait_recv()
            row_copy(2, n).wait_recv()
            o_part[n] = (
                own_part[n, 1].astype(F32) + core_in[n, 1].astype(F32) + in_x[n].astype(F32)
            )

    run_rings(rings, total, ((2, send_rows), (total - 2, take_rows)))
    pieces = column_pieces(o_in.shape[1])

    def place(other, value):
        for base, stride, off, width in pieces:
            start = pl.multiple_of(base + other * stride, 128)
            o_in[:, pl.ds(start, width)] = value[:, off : off + width]

    def across(relation):
        return remote(
            stage.at[relation - 1], landed.at[relation - 1],
            a2a_send.at[relation - 1], a2a_recv.at[relation - 1], at.peer(relation),
        )

    for ring, relation in zip(rings, relations):
        value = ring.finish()
        if relation == 0:
            place(me, value)
        else:
            stage[relation - 1] = value.astype(BF16)
            across(relation).start()
    for relation in (1, 2, 3):
        across(relation).wait_recv()
        place(flip(me, relation), landed[relation - 1].astype(F32))
    for relation in (1, 2, 3):
        across(relation).wait_send()
    close_rings(rings, total)
    for n in range(count):
        for kind in (0, 1, 2):
            row_copy(kind, n).wait_send()


def reduce_in(total, g_in, part):
    rows, width = g_in.shape[2:]
    count, _, tokens, features = part.shape
    vmem = pl.BlockSpec(memory_space=pltpu.VMEM)
    dma = pltpu.SemaphoreType.DMA
    return pl.pallas_call(
        functools.partial(reduce_in_kernel, total),
        out_shape=[
            jax.ShapeDtypeStruct((rows, width * GROUP), F32),
            jax.ShapeDtypeStruct((count, tokens, features), F32),
        ],
        in_specs=[pl.BlockSpec(memory_space=ANY)] * 2,
        out_specs=[vmem] * 2,
        scratch_shapes=[
            pltpu.VMEM((4, total, rows, width), BF16),
            pltpu.VMEM((4, total - 1, rows, width), BF16),
            pltpu.VMEM((3, rows, width), BF16),
            pltpu.VMEM((3, rows, width), BF16),
            pltpu.VMEM((count, 2, tokens, features), BF16),
            pltpu.VMEM((count, 2, tokens, features), BF16),
            pltpu.VMEM((count, tokens, features), BF16),
            pltpu.VMEM((count, tokens, features), BF16),
            dma((4, total)), dma((4, total - 1)), dma((4, total - 1)),
            dma((3,)), dma((3,)),
            dma((count, 3)), dma((count, 3)), dma((count, 2)),
        ],
        compiler_params=pltpu.CompilerParams(
            collective_id=4, has_side_effects=True, vmem_limit_bytes=60 * MIB
        ),
        name="reduce_in",
    )(g_in, part)


def reduce_vectors_kernel(total, vec, out, landed, mid, gathered, sends, recvs, far_send, far_recv):
    at = Place(total)
    me, inner = at.group, at.inner
    others = [(me, lax.rem(inner + n, total)) for n in range(1, total)]
    greet([at.peer(r) for r in (1, 2, 3)] + others)

    def near(relation):
        return remote(
            vec.at[flip(me, relation)], landed.at[relation - 1],
            sends.at[relation - 1], recvs.at[relation - 1], at.peer(relation),
        )

    for relation in (1, 2, 3):
        near(relation).start()
    for relation in (1, 2, 3):
        near(relation).wait_recv()
    mid[...] = vec[me] + landed[0] + landed[1] + landed[2]

    def far(n):
        target = lax.rem(inner + n, total)
        return remote(mid.at[target], gathered.at[n - 1], far_send.at[n - 1], far_recv.at[n - 1], (me, target))

    for n in range(1, total):
        far(n).start()
    for n in range(1, total):
        far(n).wait_recv()
    out[...] = mid[inner] + jnp.sum(gathered[...], axis=0)
    for n in range(1, total):
        far(n).wait_send()
    for relation in (1, 2, 3):
        near(relation).wait_send()


def reduce_vectors(total, vec):
    block = vec.shape[2:]
    vmem = pl.BlockSpec(memory_space=pltpu.VMEM)
    dma = pltpu.SemaphoreType.DMA
    return pl.pallas_call(
        functools.partial(reduce_vectors_kernel, total),
        out_shape=jax.ShapeDtypeStruct(block, F32),
        in_specs=[vmem],
        out_specs=vmem,
        scratch_shapes=[
            pltpu.VMEM((3, total) + block, F32),
            pltpu.VMEM((total,) + block, F32),
            pltpu.VMEM((total - 1,) + block, F32),
            dma((3,)), dma((3,)), dma((total - 1,)), dma((total - 1,)),
        ],
        compiler_params=pltpu.CompilerParams(collective_id=5, has_side_effects=True),
        name="reduce_vectors",
    )(vec)


def layout(seq_lens, seq_owner, seq_offset, device_id, buffer_len):
    positions = jnp.arange(buffer_len, dtype=jnp.int32)[:, None]
    inside = (
        (seq_owner[None, :] == device_id)
        & (seq_lens[None, :] > 0)
        & (positions >= seq_offset[None, :])
        & (positions < seq_offset[None, :] + seq_lens[None, :])
    )
    number = jnp.arange(seq_lens.shape[0], dtype=jnp.int32)[None, :] + 1
    seq_ident = jnp.sum(jnp.where(inside, number, 0), axis=1) - 1
    starts = jnp.sum(jnp.where(inside, seq_offset[None, :], 0), axis=1)
    places = jnp.where(seq_ident >= 0, positions[:, 0] - starts, 0)
    return seq_ident, places


def rotation(places):
    half_size = QKH // 2
    pair_index = jnp.arange(half_size, dtype=F32) / half_size
    inverse_freq = 10000.0 ** (-pair_index)
    zeta_base = (pair_index + 0.4) / 1.4
    offsets = places.astype(F32)[..., None]
    angles = offsets * inverse_freq
    growth = zeta_base ** (offsets / 512.0)
    return jnp.cos(angles), jnp.sin(angles), growth


def rotate_xpos(vectors, cosine, sine, scale):
    half = QKH // 2
    first, second = vectors[..., :half], vectors[..., half:]
    cosine, sine, scale = cosine[..., None, :], sine[..., None, :], scale[..., None, :]
    return jnp.concatenate(
        [(first * cosine - second * sine) * scale, (second * cosine + first * sine) * scale], axis=-1
    )


def rotate_back(vectors, cosine, sine, scale):
    return rotate_xpos(vectors, cosine, -sine, scale)


def decay_tables(ident, heads):
    positions = jnp.arange(ident.shape[-1], dtype=jnp.int32)
    distance = positions[:, None] - positions[None, :]
    linked = (distance >= 0) & (ident[:, :, None] == ident[:, None, :]) & (ident[:, :, None] >= 0)
    rates = jnp.log1p(-(2.0 ** (-5.0 - heads.astype(F32))))
    powers = jnp.maximum(distance, 0).astype(F32)
    return jnp.where(linked[:, None], jnp.exp(rates[:, None, None] * powers[None])[None], 0.0)


def dot(left, right):
    return jnp.dot(left, right, preferred_element_type=F32)


def dot_rows(left, right):
    return lax.dot_general(left, right, (((0,), (0,)), ((), ())), preferred_element_type=F32)


def dot_back(left, right):
    return lax.dot_general(left, right, (((1,), (1,)), ((), ())), preferred_element_type=F32)


def mean(values):
    return jnp.mean(values, axis=-1, keepdims=True)


def local(
    total,
    tokens,
    cotangent,
    w_in,
    w_out,
    w_up,
    w_down,
    ln1_gain,
    ln1_bias,
    group_gain,
    ln2_gain,
    ln2_bias,
    seq_lens,
    seq_owner,
    seq_offset,
):
    rows, width = tokens.shape
    heads = HEADS // GROUP
    qk, vv = heads * QKH, heads * VH
    me, inner = lax.axis_index("dp"), lax.axis_index("fsdp")
    small, large = ln1_gain.shape[0], group_gain.shape[0]

    pack = jnp.concatenate([ln1_gain, ln1_bias, ln2_gain, ln2_bias, group_gain]).astype(F32)
    pack = jnp.pad(pack, (0, 1024 - pack.shape[0])).reshape(8, 128)
    full_in, full_up, full_out, full_down, tok, cot, vec = gather_all(
        total, w_in, w_up, w_out, w_down, tokens, cotangent, pack
    )
    full_in = full_in.reshape(width, -1)
    full_up = full_up.reshape(width, -1)
    full_out = full_out.reshape(-1, width)
    full_down = full_down.reshape(-1, width)
    vec = vec.reshape(total, GROUP, 1024)

    def vector(number):
        part = vec[:, :, number * small : (number + 1) * small]
        return jnp.swapaxes(part, 0, 1).reshape(1, width)

    gain_one, bias_one, gain_two, bias_two = (vector(n) for n in range(4))
    gain_group = lax.dynamic_index_in_dim(vec, me, 1, keepdims=False)[:, 4 * small : 4 * small + large]
    gain_group = gain_group.reshape(heads, VH)

    devices = jnp.arange(GROUP, dtype=jnp.int32) * total + inner
    ident, places = jax.vmap(lambda d: layout(seq_lens, seq_owner, seq_offset, d, rows))(devices)
    valid = (ident >= 0).astype(F32)[..., None]
    own_valid = lax.dynamic_index_in_dim(valid, me, 0, keepdims=False)
    count = GROUP * rows

    normal, _ = norm_parts(tok.astype(F32), EPSILON)
    normed = (normal * gain_one + bias_one).astype(BF16).reshape(count, width)
    project = dot(normed, full_in).reshape(GROUP, rows, -1)
    cosine, sine, growth = rotation(places)
    shrink = 1.0 / growth
    query = rotate_xpos(project[..., :qk].reshape(GROUP, rows, heads, QKH), cosine, sine, growth)
    query = (query * QKH ** (-0.5)).astype(BF16)
    keys = rotate_xpos(
        project[..., qk : 2 * qk].reshape(GROUP, rows, heads, QKH), cosine, sine, shrink
    ).astype(BF16)
    values = project[..., 2 * qk : 2 * qk + vv].reshape(GROUP, rows, heads, VH).astype(BF16)
    gate = project[..., 2 * qk + vv :].reshape(GROUP, rows, heads, VH)
    decay = decay_tables(ident, me * heads + jnp.arange(heads))
    raw = jnp.einsum("bthd,bshd->bhts", query, keys, preferred_element_type=F32)
    masked = (raw * decay).astype(BF16)
    mixed = jnp.einsum("bhts,bshv->bthv", masked, values, preferred_element_type=F32)
    group_normal, group_scale = norm_parts(mixed, GROUP_EPSILON)
    sigmoid = jax.nn.sigmoid(gate)
    silu = gate * sigmoid
    gated = (silu * (group_normal * gain_group)).astype(BF16).reshape(count, vv)
    branch = dot(gated, full_out).astype(BF16).reshape(GROUP, rows, width)
    hidden, two = exchange_rows(total, False, branch, tokens, jnp.zeros((8, 128), F32), gain_two, bias_two)
    two = two.reshape(count, width)
    upper = dot(two, full_up)
    cdf = 0.5 * (1.0 + lax.erf(upper * (0.5**0.5)))
    active = (upper * cdf).astype(BF16)
    down = dot(active, full_down).astype(BF16).reshape(GROUP, rows, width)

    seed = (cot.astype(F32) * valid).astype(BF16)
    own_seed = (cotangent.astype(F32) * own_valid).astype(BF16)
    seed = seed.reshape(count, width)
    slope = cdf + upper * jnp.exp(-0.5 * upper * upper) * (2.0 * jnp.pi) ** -0.5
    d_upper = (dot_back(seed, full_down) * slope).astype(BF16)
    d_two = dot_back(d_upper, full_up).astype(BF16).reshape(GROUP, rows, width)
    d_hidden, d_branch, sums_two = exchange_rows(
        total, True, d_two, own_seed, hidden, gain_two, bias_two
    )
    d_branch = d_branch.reshape(count, width)
    g_down = dot_rows(active, seed).astype(BF16).reshape(total, -1, width)
    g_up = dot_rows(two, d_upper).astype(BF16).reshape(GROUP, total, small, -1)
    g_out = dot_rows(gated, d_branch).astype(BF16).reshape(total, -1, width)
    grad_up, grad_out, grad_down = reduce_rest(total, g_up, g_out, g_down)

    d_gated = dot_back(d_branch, full_out).reshape(GROUP, rows, heads, VH)
    d_silu = d_gated * (group_normal * gain_group)
    d_gate = d_silu * (sigmoid + silu * (1.0 - sigmoid))
    d_scaled = d_gated * silu
    d_group = jnp.sum(d_scaled * group_normal, axis=(0, 1))
    d_normal = d_scaled * gain_group
    d_mixed = group_scale * (
        d_normal - mean(d_normal) - group_normal * mean(d_normal * group_normal)
    )
    d_mixed = d_mixed.astype(BF16)
    d_values = jnp.einsum("bhts,bthv->bshv", masked, d_mixed, preferred_element_type=F32)
    d_masked = jnp.einsum("bthv,bshv->bhts", d_mixed, values, preferred_element_type=F32)
    d_raw = (d_masked * decay).astype(BF16)
    d_query = jnp.einsum("bhts,bshd->bthd", d_raw, keys, preferred_element_type=F32)
    d_keys = jnp.einsum("bhts,bthd->bshd", d_raw, query, preferred_element_type=F32)
    d_query = rotate_back(d_query * QKH ** (-0.5), cosine, sine, growth)
    d_keys = rotate_back(d_keys, cosine, sine, shrink)
    d_project = jnp.concatenate(
        [
            d_query.astype(BF16).reshape(count, qk),
            d_keys.astype(BF16).reshape(count, qk),
            d_values.astype(BF16).reshape(count, vv),
            d_gate.astype(BF16).reshape(count, vv),
        ],
        axis=1,
    )
    d_normed = dot_back(d_project, full_in).astype(BF16).reshape(GROUP, rows, width)
    g_in = dot_rows(normed, d_project).astype(BF16).reshape(GROUP, total, small, -1)
    grad_in, own_rows = reduce_in(total, g_in, jnp.stack([d_normed, down]))
    output = ((hidden + own_rows[1]) * own_valid).astype(BF16)
    e_one = own_rows[0]
    normal_one, scale_one = norm_parts(tokens.astype(F32), EPSILON)
    with_gain = e_one * gain_one
    d_tokens = d_hidden + scale_one * (
        with_gain - mean(with_gain) - normal_one * mean(with_gain * normal_one)
    )
    d_tokens = d_tokens.astype(BF16)

    sums = jnp.stack(
        [jnp.sum(e_one * normal_one, axis=0), jnp.sum(e_one, axis=0), sums_two[0], sums_two[1]]
    )
    sums = sums.reshape(4, GROUP, total, small).transpose(1, 2, 0, 3).reshape(GROUP, total, 4 * small)
    mine = (jnp.arange(GROUP) == me).astype(F32)[:, None, None]
    sums = jnp.concatenate([sums, mine * d_group.reshape(1, total, large)], axis=2)
    sums = jnp.pad(sums, ((0, 0), (0, 0), (0, 1024 - sums.shape[2]))).reshape(GROUP, total, 8, 128)
    summed = reduce_vectors(total, sums).reshape(1024)
    grads = [summed[n * small : (n + 1) * small] for n in range(4)]
    grad_group = summed[4 * small : 4 * small + large]
    return (
        output,
        d_tokens,
        grad_in,
        grad_out,
        grad_up,
        grad_down,
        grads[0],
        grads[1],
        grad_group,
        grads[2],
        grads[3],
    )


def solution(mesh):
    flat = ("dp", "fsdp")
    matrix, vector = P(flat, None), P(flat)
    return jax.shard_map(
        functools.partial(local, mesh.shape["fsdp"]),
        mesh=mesh,
        in_specs=(matrix,) * 6 + (vector,) * 5 + (P(),) * 3,
        out_specs=(matrix,) * 6 + (vector,) * 5,
        check_vma=False,
    )
```

time: 3660 us -> 890 us (0.24)
  waiting for transfers between devices: 3180 us -> 0 us
  Pallas kernels: 0 us -> 633 us
  blocking collectives: 156 us -> 0 us
  matrix products: 227 us -> 115 us
  local copies, waits for them, and re-layouts: 37.9 us -> 81 us
    reduce_scatter x4 -> x0, waiting for transfers between devices: 2740 us -> none  [the longest x1 834 us: local(): lax.psum_scatter(inner_rows(normed_low, project_low), ('dp', 'fsdp'), sca...]
    pallas_call x0 -> x6, Pallas kernels: none -> 633 us  [the longest x1 259 us: gather_all(): pl.pallas_call(functools.partial(gather_kernel, total), out_shape=[jax.Sh...]
    all_gather x4 -> x0, waiting for transfers between devices: 443 us -> none  [the longest x1 167 us: local(): lax.all_gather(w_in, ('dp', 'fsdp'), axis=0, tiled=True)]
    dot_general x18, matrix products: 227 us -> 115 us  [the longest x4 42.7 us: dot_back(): lax.dot_general(left, right, (((1,), (1,)), ((), ())), preferred_element_...]
    unnamed x2 -> x0, blocking collectives: 95.6 us -> none
    all_gather x1 -> x0, blocking collectives: 60.6 us -> none  [local(): lax.all_gather(group_gain, ('dp', 'fsdp'), axis=0, tiled=True)]
  transfers between devices with their start and end apart: 8 -> 0, of which waited for: 8 -> 0; matrix products, arithmetic and copies ran while one was open for 7% -> 0% of each run, Pallas kernels for 0% -> 0%
where the time goes in v1:
time: 890 us; the launch traced here: 883 us
  Pallas kernels  633 us (71%)
  matrix products  115 us (13%)
  local copies, waits for them, and re-layouts  81 us (9%)
  other arithmetic  51.2 us (6%)
    pallas_call x1, Pallas kernels, gather_all(): pl.pallas_call(functools.partial(gather_kernel, total), out_shape=[jax.Sh...  259 us
    pallas_call x1, Pallas kernels, reduce_in(): pl.pallas_call(functools.partial(reduce_in_kernel, total), out_shape=[jax...  138 us
    pallas_call x1, Pallas kernels, reduce_rest(): pl.pallas_call(functools.partial(reduce_rest_kernel, total), out_shape=[j...  124 us
    pallas_call x2, Pallas kernels, exchange_rows(): pl.pallas_call(functools.partial(exchange_kernel, total, chunks, backward...  103 us
    dot_general x4, matrix products, dot_back(): lax.dot_general(left, right, (((1,), (1,)), ((), ())), preferred_element_...  42.7 us
    dot_general x4, matrix products, dot_rows(): lax.dot_general(left, right, (((0,), (0,)), ((), ())), preferred_element_...  37.4 us
    unnamed x142, local copies, waits for them, and re-layouts  31.9 us
    dot_general x4, matrix products, dot(): return jnp.dot(left, right, preferred_element_type=F32)  28.8 us

profile of v1, /device:TPU:1, one launch (start us, length us, event | category | flops | bytes accessed | tf_op | source)
XLA Modules:
  0.0 882.6 jit_solution(11651453627478262532)
XLA Ops:
  3.3 3.4 concatenate.25
  16.7 3.1 fusion.43
  19.8 258.7 %gather_weights.1 = (bf16[4,8,64,3072]{3,2,1,0:T(8,128)(2,1)}, bf16[4,8,64,1024]{3,2,1,0:T(8,128)(2,1)}, bf16[8,128,2048]{2,1,0:T(8,128)(2,1)}, bf16[8,128,2048]...) custom-call(bf16[64,12288]{1,0:T(8,128)(2,1)} %w_in.1, ...), custom_call_target="tpu_custom_call" | custom-call | tf_op jit(solution)/shard_map/gather_weights/pallas_call | solution.py:263
  279.5 3.0 convert_reduce_fusion
  284.7 3.7 fusion.5
  294.7 13.3 %fusion.62 = f32[4,256,3072]{2,1,0:T(8,128)S(1)} fusion(bf16[4,256,2048]{2,1,0:T(8,128)(2,1)S(1)} %fusion.5, bf16[2048,3072,1]{1,0,2:T(8,128)(2,1)S(1)} %bitcast.184), kind=kOutput, calls=%fused_computation.160 | convolution fusion | flops 12884901888 | bytes 29360128 | tf_op jit(solution)/shard_map/dot_general | solution.py:814
  314.4 5.4 copy.100
  319.8 3.1 reshape.387
  338.8 3.9 copy.77
  345.5 4.7 convolution_convert_fusion.7
  350.3 51.4 %exchange_forward.1 = (f32[256,2048]{1,0:T(8,128)S(1)}, bf16[4,256,2048]{2,1,0:T(8,128)(2,1)S(1)}) custom-call(bf16[4,256,2048]{2,1,0:T(8,128)(2,1)S(1)} %bitcast.152, bf16[256,2048]{1,0:T(8,128)(2,1)S(1)} %copy-done, f32[8,128]{1,0:T(8,128)S(1)} %broadcast_in_dim.41.hidden_in, f32[1,2048]{1,0:T(1,128)S(1)} %reshape.392.gain, f32[1,2048]{1,0:T(1,128)S(1)} %reshape.393.bias), custom_call_target="tpu_custom_call" | custom-call | tf_op jit(solution)/shard_map/exchange_forward/pallas_call | solution.py:390
  401.7 4.8 multiply_convert_fusion.1
  406.4 5.8 fusion.11
  412.3 6.1 convolution_convert_fusion.5
  418.4 6.3 convolution_convert_fusion.2
  424.7 6.4 convolution_convert_fusion.4
  431.0 4.9 convolution_convert_fusion.6
  435.9 51.2 %exchange_backward.1 = (f32[256,2048]{1,0:T(8,128)S(1)}, bf16[4,256,2048]{2,1,0:T(8,128)(2,1)S(1)}, f32[8,2048]{1,0:T(8,128)S(1)}) custom-call(bf16[4,256,2048]{2,1,0:T(8,128)(2,1)S(1)} %bitcast.151, bf16[256,2048]{1,0:T(8,128)(2,1)S(1)} %multiply_convert_fusion.5.extra, f32[256,2048]{1,0:T(8,128)S(1)} %get-tuple-element.32.hidden_in, ...), custom_call_target="tpu_custom_call" | custom-call | tf_op jit(solution)/shard_map/exchange_backward/pallas_call | solution.py:390
  487.1 12.2 %multiply_reduce_fusion = (f32[2,512]{1,0:T(2,128)S(1)}, f32[4,256,2]{1,2,0:T(2,128)S(1)}, f32[4,256,2]{1,2,0:T(2,128)S(1)}, f32[4,256,2,512]{1,3,2,0:T(8,128)}, bf16[4,256,2,512]{1,3,2,0:T(8,128)(2,1)}) fusion(f32[4,2,512,256]{3,2,1,0:T(8,128)S(1)} %copy-done.13, f32[4,256,2]{1,2,0:T(2,128)S(1)} %add_rsqrt_fusion, ...), kind=kOutput, calls=%fused_computation.23 | convolution fusion | flops 4315933696 | bytes 23109632 | tf_op jit(solution)/shard_map/dot_general | solution.py:822
  499.5 4.8 multiply_convert_fusion.3
  508.4 6.3 copy.89
  514.7 3.7 copy.114
  527.0 6.3 convolution_convert_fusion.3
  533.3 124.2 %reduce_rest.1 = (f32[64,4096]{1,0:T(8,128)S(1)}, f32[128,2048]{1,0:T(8,128)S(1)}, f32[128,2048]{1,0:T(8,128)S(1)}) custom-call(bf16[4,8,64,1024]{3,2,1,0:T(8,128)(2,1)} %bitcast.166, bf16[8,128,2048]{2,1,0:T(8,128)(2,1)} %bitcast.167, bf16[8,128,2048]{2,1,0:T(8,128)(2,1)} %bitcast.165), custom_call_target="tpu_custom_call" | custom-call | tf_op jit(solution)/shard_map/reduce_rest/pallas_call | solution.py:561
  660.5 6.1 copy.91
  669.6 19.8 %convolution_convert_fusion.1 = bf16[1024,2048]{1,0:T(8,128)(2,1)} fusion(bf16[1024,3072]{1,0:T(8,128)(2,1)S(1)} %constant_dynamic-update-slice_fusion, bf16[2048,3072]{1,0:T(8,128)(2,1)} %bitcast.183), kind=kOutput, calls=%fused_computation.33 | convolution fusion | flops 12886999040 | bytes 23068672 | tf_op jit(solution)/shard_map/dot_general | solution.py:822
  689.4 7.6 pad_maximum_fusion.part
  697.0 18.5 %convolution_convert_fusion = bf16[2048,3072]{1,0:T(8,128)(2,1)} fusion(bf16[1024,2048]{1,0:T(8,128)(2,1)S(1)} %bitcast.168, bf16[1024,3072]{1,0:T(8,128)(2,1)} %copy-done.51), kind=kOutput, calls=%fused_computation | convolution fusion | flops 12891193344 | bytes 23068672 | tf_op jit(solution)/shard_map/dot_general | solution.py:818
  715.5 137.6 %reduce_in.1 = (f32[64,12288]{1,0:T(8,128)}, f32[2,256,2048]{2,1,0:T(8,128)}) custom-call(bf16[4,8,64,3072]{3,2,1,0:T(8,128)(2,1)} %bitcast.157, bf16[2,4,256,2048]{3,2,1,0:T(8,128)(2,1)} %pad_maximum_fusion.part), custom_call_target="tpu_custom_call" | custom-call | tf_op jit(solution)/shard_map/reduce_in/pallas_call | solution.py:684
  857.6 4.5 fusion.25
  863.1 9.8 %reduce_vectors.1 = f32[8,128]{1,0:T(8,128)} custom-call(f32[4,8,8,128]{3,2,1,0:T(8,128)} %copy.143), custom_call_target="tpu_custom_call" | custom-call | tf_op jit(solution)/shard_map/reduce_vectors/pallas_call | solution.py:749
  875.5 3.9 copy.152
  (224 shorter events, 76.2 us)
Async XLA Ops:
  0.6 15.8 %copy-start.40 = (bf16[256,2048]{1,0:T(8,128)(2,1)S(1)}, bf16[256,2048]{1,0:T(8,128)(2,1)}, u32[]{:S(2)}) copy-start(bf16[256,2048]{1,0:T(8,128)(2,1)} %cot.1) | copy-start | bytes 3145732
  8.2 8.2 copy-start.54
  12.6 265.9 %copy-start.57 = (f32[1,256]{1,0:T(1,128)}, f32[1,256]{1,0:T(1,128)S(1)}, u32[]{:S(2)}) copy-start(f32[1,256]{1,0:T(1,128)S(1)} %constant_dynamic-slice_fusion) | copy-start | bytes 3076
  284.7 10.0 %copy-start.60 = (bf16[4,8,64,3072]{3,2,1,0:T(8,128)(2,1)S(1)}, bf16[4,8,64,3072]{3,2,1,0:T(8,128)(2,1)}, u32[]{:S(2)}) copy-start(bf16[4,8,64,3072]{3,2,1,0:T(8,128)(2,1)} %get-tuple-element.30) | copy-start | bytes 37748740
  288.5 4.1 copy-start.32
  333.3 4.1 copy-start.15
  345.0 5.2 copy-start.43
  345.5 4.7 copy-start
  350.2 51.4 %copy-start.62 = (bf16[4,8,64,1024]{3,2,1,0:T(8,128)(2,1)S(1)}, bf16[4,8,64,1024]{3,2,1,0:T(8,128)(2,1)}, u32[]{:S(2)}) copy-start(bf16[4,8,64,1024]{3,2,1,0:T(8,128)(2,1)} %get-tuple-element.36) | copy-start | bytes 12582916
  401.6 4.8 copy-start.38
  401.7 4.8 copy-start.63
  431.0 56.1 %copy-start.16 = (f32[4,256,1024]{1,2,0:T(8,128)S(1)}, f32[4,256,1024]{1,2,0:T(8,128)}, u32[]{:S(2)}) copy-start(f32[4,256,1024]{1,2,0:T(8,128)} %copy.100) | copy-start | bytes 12582916
  435.9 51.2 %copy-start.13 = (f32[4,2,512,256]{3,2,1,0:T(8,128)S(1)}, f32[4,2,512,256]{3,2,1,0:T(8,128)}, u32[]{:S(2)}) copy-start(f32[4,2,512,256]{3,2,1,0:T(8,128)} %copy-done.12) | copy-start | bytes 12582916
  487.1 12.3 %copy-start.2 = (f32[256,2048]{1,0:T(8,128)}, f32[256,2048]{1,0:T(8,128)S(1)}, u32[]{:S(2)}) copy-start(f32[256,2048]{1,0:T(8,128)S(1)} %get-tuple-element.39) | copy-start | bytes 6291460
  487.1 12.3 %copy-start.10 = (bf16[4,256,2048]{2,1,0:T(8,128)(2,1)}, bf16[4,256,2048]{2,1,0:T(8,128)(2,1)S(1)}, u32[]{:S(2)}) copy-start(bf16[4,256,2048]{2,1,0:T(8,128)(2,1)S(1)} %get-tuple-element.37) | copy-start | bytes 12582916
  499.5 4.8 copy-start.19
  499.5 4.8 copy-start.50
  508.4 10.0 %copy-start.29 = (f32[4,256,2,128]{3,1,2,0:T(8,128)S(1)}, f32[4,256,2,128]{3,1,2,0:T(8,128)}, u32[]{:S(2)}) copy-start(f32[4,256,2,128]{3,1,2,0:T(8,128)} %copy-done.28) | copy-start | bytes 3145732
  514.7 4.3 copy-start.46
  514.7 4.3 copy-start.48
  523.2 3.8 copy-start.11
  523.2 3.8 copy-start.44
  669.6 19.8 %copy-start.51 = (bf16[1024,3072]{1,0:T(8,128)(2,1)}, bf16[1024,3072]{1,0:T(8,128)(2,1)S(1)}, u32[]{:S(2)}) copy-start(bf16[1024,3072]{1,0:T(8,128)(2,1)S(1)} %constant_dynamic-update-slice_fusion) | copy-start | bytes 18874372
  689.4 7.6 copy-start.33
  715.5 139.5 %copy-start.1 = (bf16[256,2048]{1,0:T(8,128)(2,1)S(1)}, bf16[256,2048]{1,0:T(8,128)(2,1)}, u32[]{:S(2)}) copy-start(bf16[256,2048]{1,0:T(8,128)(2,1)} %extra.1) | copy-start | bytes 3145732
  715.5 139.5 %copy-start.53 = (f32[2048]{0:T(1024)S(1)}, f32[2048]{0:T(1024)}, u32[]{:S(2)}) copy-start(f32[2048]{0:T(1024)} %copy-done.52) | copy-start | bytes 24580
  715.5 139.5 %copy-start.55 = (f32[256]{0:T(256)S(1)}, f32[256]{0:T(256)}, u32[]{:S(2)}) copy-start(f32[256]{0:T(256)} %copy-done.54) | copy-start | bytes 3076
  715.5 139.5 %copy-start.56 = (f32[256]{0:T(256)S(1)}, f32[256]{0:T(256)}, u32[]{:S(2)}) copy-start(f32[256]{0:T(256)} %add_rsqrt_fusion.2) | copy-start | bytes 3076
  853.1 4.5 copy-start.58
  862.1 17.3 %copy-start.9 = (f32[128,2048]{1,0:T(8,128)S(1)}, f32[128,2048]{1,0:T(8,128)}, u32[]{:S(2)}) copy-start(f32[128,2048]{1,0:T(8,128)} %copy-done.8) | copy-start | bytes 3145732
  875.5 4.9 copy-start.7
  875.5 5.9 copy-start.5
  (32 other events, 71.9 us)

commit v2 on v1

--- a/solution.py
+++ b/solution.py
@@ -90,19 +90,27 @@
     )
 
 
+def dot(left, right):
+    return jnp.dot(left, right, preferred_element_type=F32)
+
+
+def dot_rows(left, right):
+    return lax.dot_general(left, right, (((0,), (0,)), ((), ())), preferred_element_type=F32)
+
+
+def dot_back(left, right):
+    return lax.dot_general(left, right, (((1,), (1,)), ((), ())), preferred_element_type=F32)
+
+
 def gather_kernel(
     total,
     w_in,
     w_up,
-    w_out,
-    w_down,
     tok,
     cot,
     vec,
     full_in,
-    full_up,
-    full_out,
-    full_down,
+    own_up,
     full_tok,
     full_cot,
     full_vec,
@@ -116,8 +124,7 @@
     me, inner = at.group, at.inner
     peers = [at.peer(r) for r in (1, 2, 3)]
     greet(peers + [at.neighbour(0), at.neighbour(1)])
-    up_width = full_up.shape[-1]
-    half_out = w_out.shape[0] // 2
+    up_width = own_up.shape[-1]
     pieces = column_pieces(w_in.shape[1])
 
     def exchange(relation, slot):
@@ -129,7 +136,7 @@
             dst = full_in.at[me, inner, :, pl.ds(off, width)]
         elif slot == 4:
             src = w_up.at[:, pl.ds(pl.multiple_of(other * up_width, 128), up_width)]
-            dst = full_up.at[me, inner]
+            dst = own_up.at[me]
         elif slot == 5:
             src, dst = vec, full_vec.at[inner, me]
         elif slot == 6:
@@ -146,31 +153,19 @@
             at.peer(relation),
         )
 
-    def own_block(which):
-        src, dst = ((w_out, full_out), (w_down, full_down))[which]
-        rows = src.shape[0]
-        return pltpu.make_async_copy(src, dst.at[inner], own_sem.at[8 + which])
-
     for relation in (1, 0, 2, 3):
         for slot in (0, 1, 2, 3):
             exchange(relation, slot).start()
     for relation in (1, 0, 2, 3):
         for slot in (5, 4):
             exchange(relation, slot).start()
-    own_block(0).start()
-    own_block(1).start()
 
     ways = ((0, 2), (1, 3))
 
     def block(item, way, which):
         if item < 2:
             return full_in.at[flip(me, ways[way][item]), which]
-        if item < 4:
-            return full_up.at[flip(me, ways[way][item - 2]), which]
-        if item == 4:
-            return full_vec.at[which]
-        part = full_out if item == 5 else full_down
-        return part.at[which, pl.ds(way * half_out, half_out)]
+        return full_vec.at[which]
 
     def hop(item, way, step):
         which = at.behind(way, step)
@@ -180,30 +175,20 @@
         )
 
     def active(item, way):
-        return not (item == 4 and way == 1)
+        return not (item == 2 and way == 1)
 
     def first(item, way):
-        if item < 4:
-            relation = ways[way][item % 2]
-            slots = (0, 1, 2, 3) if item < 2 else (4,)
+        relations, slots = ((ways[way][item],), (0, 1, 2, 3)) if item < 2 else (range(4), (5,))
+        for relation in relations:
             for slot in slots:
                 copy = exchange(relation, slot)
                 if relation == 0:
                     copy.wait()
                 else:
                     copy.wait_recv()
-        elif item == 4:
-            for relation in range(4):
-                copy = exchange(relation, 5)
-                if relation == 0:
-                    copy.wait()
-                else:
-                    copy.wait_recv()
-        elif way == 0:
-            own_block(item - 5).wait()
         hop(item, way, 0).start()
 
-    groups = ((0, 1), (4, 5, 2, 3, 6))
+    groups = ((0, 1, 2),)
     for number, group in enumerate(groups):
         for item in group:
             for way in (0, 1):
@@ -242,20 +227,19 @@
     for relation in (1, 2, 3):
         for slot in range(8):
             exchange(relation, slot).wait_send()
-            if slot >= 6:
+            if slot in (4, 6, 7):
                 exchange(relation, slot).wait_recv()
+    exchange(0, 4).wait()
     exchange(0, 6).wait()
     exchange(0, 7).wait()
 
 
-def gather_all(total, w_in, w_up, w_out, w_down, tok, cot, vec):
+def gather_all(total, w_in, w_up, tok, cot, vec):
     width = w_in.shape[1] // GROUP
     up_width = w_up.shape[1] // GROUP
     shapes = (
         ((GROUP, total, w_in.shape[0], width), BF16),
-        ((GROUP, total, w_up.shape[0], up_width), BF16),
-        ((total,) + w_out.shape, BF16),
-        ((total,) + w_down.shape, BF16),
+        ((GROUP, w_up.shape[0], up_width), BF16),
         ((GROUP,) + tok.shape, BF16),
         ((GROUP,) + cot.shape, BF16),
         ((total, GROUP) + vec.shape, F32),
@@ -263,18 +247,18 @@
     return pl.pallas_call(
         functools.partial(gather_kernel, total),
         out_shape=[jax.ShapeDtypeStruct(s, d) for s, d in shapes],
-        in_specs=[pl.BlockSpec(memory_space=ANY)] * 7,
-        out_specs=[pl.BlockSpec(memory_space=ANY)] * 7,
+        in_specs=[pl.BlockSpec(memory_space=ANY)] * 5,
+        out_specs=[pl.BlockSpec(memory_space=ANY)] * 5,
         scratch_shapes=[
             pltpu.SemaphoreType.DMA((3, 8)),
             pltpu.SemaphoreType.DMA((3, 8)),
-            pltpu.SemaphoreType.DMA((10,)),
-            pltpu.SemaphoreType.DMA((7, 2, total - 1)),
-            pltpu.SemaphoreType.DMA((7, 2, total - 1)),
+            pltpu.SemaphoreType.DMA((8,)),
+            pltpu.SemaphoreType.DMA((3, 2, total - 1)),
+            pltpu.SemaphoreType.DMA((3, 2, total - 1)),
         ],
         compiler_params=pltpu.CompilerParams(collective_id=0, has_side_effects=True),
         name="gather_weights",
-    )(w_in, w_up, w_out, w_down, tok, cot, vec)
+    )(w_in, w_up, tok, cot, vec)
 
 
 def norm_parts(values, epsilon):
@@ -409,6 +393,411 @@
     )(part, extra, hidden, gain, bias)
 
 
+RELATIONS = ((2, 0), (3, 1))
+
+
+class Passing:
+    def __init__(self, at, way, own, place, sends, recvs):
+        self.at, self.way, self.own, self.place = at, way, own, place
+        self.sends, self.recvs = sends, recvs
+
+    def hop(self, step, first=False):
+        which = self.at.inner if first else self.at.behind(self.way, step)
+        dst = self.place(which)
+        return remote(
+            self.own if first else dst, dst, self.sends.at[step], self.recvs.at[step],
+            self.at.neighbour(self.way),
+        )
+
+    def begin(self):
+        self.hop(0, True).start()
+
+    def onward(self, step):
+        self.hop(step - 1).wait_recv()
+        self.hop(step).start()
+
+    def finish(self):
+        self.hop(self.at.total - 2).wait_recv()
+
+
+def wait_sent(rings, total):
+    def body(step, carry):
+        for ring in rings:
+            ring.hop(step).wait_send()
+        return carry
+
+    lax.fori_loop(0, total - 1, body, 0)
+
+
+def tick_plan(total, places):
+    steps = total - 2
+    cuts = [1 + (steps * n) // places for n in range(places + 1)]
+    return list(zip(cuts[:-1], cuts[1:]))
+
+
+def run_steps(rings, start, stop):
+    def body(step, carry):
+        for ring in rings:
+            ring.onward(step)
+        return carry
+
+    lax.fori_loop(start, stop, body, 0)
+
+
+def weight_rings(at, own_up, w_out, w_down, full_up, full_out, full_down, sends, recvs):
+    me = at.group
+    half = w_out.shape[0] // 2
+    side = w_out.shape[1] // 2
+
+    def halves(own, full, slot):
+        return [
+            Passing(
+                at, way,
+                own.at[pl.ds(way * half, half), pl.ds(c * side, side)],
+                lambda which, way=way, c=c: full.at[which, pl.ds(way * half, half), pl.ds(c * side, side)],
+                sends.at[slot + 2 * c + way], recvs.at[slot + 2 * c + way],
+            )
+            for c in (0, 1)
+            for way in (0, 1)
+        ]
+
+    ups = []
+    for order in (0, 1):
+        for way in (0, 1):
+            relation = RELATIONS[way][order]
+            slot = 8 + 2 * order + way
+            ups.append(
+                Passing(
+                    at, way, own_up.at[flip(me, relation)],
+                    lambda which, relation=relation: full_up.at[flip(me, relation), which],
+                    sends.at[slot], recvs.at[slot],
+                )
+            )
+    return halves(w_out, full_out, 0), ups, halves(w_down, full_down, 4)
+
+
+def rotated(value, cosine, sine, scale):
+    half = QKH // 2
+    first, second = value[:, :half], value[:, half:]
+    return jnp.concatenate(
+        [(first * cosine - second * sine) * scale, (second * cosine + first * sine) * scale], axis=1
+    )
+
+
+def forward_kernel(
+    total, own_up, w_out, w_down, full_in, tok, gain_one, bias_one, gain_group, cosine, sine, growth, shrink,
+    powers, ident_col, ident_row, own_tok, gain_two, bias_two,
+    full_up, full_out, full_down, o_normed, o_query, o_keys, o_values, o_gate, o_mixed, o_gated, hidden, full_two,
+    win, part, x, query, keys, values, gate, mixed, gated, wo, core_in, out_x, in_x, low,
+    ring_send, ring_recv, own_sem, load_sem, win_sem, store_sem, row_send, row_recv, row_own,
+):
+    at = Place(total)
+    me, inner = at.group, at.inner
+    core, across = at.peer(1), at.peer(2)
+    greet([core, across, at.neighbour(0), at.neighbour(1)])
+    rows, width = own_tok.shape
+    count = GROUP * rows
+    heads = HEADS // GROUP
+    outs, ups, downs = weight_rings(
+        at, own_up, w_out, w_down, full_up, full_out, full_down, ring_send, ring_recv
+    )
+    for ring in outs:
+        ring.begin()
+    own_copies = [
+        pltpu.make_async_copy(w_out, full_out.at[inner], own_sem.at[0]),
+        pltpu.make_async_copy(w_down, full_down.at[inner], own_sem.at[1]),
+        pltpu.make_async_copy(own_up, full_up.at[:, inner], own_sem.at[2]),
+    ]
+    for b in range(GROUP):
+        pltpu.make_async_copy(tok.at[b], part.at[b], load_sem.at[b]).start()
+
+    def win_copies(h):
+        qk, vv = heads * QKH, heads * VH
+        table = (
+            (h * QKH, 0, QKH),
+            (qk + h * QKH, QKH, QKH),
+            (2 * qk + h * VH, 2 * QKH, VH),
+            (2 * qk + vv + h * VH, 2 * QKH + VH, VH),
+        )
+        return [
+            pltpu.make_async_copy(
+                full_in.at[:, pl.ds(pl.multiple_of(start, 128), size)],
+                win.at[h, :, pl.ds(off, size)],
+                win_sem.at[h, n],
+            )
+            for n, (start, off, size) in enumerate(table)
+        ]
+
+    for h in range(heads):
+        for copy in win_copies(h):
+            copy.start()
+    for copy in own_copies:
+        copy.start()
+
+    step_rows = 32
+
+    def norm_buffer(b, carry):
+        pltpu.make_async_copy(tok.at[b], part.at[b], load_sem.at[b]).wait()
+
+        def norm_rows(n, carry):
+            r = pl.multiple_of(n * step_rows, step_rows)
+            normal, _ = norm_parts(part[b, pl.ds(r, step_rows), :].astype(F32), EPSILON)
+            at_rows = pl.ds(pl.multiple_of(b * rows + r, step_rows), step_rows)
+            x[at_rows, :] = (normal * gain_one[...] + bias_one[...]).astype(BF16)
+            return carry
+
+        lax.fori_loop(0, rows // step_rows, norm_rows, 0)
+        return carry
+
+    lax.fori_loop(0, GROUP, norm_buffer, 0)
+    pltpu.make_async_copy(x, o_normed, store_sem.at[0]).start()
+
+    tile = 512
+    spots = 6
+    plan = tick_plan(total, spots)
+    span = [stop - start for start, stop in plan]
+
+    def spot(h, number):
+        lows = [plan[k * (spots // heads) + number][0] for k in range(heads)]
+        highs = [plan[k * (spots // heads) + number][1] for k in range(heads)]
+        low_step = lows[0] + h * (lows[1] - lows[0])
+        high_step = highs[0] + h * (highs[1] - highs[0])
+        run_steps(outs, low_step, high_step)
+
+    def project(h, off):
+        def at_tile(m, use):
+            r = pl.ds(pl.multiple_of(m * tile, tile), tile)
+            use(r, dot(x[r, :], win[h, :, off : off + QKH]))
+
+        return at_tile
+
+    def head(h, carry):
+        for copy in win_copies(h):
+            copy.wait()
+
+        def rotate_tiles(m, carry):
+            def put_query(r, value):
+                turned = rotated(value, cosine[r, :], sine[r, :], growth[r, :])
+                query[h, r, :] = (turned * QKH ** (-0.5)).astype(BF16)
+
+            def put_keys(r, value):
+                keys[h, r, :] = rotated(value, cosine[r, :], sine[r, :], shrink[r, :]).astype(BF16)
+
+            project(h, 0)(m, put_query)
+            project(h, QKH)(m, put_keys)
+            return carry
+
+        lax.fori_loop(0, count // tile, rotate_tiles, 0)
+        spot(h, 0)
+
+        def plain_tiles(m, carry):
+            for c in range(VH // QKH):
+                off = c * QKH
+
+                def put_values(r, value, off=off):
+                    values[h, r, off : off + QKH] = value.astype(BF16)
+
+                def put_gate(r, value, off=off):
+                    gate[h, r, off : off + QKH] = value
+
+                project(h, 2 * QKH + off)(m, put_values)
+                project(h, 2 * QKH + VH + off)(m, put_gate)
+            return carry
+
+        lax.fori_loop(0, count // tile, plain_tiles, 0)
+        spot(h, 1)
+
+        def buffer(b, carry):
+            r = pl.ds(pl.multiple_of(b * rows, rows), rows)
+            raw = dot_back(query[h, r, :], keys[h, r, :])
+            linked = (ident_col[b] == ident_row[b]) & (ident_col[b] >= 0)
+            masked = (raw * jnp.where(linked, powers[h], 0.0)).astype(BF16)
+            value = dot(masked, values[h, r, :])
+            mixed[h, r, :] = value
+            normal, _ = norm_parts(value, GROUP_EPSILON)
+            z = gate[h, r, :]
+            result = z / (1.0 + jnp.exp(-z)) * (normal * gain_group[h])
+            gated[r, pl.ds(pl.multiple_of(h * VH, VH), VH)] = result.astype(BF16)
+            return carry
+
+        lax.fori_loop(0, GROUP, buffer, 0)
+        spot(h, 2)
+        return carry
+
+    lax.fori_loop(0, heads, head, 0)
+    for ring in outs:
+        ring.finish()
+    for ring in ups + downs:
+        ring.begin()
+    stores = [
+        pltpu.make_async_copy(src, dst, store_sem.at[1 + n])
+        for n, (src, dst) in enumerate(
+            ((query, o_query), (keys, o_keys), (values, o_values), (gate, o_gate), (mixed, o_mixed), (gated, o_gated))
+        )
+    ]
+    for copy in stores:
+        copy.start()
+    own_copies[0].wait()
+    block = w_out.shape[0]
+    fetch = pltpu.make_async_copy(full_out, wo, load_sem.at[GROUP])
+    fetch.start()
+    fetch.wait()
+
+    chunks = 4
+    size = rows // chunks
+    rest = ups + downs
+    later = tick_plan(total, 6)
+
+    def branch(relation):
+        b = flip(me, relation)
+
+        def column(n, carry):
+            wide = 512
+            c = pl.ds(pl.multiple_of(n * wide, wide), wide)
+            r = pl.ds(pl.multiple_of(b * rows, rows), rows)
+            acc = jnp.zeros((rows, wide), F32)
+            piece = gated[r, :]
+            acc = dot(piece, wo[:, :, c].reshape(total * block, wide))
+            part[b, :, c] = acc.astype(BF16)
+            return carry
+
+        lax.fori_loop(0, width // 512, column, 0)
+
+    def rows_of(c):
+        return pl.ds(c * size, size)
+
+    far = flip(me, 2)
+
+    def copy(kind, c):
+        r = rows_of(c)
+        if kind == 0:
+            src, dst, dev = part.at[flip(me, 3), r], core_in.at[0, r], core
+        elif kind == 1:
+            src, dst, dev = part.at[flip(me, 1), r], core_in.at[1, r], core
+        elif kind == 2:
+            src, dst, dev = out_x.at[r], in_x.at[r], across
+        elif kind == 3:
+            src, dst, dev = low.at[r], full_two.at[me, r], across
+        elif kind == 4:
+            src, dst, dev = low.at[r], full_two.at[me, r], core
+        else:
+            src, dst, dev = full_two.at[far, r], full_two.at[far, r], core
+        return remote(src, dst, row_send.at[kind, c], row_recv.at[kind, c], dev)
+
+    def store(c):
+        r = rows_of(c)
+        return pltpu.make_async_copy(low.at[r], full_two.at[me, r], row_own.at[c])
+
+    branch(3)
+    for c in range(chunks):
+        copy(0, c).start()
+    branch(2)
+    for c in range(chunks):
+        r = rows_of(c)
+        copy(0, c).wait_recv()
+        out_x[r, :] = (part[far, r, :].astype(F32) + core_in[0, r, :].astype(F32)).astype(BF16)
+        copy(2, c).start()
+    branch(1)
+    for c in range(chunks):
+        copy(1, c).start()
+    branch(0)
+    run_steps(rest, *later[0])
+    for c in range(chunks):
+        r = rows_of(c)
+        copy(1, c).wait_recv()
+        copy(2, c).wait_recv()
+
+        def finish_rows(n, carry, c=c):
+            s = pl.ds(pl.multiple_of(c * size + n * step_rows, step_rows), step_rows)
+            value = own_tok[s, :].astype(F32) + (
+                part[me, s, :].astype(F32) + core_in[1, s, :].astype(F32) + in_x[s, :].astype(F32)
+            )
+            hidden[s, :] = value
+            normal, _ = norm_parts(value, EPSILON)
+            low[s, :] = (normal * gain_two[...] + bias_two[...]).astype(BF16)
+            return carry
+
+        lax.fori_loop(0, size // step_rows, finish_rows, 0)
+        copy(3, c).start()
+        copy(4, c).start()
+        store(c).start()
+        if c % 2:
+            run_steps(rest, *later[1 + c // 2])
+    for c in range(chunks):
+        copy(3, c).wait_recv()
+        copy(5, c).start()
+        if c % 2:
+            run_steps(rest, *later[3 + c // 2])
+    for c in range(chunks):
+        copy(4, c).wait_recv()
+        copy(5, c).wait_recv()
+        store(c).wait()
+        for kind in range(6):
+            copy(kind, c).wait_send()
+    run_steps(rest, *later[5])
+    for ring in rest:
+        ring.finish()
+    wait_sent(outs + rest, total)
+    own_copies[1].wait()
+    own_copies[2].wait()
+    pltpu.make_async_copy(x, o_normed, store_sem.at[0]).wait()
+    for c in stores:
+        c.wait()
+
+
+def forward(
+    total, own_up, w_out, w_down, full_in, tok, gain_one, bias_one, gain_group, tables, powers, ident_col, ident_row,
+    own_tok, gain_two, bias_two,
+):
+    rows, width = own_tok.shape
+    count = GROUP * rows
+    heads = HEADS // GROUP
+    vmem, hbm = pl.BlockSpec(memory_space=pltpu.VMEM), pl.BlockSpec(memory_space=ANY)
+    dma = pltpu.SemaphoreType.DMA
+    kept = (
+        ((count, width), BF16),
+        ((heads, count, QKH), BF16),
+        ((heads, count, QKH), BF16),
+        ((heads, count, VH), BF16),
+        ((heads, count, VH), F32),
+        ((heads, count, VH), F32),
+        ((count, heads * VH), BF16),
+    )
+    shapes = (
+        ((GROUP, total) + own_up.shape[1:], BF16),
+        ((total,) + w_out.shape, BF16),
+        ((total,) + w_down.shape, BF16),
+        *kept,
+        ((rows, width), F32),
+        ((GROUP, rows, width), BF16),
+    )
+    return pl.pallas_call(
+        functools.partial(forward_kernel, total),
+        out_shape=[jax.ShapeDtypeStruct(s, d) for s, d in shapes],
+        in_specs=[hbm] * 5 + [vmem] * 13,
+        out_specs=[hbm] * 10 + [vmem, hbm],
+        scratch_shapes=[
+            pltpu.VMEM((heads, width, 2 * QKH + 2 * VH), BF16),
+            pltpu.VMEM((GROUP, rows, width), BF16),
+            *[pltpu.VMEM(s, d) for s, d in kept],
+            pltpu.VMEM((total,) + w_out.shape, BF16),
+            pltpu.VMEM((2, rows, width), BF16),
+            pltpu.VMEM((rows, width), BF16),
+            pltpu.VMEM((rows, width), BF16),
+            pltpu.VMEM((rows, width), BF16),
+            dma((12, total - 1)), dma((12, total - 1)), dma((3,)), dma((GROUP + 1,)), dma((heads, 4)),
+            dma((7,)), dma((6, 4)), dma((6, 4)), dma((4,)),
+        ],
+        compiler_params=pltpu.CompilerParams(
+            collective_id=1, has_side_effects=True, vmem_limit_bytes=63 * MIB
+        ),
+        name="forward_retention",
+    )(
+        own_up, w_out, w_down, full_in, tok, gain_one, bias_one, gain_group, *tables, powers, ident_col,
+        ident_row, own_tok, gain_two, bias_two,
+    )
+
+
 class Ring:
     def __init__(self, at, way, source, local, arrived, loads, sends, recvs):
         self.at, self.way, self.source = at, way, source
@@ -487,108 +876,10 @@
     lax.fori_loop(1, total - 1, body, 0)
 
 
-RELATIONS = ((2, 0), (3, 1))
-
-
-def reduce_rest_kernel(
-    total, g_up, g_out, g_down, o_up, o_out, o_down, l_up, r_up, l_od, r_od, stage, landed,
-    loads_up, send_up, recv_up, loads_od, send_od, recv_od, a2a_send, a2a_recv,
-):
-    at = Place(total)
-    me = at.group
-    greet([at.peer(r) for r in (1, 2, 3)] + [at.neighbour(0), at.neighbour(1)])
-    half = g_out.shape[1] // 2
-    rings, kinds = [], []
-    for order in (0, 1):
-        for way in (0, 1):
-            relation = RELATIONS[way][order]
-            slot = 2 * way + order
-            rings.append(
-                Ring(
-                    at, way,
-                    lambda which, relation=relation: g_up.at[flip(me, relation), which],
-                    l_up.at[slot], r_up.at[slot], loads_up.at[slot], send_up.at[slot], recv_up.at[slot],
-                )
-            )
-            kinds.append(("up", relation))
-    for number, source in enumerate((g_out, g_down)):
-        for way in (0, 1):
-            slot = 2 * number + way
-            rings.append(
-                Ring(
-                    at, way,
-                    lambda which, source=source, way=way: source.at[which, pl.ds(way * half, half)],
-                    l_od.at[slot], r_od.at[slot], loads_od.at[slot], send_od.at[slot], recv_od.at[slot],
-                )
-            )
-            kinds.append((number, way))
-    run_rings(rings, total)
-    width = o_up.shape[1] // GROUP
-
-    def across(relation):
-        return remote(
-            stage.at[relation - 1], landed.at[relation - 1],
-            a2a_send.at[relation - 1], a2a_recv.at[relation - 1], at.peer(relation),
-        )
-
-    for ring, (kind, what) in zip(rings, kinds):
-        value = ring.finish()
-        if kind == "up":
-            if what == 0:
-                o_up[:, pl.ds(pl.multiple_of(me * width, 128), width)] = value
-            else:
-                stage[what - 1] = value.astype(BF16)
-                across(what).start()
-        else:
-            out = (o_out, o_down)[kind]
-            out[pl.ds(what * half, half), :] = value
-    for relation in (1, 2, 3):
-        across(relation).wait_recv()
-        o_up[:, pl.ds(pl.multiple_of(flip(me, relation) * width, 128), width)] = landed[
-            relation - 1
-        ].astype(F32)
-    for relation in (1, 2, 3):
-        across(relation).wait_send()
-    close_rings(rings, total)
-
-
-def reduce_rest(total, g_up, g_out, g_down):
-    rows_up, width_up = g_up.shape[2:]
-    rows_out, width_out = g_out.shape[1:]
-    half = rows_out // 2
-    vmem = pl.BlockSpec(memory_space=pltpu.VMEM)
-    dma = pltpu.SemaphoreType.DMA
-    return pl.pallas_call(
-        functools.partial(reduce_rest_kernel, total),
-        out_shape=[
-            jax.ShapeDtypeStruct((rows_up, width_up * GROUP), F32),
-            jax.ShapeDtypeStruct((rows_out, width_out), F32),
-            jax.ShapeDtypeStruct((rows_out, width_out), F32),
-        ],
-        in_specs=[pl.BlockSpec(memory_space=ANY)] * 3,
-        out_specs=[vmem] * 3,
-        scratch_shapes=[
-            pltpu.VMEM((4, total, rows_up, width_up), BF16),
-            pltpu.VMEM((4, total - 1, rows_up, width_up), BF16),
-            pltpu.VMEM((4, total, half, width_out), BF16),
-            pltpu.VMEM((4, total - 1, half, width_out), BF16),
-            pltpu.VMEM((3, rows_up, width_up), BF16),
-            pltpu.VMEM((3, rows_up, width_up), BF16),
-            dma((4, total)), dma((4, total - 1)), dma((4, total - 1)),
-            dma((4, total)), dma((4, total - 1)), dma((4, total - 1)),
-            dma((3,)), dma((3,)),
-        ],
-        compiler_params=pltpu.CompilerParams(
-            collective_id=3, has_side_effects=True, vmem_limit_bytes=48 * MIB
-        ),
-        name="reduce_rest",
-    )(g_up, g_out, g_down)
-
-
 def reduce_in_kernel(
-    total, g_in, part, o_in, o_part, local, arrived, stage, landed,
+    total, g_in, part, up, o_in, o_part, o_up, up_in, local, arrived, stage, landed,
     core_in, own_part, out_x, in_x, loads, ring_send, ring_recv, a2a_send, a2a_recv,
-    row_send, row_recv, row_own,
+    row_send, row_recv, row_own, up_send, up_recv,
 ):
     at = Place(total)
     me = at.group
@@ -608,6 +899,13 @@
             relations.append(relation)
 
     count = part.shape[0]
+    up_width = up.shape[-1]
+
+    def up_copy(relation):
+        return remote(
+            up.at[flip(me, relation)], up_in.at[relation - 1],
+            up_send.at[relation - 1], up_recv.at[relation - 1], at.peer(relation),
+        )
 
     def row_copy(kind, n):
         if kind == 0:
@@ -627,6 +925,8 @@
         for kind in (0, 1):
             row_copy(kind, n).start()
             row_load(n, kind).start()
+    for relation in (1, 2, 3):
+        up_copy(relation).start()
 
     def send_rows():
         for n in range(count):
@@ -643,6 +943,14 @@
             o_part[n] = (
                 own_part[n, 1].astype(F32) + core_in[n, 1].astype(F32) + in_x[n].astype(F32)
             )
+        for relation in range(4):
+            if relation:
+                up_copy(relation).wait_recv()
+            value = up_in[relation - 1] if relation else up[me]
+            start = pl.multiple_of(flip(me, relation) * up_width, 128)
+            o_up[:, pl.ds(start, up_width)] = value.astype(F32)
+        for relation in (1, 2, 3):
+            up_copy(relation).wait_send()
 
     run_rings(rings, total, ((2, send_rows), (total - 2, take_rows)))
     pieces = column_pieces(o_in.shape[1])
@@ -676,7 +984,7 @@
             row_copy(kind, n).wait_send()
 
 
-def reduce_in(total, g_in, part):
+def reduce_in(total, g_in, part, up):
     rows, width = g_in.shape[2:]
     count, _, tokens, features = part.shape
     vmem = pl.BlockSpec(memory_space=pltpu.VMEM)
@@ -686,10 +994,12 @@
         out_shape=[
             jax.ShapeDtypeStruct((rows, width * GROUP), F32),
             jax.ShapeDtypeStruct((count, tokens, features), F32),
+            jax.ShapeDtypeStruct((up.shape[1], up.shape[2] * GROUP), F32),
         ],
-        in_specs=[pl.BlockSpec(memory_space=ANY)] * 2,
-        out_specs=[vmem] * 2,
+        in_specs=[pl.BlockSpec(memory_space=ANY)] * 2 + [vmem],
+        out_specs=[vmem] * 3,
         scratch_shapes=[
+            pltpu.VMEM((3,) + up.shape[1:], BF16),
             pltpu.VMEM((4, total, rows, width), BF16),
             pltpu.VMEM((4, total - 1, rows, width), BF16),
             pltpu.VMEM((3, rows, width), BF16),
@@ -700,13 +1010,13 @@
             pltpu.VMEM((count, tokens, features), BF16),
             dma((4, total)), dma((4, total - 1)), dma((4, total - 1)),
             dma((3,)), dma((3,)),
-            dma((count, 3)), dma((count, 3)), dma((count, 2)),
+            dma((count, 3)), dma((count, 3)), dma((count, 2)), dma((3,)), dma((3,)),
         ],
         compiler_params=pltpu.CompilerParams(
             collective_id=4, has_side_effects=True, vmem_limit_bytes=60 * MIB
         ),
         name="reduce_in",
-    )(g_in, part)
+    )(g_in, part, up)
 
 
 def reduce_vectors_kernel(total, vec, out, landed, mid, gathered, sends, recvs, far_send, far_recv):
@@ -808,18 +1118,6 @@
     rates = jnp.log1p(-(2.0 ** (-5.0 - heads.astype(F32))))
     powers = jnp.maximum(distance, 0).astype(F32)
     return jnp.where(linked[:, None], jnp.exp(rates[:, None, None] * powers[None])[None], 0.0)
-
-
-def dot(left, right):
-    return jnp.dot(left, right, preferred_element_type=F32)
-
-
-def dot_rows(left, right):
-    return lax.dot_general(left, right, (((0,), (0,)), ((), ())), preferred_element_type=F32)
-
-
-def dot_back(left, right):
-    return lax.dot_general(left, right, (((1,), (1,)), ((), ())), preferred_element_type=F32)
 
 
 def mean(values):
@@ -851,13 +1149,8 @@
 
     pack = jnp.concatenate([ln1_gain, ln1_bias, ln2_gain, ln2_bias, group_gain]).astype(F32)
     pack = jnp.pad(pack, (0, 1024 - pack.shape[0])).reshape(8, 128)
-    full_in, full_up, full_out, full_down, tok, cot, vec = gather_all(
-        total, w_in, w_up, w_out, w_down, tokens, cotangent, pack
-    )
+    full_in, own_up, tok, cot, vec = gather_all(total, w_in, w_up, tokens, cotangent, pack)
     full_in = full_in.reshape(width, -1)
-    full_up = full_up.reshape(width, -1)
-    full_out = full_out.reshape(-1, width)
-    full_down = full_down.reshape(-1, width)
     vec = vec.reshape(total, GROUP, 1024)
 
     def vector(number):
@@ -866,7 +1159,7 @@
 
     gain_one, bias_one, gain_two, bias_two = (vector(n) for n in range(4))
     gain_group = lax.dynamic_index_in_dim(vec, me, 1, keepdims=False)[:, 4 * small : 4 * small + large]
-    gain_group = gain_group.reshape(heads, VH)
+    gain_group = gain_group.reshape(heads, 1, VH)
 
     devices = jnp.arange(GROUP, dtype=jnp.int32) * total + inner
     ident, places = jax.vmap(lambda d: layout(seq_lens, seq_owner, seq_offset, d, rows))(devices)
@@ -874,28 +1167,21 @@
     own_valid = lax.dynamic_index_in_dim(valid, me, 0, keepdims=False)
     count = GROUP * rows
 
-    normal, _ = norm_parts(tok.astype(F32), EPSILON)
-    normed = (normal * gain_one + bias_one).astype(BF16).reshape(count, width)
-    project = dot(normed, full_in).reshape(GROUP, rows, -1)
-    cosine, sine, growth = rotation(places)
-    shrink = 1.0 / growth
-    query = rotate_xpos(project[..., :qk].reshape(GROUP, rows, heads, QKH), cosine, sine, growth)
-    query = (query * QKH ** (-0.5)).astype(BF16)
-    keys = rotate_xpos(
-        project[..., qk : 2 * qk].reshape(GROUP, rows, heads, QKH), cosine, sine, shrink
-    ).astype(BF16)
-    values = project[..., 2 * qk : 2 * qk + vv].reshape(GROUP, rows, heads, VH).astype(BF16)
-    gate = project[..., 2 * qk + vv :].reshape(GROUP, rows, heads, VH)
-    decay = decay_tables(ident, me * heads + jnp.arange(heads))
-    raw = jnp.einsum("bthd,bshd->bhts", query, keys, preferred_element_type=F32)
-    masked = (raw * decay).astype(BF16)
-    mixed = jnp.einsum("bhts,bshv->bthv", masked, values, preferred_element_type=F32)
-    group_normal, group_scale = norm_parts(mixed, GROUP_EPSILON)
-    sigmoid = jax.nn.sigmoid(gate)
-    silu = gate * sigmoid
-    gated = (silu * (group_normal * gain_group)).astype(BF16).reshape(count, vv)
-    branch = dot(gated, full_out).astype(BF16).reshape(GROUP, rows, width)
-    hidden, two = exchange_rows(total, False, branch, tokens, jnp.zeros((8, 128), F32), gain_two, bias_two)
+    tables = rotation(places.reshape(count))
+    tables = (*tables, 1.0 / tables[2])
+    distance = jnp.arange(rows)[:, None] - jnp.arange(rows)[None, :]
+    rates = jnp.log1p(-(2.0 ** (-5.0 - (me * heads + jnp.arange(heads)).astype(F32))))
+    powers = jnp.exp(rates[:, None, None] * jnp.maximum(distance, 0).astype(F32)[None])
+    powers = jnp.where(distance[None] >= 0, powers, 0.0)
+    (
+        full_up, full_out, full_down, normed, query, keys, values, gate, mixed, gated, hidden, two,
+    ) = forward(
+        total, own_up, w_out, w_down, full_in, tok, gain_one, bias_one, gain_group, tables, powers,
+        ident[:, :, None], ident[:, None, :], tokens, gain_two, bias_two,
+    )
+    full_up = full_up.reshape(width, -1)
+    full_out = full_out.reshape(-1, width)
+    full_down = full_down.reshape(-1, width)
     two = two.reshape(count, width)
     upper = dot(two, full_up)
     cdf = 0.5 * (1.0 + lax.erf(upper * (0.5**0.5)))
@@ -912,40 +1198,60 @@
         total, True, d_two, own_seed, hidden, gain_two, bias_two
     )
     d_branch = d_branch.reshape(count, width)
-    g_down = dot_rows(active, seed).astype(BF16).reshape(total, -1, width)
-    g_up = dot_rows(two, d_upper).astype(BF16).reshape(GROUP, total, small, -1)
-    g_out = dot_rows(gated, d_branch).astype(BF16).reshape(total, -1, width)
-    grad_up, grad_out, grad_down = reduce_rest(total, g_up, g_out, g_down)
-
-    d_gated = dot_back(d_branch, full_out).reshape(GROUP, rows, heads, VH)
-    d_silu = d_gated * (group_normal * gain_group)
+    def summed_over(value, dim):
+        return lax.psum_scatter(value, "fsdp", scatter_dimension=dim, tiled=True)
+
+    grad_down = summed_over(dot_rows(active, seed).astype(BF16), 0).astype(F32)
+    g_up = summed_over(dot_rows(two, d_upper).astype(BF16).reshape(GROUP, total * small, -1), 1)
+    grad_out = summed_over(dot_rows(gated, d_branch).astype(BF16), 0).astype(F32)
+
+    split = (heads, GROUP, rows)
+    query, keys, values = (v.reshape(split + v.shape[2:]) for v in (query, keys, values))
+    gate, mixed = gate.reshape(split + (VH,)), mixed.reshape(split + (VH,))
+    gains = gain_group[:, None]
+    linked = (ident[:, :, None] == ident[:, None, :]) & (ident[:, :, None] >= 0)
+    decay = jnp.where(linked[None], powers[:, None], 0.0)
+    masked = (jnp.einsum("hbtd,hbsd->hbts", query, keys, preferred_element_type=F32) * decay).astype(BF16)
+    d_gated = jnp.stack(
+        [dot_back(d_branch, full_out[h * VH : (h + 1) * VH]) for h in range(heads)]
+    ).reshape(split + (VH,))
+    group_normal, group_scale = norm_parts(mixed, GROUP_EPSILON)
+    sigmoid = jax.nn.sigmoid(gate)
+    silu = gate * sigmoid
+    d_silu = d_gated * (group_normal * gains)
     d_gate = d_silu * (sigmoid + silu * (1.0 - sigmoid))
     d_scaled = d_gated * silu
-    d_group = jnp.sum(d_scaled * group_normal, axis=(0, 1))
-    d_normal = d_scaled * gain_group
+    d_group = jnp.sum(d_scaled * group_normal, axis=(1, 2))
+    d_normal = d_scaled * gains
     d_mixed = group_scale * (
         d_normal - mean(d_normal) - group_normal * mean(d_normal * group_normal)
     )
     d_mixed = d_mixed.astype(BF16)
-    d_values = jnp.einsum("bhts,bthv->bshv", masked, d_mixed, preferred_element_type=F32)
-    d_masked = jnp.einsum("bthv,bshv->bhts", d_mixed, values, preferred_element_type=F32)
+    d_values = jnp.einsum("hbts,hbtv->hbsv", masked, d_mixed, preferred_element_type=F32)
+    d_masked = jnp.einsum("hbtv,hbsv->hbts", d_mixed, values, preferred_element_type=F32)
     d_raw = (d_masked * decay).astype(BF16)
-    d_query = jnp.einsum("bhts,bshd->bthd", d_raw, keys, preferred_element_type=F32)
-    d_keys = jnp.einsum("bhts,bthd->bshd", d_raw, query, preferred_element_type=F32)
-    d_query = rotate_back(d_query * QKH ** (-0.5), cosine, sine, growth)
-    d_keys = rotate_back(d_keys, cosine, sine, shrink)
-    d_project = jnp.concatenate(
-        [
-            d_query.astype(BF16).reshape(count, qk),
-            d_keys.astype(BF16).reshape(count, qk),
-            d_values.astype(BF16).reshape(count, vv),
-            d_gate.astype(BF16).reshape(count, vv),
-        ],
-        axis=1,
-    )
+    d_query = jnp.einsum("hbts,hbsd->hbtd", d_raw, keys, preferred_element_type=F32)
+    d_keys = jnp.einsum("hbts,hbtd->hbsd", d_raw, query, preferred_element_type=F32)
+    cosine, sine, growth, shrink = (t.reshape(GROUP, rows, -1) for t in tables)
+
+    def back(value, scale):
+        half = QKH // 2
+        first, second = value[..., :half], value[..., half:]
+        return jnp.concatenate(
+            [(first * cosine + second * sine) * scale, (second * cosine - first * sine) * scale], axis=-1
+        )
+
+    d_query = back(d_query * QKH ** (-0.5), growth).astype(BF16)
+    d_keys = back(d_keys, shrink).astype(BF16)
+    parts = [
+        value[h].reshape(count, -1).astype(BF16)
+        for value in (d_query, d_keys, d_values, d_gate)
+        for h in range(heads)
+    ]
+    d_project = jnp.concatenate(parts, axis=1)
     d_normed = dot_back(d_project, full_in).astype(BF16).reshape(GROUP, rows, width)
     g_in = dot_rows(normed, d_project).astype(BF16).reshape(GROUP, total, small, -1)
-    grad_in, own_rows = reduce_in(total, g_in, jnp.stack([d_normed, down]))
+    grad_in, own_rows, grad_up = reduce_in(total, g_in, jnp.stack([d_normed, down]), g_up)
     output = ((hidden + own_rows[1]) * own_valid).astype(BF16)
     e_one = own_rows[0]
     normal_one, scale_one = norm_parts(tokens.astype(F32), EPSILON)

time: 890 us -> 761 us (0.86)
  Pallas kernels: 633 us -> 503 us
  local copies, waits for them, and re-layouts: 81 us -> 59.7 us
  between operations: 1.91 us -> 14.8 us
    pallas_call x1, Pallas kernels: 259 us -> 140 us  [gather_all(): pl.pallas_call(functools.partial(gather_kernel, total), out_shape=[jax.Sh...]
    pallas_call x2 -> x1, Pallas kernels: 103 us -> 51.4 us  [exchange_rows(): pl.pallas_call(functools.partial(exchange_kernel, total, chunks, backward...]
    pallas_call x1, Pallas kernels: 124 us -> 144 us  [forward(): pl.pallas_call(functools.partial(forward_kernel, total), out_shape=[jax.S...]
    pallas_call x1, Pallas kernels: 138 us -> 155 us  [reduce_in(): pl.pallas_call(functools.partial(reduce_in_kernel, total), out_shape=[jax...]
    convert_element_type x3 -> x0, local copies, waits for them, and re-layouts: 16.3 us -> none  [the longest x1 6.26 us: local(): d_values.astype(BF16).reshape(count, vv)]
    reshape x3 -> x0, local copies, waits for them, and re-layouts: 11.1 us -> none  [the longest x1 5.41 us: local(): gate = project[..., 2 * qk + vv:].reshape(GROUP, rows, heads, VH)]
    another operation x2 -> x3, other arithmetic: 9.24 us -> 19.9 us  [the longest x1 7.59 us: local(): grad_in, own_rows = reduce_in(total, g_in, jnp.stack([d_normed, down]))]
    dot_general x4 -> x2, matrix products: 28.8 us -> 19.3 us  [dot(): return jnp.dot(left, right, preferred_element_type=F32)]
  transfers between devices with their start and end apart: 0 -> 3, of which waited for: 0 -> 0; matrix products, arithmetic and copies ran while one was open for 0% -> 23% of each run, Pallas kernels for 0% -> 29%
where the time goes in v2:
time: 761 us; the launch traced here: 747 us
  Pallas kernels  503 us (66%)
  matrix products  110 us (14%)
  local copies, waits for them, and re-layouts  59.7 us (8%)
  other arithmetic  58.8 us (8%)
  between operations  14.8 us (2%)
    pallas_call x1, Pallas kernels, reduce_in(): pl.pallas_call(functools.partial(reduce_in_kernel, total), out_shape=[jax...  155 us
    pallas_call x1, Pallas kernels, forward(): pl.pallas_call(functools.partial(forward_kernel, total), out_shape=[jax.S...  144 us
    pallas_call x1, Pallas kernels, gather_all(): pl.pallas_call(functools.partial(gather_kernel, total), out_shape=[jax.Sh...  140 us
    pallas_call x1, Pallas kernels, exchange_rows(): pl.pallas_call(functools.partial(exchange_kernel, total, chunks, backward...  51.4 us
    dot_general x4, matrix products, dot_rows(): lax.dot_general(left, right, (((0,), (0,)), ((), ())), preferred_element_...  41.2 us
    dot_general x5, matrix products, dot_back(): lax.dot_general(left, right, (((1,), (1,)), ((), ())), preferred_element_...  40.3 us
    unnamed x70, local copies, waits for them, and re-layouts  28.7 us
    dot_general x2, matrix products, dot(): return jnp.dot(left, right, preferred_element_type=F32)  19.3 us
  transfers between devices with their start and end apart: 3, of which 0 were waited for; matrix products, arithmetic and copies ran while one was open for 23% of the time, Pallas kernels for 29%

profile of v2, /device:TPU:1, one launch (start us, length us, event | category | flops | bytes accessed | tf_op | source)
XLA Modules:
  0.0 747.3 jit_solution(12996889806056798481)
XLA Ops:
  7.4 3.4 concatenate.22
  11.4 139.7 %gather_weights.1 = (bf16[4,8,64,3072]{3,2,1,0:T(8,128)(2,1)}, bf16[4,64,1024]{2,1,0:T(8,128)(2,1)}, bf16[4,256,2048]{2,1,0:T(8,128)(2,1)}, bf16[4,256,2048]{2,1,0:T(8,128)(2,1)}, f32[8,4,8,128]{3,2,1,0:T(8,128)}) custom-call(bf16[64,12288]{1,0:T(8,128)(2,1)} %w_in.1, bf16[64,4096]{1,0:T(8,128)(2,1)} %w_up.1, bf16[256,2048]{1,0:T(8,128)(2,1)} %own_tok.1, ...), custom_call_target="tpu_custom_call" | custom-call | tf_op jit(solution)/shard_map/gather_weights/pallas_call | solution.py:247
  154.6 3.1 multiply_sine_fusion.1
  163.8 144.3 %forward_retention.1 = (bf16[4,8,64,1024]{3,2,1,0:T(8,128)(2,1)}, bf16[8,128,2048]{2,1,0:T(8,128)(2,1)}, bf16[8,128,2048]{2,1,0:T(8,128)(2,1)}, bf16[1024,2048]{...) custom-call(bf16[4,64,1024]{2,1,0:T(8,128)(2,1)} %get-tuple-element., ...), custom_call_target="tpu_custom_call" | custom-call | tf_op jit(solution)/shard_map/forward_retention/pallas_call | solution.py:774
  308.1 9.7 %multiply_convert_fusion.1 = (bf16[1024,1024]{1,0:T(8,128)(2,1)}, f32[1024,1024]{1,0:T(8,128)S(1)}) fusion(bf16[1024,2048]{1,0:T(8,128)(2,1)} %bitcast.154, bf16[2048,1024]{1,0:T(8,128)(2,1)} %bitcast.152), kind=kOutput, calls=%fused_computation.13 | convolution fusion | flops 4300210176 | bytes 14680064 | tf_op jit(solution)/shard_map/dot_general | solution.py:94
  318.6 2.7 copy-done.23
  321.2 5.8 fusion.5
  327.1 6.2 convolution_convert_fusion.4
  334.8 7.5 %convolution_convert_fusion.6 = bf16[1024,2048]{1,0:T(8,128)(2,1)S(1)} fusion(bf16[1024,1024]{1,0:T(8,128)(2,1)} %copy-done.28, bf16[2048,1024]{1,0:T(8,128)(2,1)} %bitcast.153), kind=kOutput, calls=%fused_computation.27 | convolution fusion | flops 4297064448 | bytes 10485760 | tf_op jit(solution)/shard_map/dot_general | solution.py:102
  342.3 51.4 %exchange_backward.1 = (f32[256,2048]{1,0:T(8,128)S(1)}, bf16[4,256,2048]{2,1,0:T(8,128)(2,1)S(1)}, f32[8,2048]{1,0:T(8,128)S(1)}) custom-call(bf16[4,256,2048]{2,1,0:T(8,128)(2,1)S(1)} %bitcast.110, bf16[256,2048]{1,0:T(8,128)(2,1)S(1)} %multiply_convert_fusion.4.extra, f32[256,2048]{1,0:T(8,128)S(1)} %copy-done, f32[1,2048]{1,0:T(1,128)S(1)} %copy-done.2, ...), custom_call_target="tpu_custom_call" | custom-call | tf_op jit(solution)/shard_map/exchange_backward/pallas_call | solution.py:374
  397.0 6.1 convolution_convert_fusion.3
  403.5 9.4 %convolution_convert_fusion.2 = bf16[1024,2048]{1,0:T(8,128)(2,1)} fusion(bf16[1024,1024]{1,0:T(8,128)(2,1)} %get-tuple-element.108, bf16[1024,2048]{1,0:T(8,128)(2,1)} %bitcast.129), kind=kOutput, calls=%fused_computation.23 | convolution fusion | flops 4297064448 | bytes 10485760 | tf_op jit(solution)/shard_map/dot_general | solution.py:98
  413.6 2.6 reduce_sum.119
  416.2 3.0 multiply_reduce_fusion.2
  419.6 3.3 multiply_cosine_fusion
  425.0 3.7 fusion.41
  428.7 3.7 fusion.40
  432.5 6.0 multiply_reduce_fusion
  438.6 8.2 %multiply_convert_fusion.2 = (bf16[2,4,256,512]{3,2,1,0:T(8,128)(2,1)}, bf16[2,4,256,512]{3,2,1,0:T(8,128)(2,1)S(1)}) fusion(f32[2,4,256,512]{3,2,1,0:T(8,128)} %bitcast.114, f32[1,4,256,512]{3,2,1,0:T(8,128)} %bitcast.120, f32[1,4,256,512]{3,2,1,0:T(8,128)} %bitcast.122, f32[2,4,256,512]{3,2,1,0:T(8,128)} %bitcast.115, f32[2,4,256]{2,1,0:T(4,128)S(1)} %div.90, ...), kind=kLoop, calls=%fused_computation.14 | loop fusion | flops 22020096 | bytes 16814080 | tf_op jit(solution)/shard_map/convert.4
  452.5 4.8 convolution_convert_fusion.7
  457.3 9.6 %convolution_convert_fusion.5 = bf16[1024,2048]{1,0:T(8,128)(2,1)} fusion(bf16[1024,1024]{1,0:T(8,128)(2,1)} %get-tuple-element.108, bf16[1024,2048]{1,0:T(8,128)(2,1)} %bitcast.150), kind=kOutput, calls=%fused_computation.26 | convolution fusion | flops 4297064448 | bytes 10485760 | tf_op jit(solution)/shard_map/dot_general | solution.py:94
  468.9 4.2 multiply_convert_fusion.5
  486.5 3.1 fusion.37
  498.0 2.3 constant_dynamic-update-slice_fusion.3
  503.8 19.6 %convolution_convert_fusion.1 = bf16[1024,2048]{1,0:T(8,128)(2,1)} fusion(bf16[1024,3072]{1,0:T(8,128)(2,1)} %constant_dynamic-update-slice_fusion, bf16[2048,3072]{1,0:T(8,128)(2,1)} %bitcast.117), kind=kOutput, calls=%fused_computation.22 | convolution fusion | flops 12886999040 | bytes 23068672 | tf_op jit(solution)/shard_map/dot_general | solution.py:102
  523.5 7.4 pad_maximum_fusion.part
  530.9 19.5 %convolution_convert_fusion = bf16[2048,3072]{1,0:T(8,128)(2,1)} fusion(bf16[1024,2048]{1,0:T(8,128)(2,1)} %get-tuple-element.39, bf16[1024,3072]{1,0:T(8,128)(2,1)} %constant_dynamic-update-slice_fusion), kind=kOutput, calls=%fused_computation | convolution fusion | flops 12891193344 | bytes 23068672 | tf_op jit(solution)/shard_map/dot_general | solution.py:98
  550.4 155.1 %reduce_in.1 = (f32[64,12288]{1,0:T(8,128)}, f32[2,256,2048]{2,1,0:T(8,128)}, f32[64,4096]{1,0:T(8,128)}) custom-call(bf16[4,8,64,3072]{3,2,1,0:T(8,128)(2,1)} %bitcast.118, bf16[2,4,256,2048]{3,2,1,0:T(8,128)(2,1)} %pad_maximum_fusion.part, bf16[4,64,1024]{2,1,0:T(8,128)(2,1)} %reduce-scatter.4.cloned.1.call-done.up), custom_call_target="tpu_custom_call" | custom-call | tf_op jit(solution)/shard_map/reduce_in/pallas_call | solution.py:992
  707.3 2.5 fusion.17
  710.7 12.8 %reduce_vectors.1 = f32[8,128]{1,0:T(8,128)} custom-call(f32[4,8,8,128]{3,2,1,0:T(8,128)} %copy.76), custom_call_target="tpu_custom_call" | custom-call | tf_op jit(solution)/shard_map/reduce_vectors/pallas_call | solution.py:1059
  728.3 5.1 fusion.16
  735.6 3.8 copy.87
  (157 shorter events, 62.9 us)
Async XLA Ops:
  7.2 146.9 %copy-start.27 = (s32[64]{0:T(128)S(1)}, s32[64]{0:T(128)}, u32[]{:S(2)}) copy-start(s32[64]{0:T(128)} %param.25) | copy-start | bytes 772
  7.2 146.9 %copy-start.21 = (s32[64]{0:T(128)S(1)}, s32[64]{0:T(128)}, u32[]{:S(2)}) copy-start(s32[64]{0:T(128)} %param.27) | copy-start | bytes 772
  7.2 147.1 %copy-start.22 = (s32[64]{0:T(128)S(1)}, s32[64]{0:T(128)}, u32[]{:S(2)}) copy-start(s32[64]{0:T(128)} %param.26) | copy-start | bytes 772
  7.2 543.2 %reduce-scatter.4.cloned.1.call-start = ((), (), s32[]{:S(2)}) async-start(), calls=%async_computation.3 | async-start | bytes 4718592 | tf_op jit(solution)/shard_map/reduce_scatter | solution.py:1202
  308.1 9.7 %copy-start.14 = (bf16[4,256,2048]{2,1,0:T(8,128)(2,1)S(1)}, bf16[4,256,2048]{2,1,0:T(8,128)(2,1)}, u32[]{:S(2)}) copy-start(bf16[4,256,2048]{2,1,0:T(8,128)(2,1)} %get-tuple-element.41) | copy-start | bytes 12582916
  317.8 3.4 copy-start.23
  318.6 8.5 %copy-start.15 = (bf16[4,256,2048]{2,1,0:T(8,128)(2,1)}, bf16[4,256,2048]{2,1,0:T(8,128)(2,1)S(1)}, u32[]{:S(2)}) copy-start(bf16[4,256,2048]{2,1,0:T(8,128)(2,1)S(1)} %multiply_convert_fusion) | copy-start | bytes 12582916
  321.2 5.8 copy-start.24
  327.1 6.2 copy-start.28
  333.3 1.2 copy-start.10
  333.3 390.2 %reduce-scatter.6.cloned.1.call-start = ((), (), s32[]{:S(2)}) async-start(), calls=%async_computation.4 | async-start | bytes 4718592 | tf_op jit(solution)/shard_map/reduce_scatter | solution.py:1202
  334.8 7.5 %copy-start = (f32[256,2048]{1,0:T(8,128)S(1)}, f32[256,2048]{1,0:T(8,128)}, u32[]{:S(2)}) copy-start(f32[256,2048]{1,0:T(8,128)} %get-tuple-element.38.hidden_in) | copy-start | bytes 6291460
  334.8 7.5 %copy-start.2 = (f32[1,2048]{1,0:T(1,128)S(1)}, f32[1,2048]{1,0:T(1,128)}, u32[]{:S(2)}) copy-start(f32[1,2048]{1,0:T(1,128)} %reshape.494.gain_two.gain) | copy-start | bytes 24580
  334.8 7.5 %copy-start.3 = (f32[1,2048]{1,0:T(1,128)S(1)}, f32[1,2048]{1,0:T(1,128)}, u32[]{:S(2)}) copy-start(f32[1,2048]{1,0:T(1,128)} %reshape.495.bias_two.bias) | copy-start | bytes 24580
  342.3 54.7 %copy-start.26 = (bf16[1024,1024]{1,0:T(8,128)(2,1)S(1)}, bf16[1024,1024]{1,0:T(8,128)(2,1)}, u32[]{:S(2)}) copy-start(bf16[1024,1024]{1,0:T(8,128)(2,1)} %get-tuple-element.54) | copy-start | bytes 6291460
  393.8 1.3 copy-start.1
  395.1 1.9 copy-start.4
  403.2 330.2 %reduce-scatter.8.cloned.1.call-start = ((), (), s32[]{:S(2)}) async-start(), calls=%async_computation.5 | async-start | bytes 4718592 | tf_op jit(solution)/shard_map/reduce_scatter | solution.py:1202
  412.9 0.7 copy-start.20
  416.2 6.7 copy-start.11
  422.9 2.2 copy-start.5
  438.6 8.3 %copy-start.9 = (f32[2,256,256]{2,1,0:T(8,128)S(1)}, f32[2,256,256]{2,1,0:T(8,128)}, u32[]{:S(2)}) copy-start(f32[2,256,256]{2,1,0:T(8,128)} %exponential_select_fusion.powers) | copy-start | bytes 1572868
  438.6 8.3 %copy-start.25 = (bf16[2,1024,512]{2,1,0:T(8,128)(2,1)S(1)}, bf16[2,1024,512]{2,1,0:T(8,128)(2,1)}, u32[]{:S(2)}) copy-start(bf16[2,1024,512]{2,1,0:T(8,128)(2,1)} %get-tuple-element.48) | copy-start | bytes 6291460
  446.8 3.8 copy-start.7
  446.8 2.0 copy-start.12
  446.9 3.8 copy-start.13
  457.3 9.6 %copy-start.6 = (bf16[256,2048]{1,0:T(8,128)(2,1)S(1)}, bf16[256,2048]{1,0:T(8,128)(2,1)}, u32[]{:S(2)}) copy-start(bf16[256,2048]{1,0:T(8,128)(2,1)} %own_tok.1) | copy-start | bytes 3145732
  486.5 3.1 copy-start.8
  491.8 8.6 %copy-start.17 = (bf16[1,4,256,512]{3,2,1,0:T(8,128)(2,1)S(1)}, bf16[1,4,256,512]{3,2,1,0:T(8,128)(2,1)}, u32[]{:S(2)}) copy-start(bf16[1,4,256,512]{3,2,1,0:T(8,128)(2,1)} %get-tuple-element.80) | copy-start | bytes 3145732
  491.8 9.8 %copy-start.18 = (bf16[1,4,256,512]{3,2,1,0:T(8,128)(2,1)S(1)}, bf16[1,4,256,512]{3,2,1,0:T(8,128)(2,1)}, u32[]{:S(2)}) copy-start(bf16[1,4,256,512]{3,2,1,0:T(8,128)(2,1)} %get-tuple-element.79) | copy-start | bytes 3145732
  493.9 8.8 %copy-start.16 = (bf16[1,4,256,512]{3,2,1,0:T(8,128)(2,1)S(1)}, bf16[1,4,256,512]{3,2,1,0:T(8,128)(2,1)}, u32[]{:S(2)}) copy-start(bf16[1,4,256,512]{3,2,1,0:T(8,128)(2,1)} %get-tuple-element.78) | copy-start | bytes 3145732
  733.4 6.0 copy-start.19
Sparse Core Ops, SparseCore 0:
  333.4 86.1 reduce-scatter.3
  423.7 87.7 reduce-scatter.5
  515.1 114.3 reduce-scatter.7

commit v3 on v2

--- a/solution.py
+++ b/solution.py
@@ -268,131 +268,6 @@
     return center * scale, scale
 
 
-def exchange_kernel(total, chunks, backward, part, extra, hidden_in, gain, bias, *refs):
-    if backward:
-        (keep, full, sums, core_in, out_x, in_x, low, own_part, sends, recvs, own_sem) = refs
-    else:
-        (keep, full, core_in, out_x, in_x, low, own_part, sends, recvs, own_sem) = refs
-    at = Place(total)
-    me = at.group
-    core, across = at.peer(1), at.peer(2)
-    rows = low.shape[0] // chunks
-    greet([core, across])
-    mine, far = me, flip(me, 2)
-
-    def rows_of(c):
-        return pl.ds(c * rows, rows)
-
-    def copy(kind, c):
-        r = rows_of(c)
-        if kind == 0:
-            src, dst, dev = part.at[flip(me, 3), r], core_in.at[0, r], core
-        elif kind == 1:
-            src, dst, dev = part.at[flip(me, 1), r], core_in.at[1, r], core
-        elif kind == 2:
-            src, dst, dev = out_x.at[r], in_x.at[r], across
-        elif kind == 3:
-            src, dst, dev = low.at[r], full.at[me, r], across
-        elif kind == 4:
-            src, dst, dev = low.at[r], full.at[me, r], core
-        else:
-            src, dst, dev = full.at[far, r], full.at[far, r], core
-        return remote(src, dst, sends.at[kind, c], recvs.at[kind, c], dev)
-
-    def load(which, c):
-        r = rows_of(c)
-        source = far if which == 0 else mine
-        return pltpu.make_async_copy(part.at[source, r], own_part.at[which, r], own_sem.at[which, c])
-
-    def store(c):
-        r = rows_of(c)
-        return pltpu.make_async_copy(low.at[r], full.at[me, r], own_sem.at[2, c])
-
-    for c in range(chunks):
-        copy(0, c).start()
-        load(0, c).start()
-    for c in range(chunks):
-        copy(1, c).start()
-        load(1, c).start()
-    for c in range(chunks):
-        r = rows_of(c)
-        load(0, c).wait()
-        copy(0, c).wait_recv()
-        out_x[r, :] = (own_part[0, r, :].astype(F32) + core_in[0, r, :].astype(F32)).astype(BF16)
-        copy(2, c).start()
-    if backward:
-        sums[...] = jnp.zeros_like(sums)
-    for c in range(chunks):
-        r = rows_of(c)
-        load(1, c).wait()
-        copy(1, c).wait_recv()
-        copy(2, c).wait_recv()
-        total_rows = (
-            own_part[1, r, :].astype(F32) + core_in[1, r, :].astype(F32) + in_x[r, :].astype(F32)
-        )
-        if backward:
-            normal, scale = norm_parts(hidden_in[r, :], EPSILON)
-            with_gain = total_rows * gain[...]
-            both = with_gain * normal
-            sums[0:1, :] += jnp.sum(total_rows * normal, axis=0, keepdims=True)
-            sums[1:2, :] += jnp.sum(total_rows, axis=0, keepdims=True)
-            result = extra[r, :].astype(F32) + scale * (
-                with_gain
-                - jnp.mean(with_gain, axis=-1, keepdims=True)
-                - normal * jnp.mean(both, axis=-1, keepdims=True)
-            )
-            keep[r, :] = result
-            low[r, :] = result.astype(BF16)
-        else:
-            hidden = extra[r, :].astype(F32) + total_rows
-            keep[r, :] = hidden
-            normal, scale = norm_parts(hidden, EPSILON)
-            low[r, :] = (normal * gain[...] + bias[...]).astype(BF16)
-        copy(3, c).start()
-        copy(4, c).start()
-        store(c).start()
-    for c in range(chunks):
-        copy(3, c).wait_recv()
-        copy(5, c).start()
-    for c in range(chunks):
-        copy(4, c).wait_recv()
-        copy(5, c).wait_recv()
-        store(c).wait()
-        for kind in range(6):
-            copy(kind, c).wait_send()
-
-
-def exchange_rows(total, backward, part, extra, hidden, gain, bias):
-    rows, width = extra.shape
-    chunks = 4
-    vmem = pl.BlockSpec(memory_space=pltpu.VMEM)
-    shapes = [jax.ShapeDtypeStruct((rows, width), F32), jax.ShapeDtypeStruct((GROUP, rows, width), BF16)]
-    specs = [vmem, pl.BlockSpec(memory_space=ANY)]
-    if backward:
-        shapes.append(jax.ShapeDtypeStruct((8, width), F32))
-        specs.append(vmem)
-    return pl.pallas_call(
-        functools.partial(exchange_kernel, total, chunks, backward),
-        out_shape=shapes,
-        in_specs=[pl.BlockSpec(memory_space=ANY)] + [vmem] * 4,
-        out_specs=specs,
-        scratch_shapes=[
-            pltpu.VMEM((2, rows, width), BF16),
-            pltpu.VMEM((rows, width), BF16),
-            pltpu.VMEM((rows, width), BF16),
-            pltpu.VMEM((rows, width), BF16),
-            pltpu.VMEM((2, rows, width), BF16),
-            pltpu.SemaphoreType.DMA((6, chunks)),
-            pltpu.SemaphoreType.DMA((6, chunks)),
-            pltpu.SemaphoreType.DMA((3, chunks)),
-        ],
-        compiler_params=pltpu.CompilerParams(
-            collective_id=2 if backward else 1, has_side_effects=True, vmem_limit_bytes=40 * MIB
-        ),
-        name="exchange_backward" if backward else "exchange_forward",
-    )(part, extra, hidden, gain, bias)
-
-
 RELATIONS = ((2, 0), (3, 1))
 
 
@@ -487,7 +362,7 @@
 def forward_kernel(
     total, own_up, w_out, w_down, full_in, tok, gain_one, bias_one, gain_group, cosine, sine, growth, shrink,
     powers, ident_col, ident_row, own_tok, gain_two, bias_two,
-    full_up, full_out, full_down, o_normed, o_query, o_keys, o_values, o_gate, o_mixed, o_gated, hidden, full_two,
+    full_up, full_out, full_down, o_turned, o_query, o_keys, o_values, o_gate, o_mixed, o_gated, hidden, full_two,
     win, part, x, query, keys, values, gate, mixed, gated, wo, core_in, out_x, in_x, low,
     ring_send, ring_recv, own_sem, load_sem, win_sem, store_sem, row_send, row_recv, row_own,
 ):
@@ -550,8 +425,6 @@
         return carry
 
     lax.fori_loop(0, GROUP, norm_buffer, 0)
-    pltpu.make_async_copy(x, o_normed, store_sem.at[0]).start()
-
     tile = 512
     spots = 6
     plan = tick_plan(total, spots)
@@ -702,6 +575,16 @@
         copy(1, c).start()
     branch(0)
     run_steps(rest, *later[0])
+
+    def turn(n, carry):
+        i, j = n // (count // 256), lax.rem(n, count // 256)
+        i, j = (pl.ds(pl.multiple_of(k * 256, 256), 256) for k in (i, j))
+        win[0, i, j] = x[j, i].T
+        return carry
+
+    lax.fori_loop(0, (width // 256) * (count // 256), turn, 0)
+    store_turned = pltpu.make_async_copy(win.at[0, :, pl.ds(0, count)], o_turned, store_sem.at[0])
+    store_turned.start()
     for c in range(chunks):
         r = rows_of(c)
         copy(1, c).wait_recv()
@@ -740,7 +623,7 @@
     wait_sent(outs + rest, total)
     own_copies[1].wait()
     own_copies[2].wait()
-    pltpu.make_async_copy(x, o_normed, store_sem.at[0]).wait()
+    store_turned.wait()
     for c in stores:
         c.wait()
 
@@ -755,7 +638,6 @@
     vmem, hbm = pl.BlockSpec(memory_space=pltpu.VMEM), pl.BlockSpec(memory_space=ANY)
     dma = pltpu.SemaphoreType.DMA
     kept = (
-        ((count, width), BF16),
         ((heads, count, QKH), BF16),
         ((heads, count, QKH), BF16),
         ((heads, count, VH), BF16),
@@ -767,6 +649,7 @@
         ((GROUP, total) + own_up.shape[1:], BF16),
         ((total,) + w_out.shape, BF16),
         ((total,) + w_down.shape, BF16),
+        ((width, count), BF16),
         *kept,
         ((rows, width), F32),
         ((GROUP, rows, width), BF16),
@@ -779,6 +662,7 @@
         scratch_shapes=[
             pltpu.VMEM((heads, width, 2 * QKH + 2 * VH), BF16),
             pltpu.VMEM((GROUP, rows, width), BF16),
+            pltpu.VMEM((count, width), BF16),
             *[pltpu.VMEM(s, d) for s, d in kept],
             pltpu.VMEM((total,) + w_out.shape, BF16),
             pltpu.VMEM((2, rows, width), BF16),
@@ -798,278 +682,771 @@
     )
 
 
-class Ring:
-    def __init__(self, at, way, source, local, arrived, loads, sends, recvs):
-        self.at, self.way, self.source = at, way, source
-        self.local, self.arrived = local, arrived
-        self.loads, self.sends, self.recvs = loads, sends, recvs
-
-    def load(self, which):
-        return pltpu.make_async_copy(self.source(which), self.local.at[which], self.loads.at[which])
+class Adding:
+    def __init__(self, at, way, term, arrived, sends, recvs):
+        self.at, self.way, self.term, self.arrived = at, way, term, arrived
+        self.sends, self.recvs = sends, recvs
 
     def hop(self, step, first=False):
-        src = self.local.at[self.at.behind(self.way, 1)] if first else self.arrived.at[step - 1]
+        src = self.term(self.at.behind(self.way, 1)) if first else self.arrived.at[step - 1]
         return remote(
             src, self.arrived.at[step], self.sends.at[step], self.recvs.at[step], self.at.neighbour(self.way)
         )
 
     def begin(self):
-        self.load(self.at.behind(self.way, 1)).wait()
         self.hop(0, True).start()
 
+    def sum_at(self, step, which):
+        self.hop(step, True).wait_recv()
+        return self.arrived[step].astype(F32) + self.term(which)[...].astype(F32)
+
     def onward(self, step):
-        which = self.at.behind(self.way, step + 1)
-        self.load(which).wait()
-        self.hop(step - 1, True).wait_recv()
-        self.arrived[step - 1] = (
-            self.arrived[step - 1].astype(F32) + self.local[which].astype(F32)
-        ).astype(BF16)
+        self.arrived[step - 1] = self.sum_at(step - 1, self.at.behind(self.way, step + 1)).astype(BF16)
         self.hop(step).start()
 
     def finish(self):
-        last = self.at.total - 2
-        self.load(self.at.inner).wait()
-        self.hop(last, True).wait_recv()
-        return self.arrived[last].astype(F32) + self.local[self.at.inner].astype(F32)
-
-    def sent(self, step):
-        self.hop(step, True).wait_send()
-
-
-def run_rings(rings, total, between=()):
-    at = rings[0].at
-    for ring in rings:
-        ring.load(at.behind(ring.way, 1)).start()
-
-    def loads(step, carry):
-        for ring in rings:
-            ring.load(at.behind(ring.way, step + 1)).start()
-        return carry
-
-    lax.fori_loop(1, total, loads, 0)
-    for ring in rings:
-        ring.begin()
-    marks = dict(between)
-    last = 1
-    for stop in sorted(marks) + [total - 1]:
-
-        def body(step, carry):
-            for ring in rings:
-                ring.onward(step)
-            return carry
-
-        lax.fori_loop(last, stop, body, 0)
-        last = stop
-        if stop in marks:
-            marks[stop]()
-
-
-def close_rings(rings, total):
-    for ring in rings:
-        ring.sent(0)
-
+        return self.sum_at(self.at.total - 2, self.at.inner)
+
+
+def wait_added(rings, total):
     def body(step, carry):
         for ring in rings:
-            ring.sent(step)
+            ring.hop(step, True).wait_send()
         return carry
 
-    lax.fori_loop(1, total - 1, body, 0)
-
-
-def reduce_in_kernel(
-    total, g_in, part, up, o_in, o_part, o_up, up_in, local, arrived, stage, landed,
-    core_in, own_part, out_x, in_x, loads, ring_send, ring_recv, a2a_send, a2a_recv,
-    row_send, row_recv, row_own, up_send, up_recv,
+    lax.fori_loop(0, total - 1, body, 0)
+
+
+def backward_kernel(
+    total, g_down, two, d_upper, part, seed, hidden, gain_two, h_gated, h_out, h_query, h_keys, h_values, h_gate,
+    h_mixed, cosine, sine, growth, shrink, powers, ident_col, ident_row, gain_group,
+    o_down, o_up, o_out, d_hidden, full_branch, sums, o_group, o_project,
+    g_up, g_out, arrived, wide_buf, narrow_buf, wo, own_part, core_in, out_x, in_x, low,
+    query, keys, values, gate, mixed, back, d_mixed, staged, stage, landed,
+    ring_send, ring_recv, row_send, row_recv, row_own, load_sem, unit_sem, out_sem, a2a_send, a2a_recv,
 ):
     at = Place(total)
     me = at.group
-    greet([at.peer(r) for r in (1, 2, 3)] + [at.neighbour(0), at.neighbour(1)])
-    rings, relations = [], []
+    core, across = at.peer(1), at.peer(2)
+    greet([core, across, at.peer(3), at.neighbour(0), at.neighbour(1)])
+    rows, width = seed.shape
+    count = GROUP * rows
+    heads = HEADS // GROUP
+    r_up, r_out = o_up.shape[0], o_out.shape[0]
+    up_width = o_up.shape[1] // GROUP
+    half, side = r_out // 2, width // 2
+
+    def halves(source, base):
+        return [
+            Adding(
+                at, way,
+                lambda which, way=way, c=c: source.at[
+                    pl.ds(pl.multiple_of(which * r_out + way * half, half), half), pl.ds(c * side, side)
+                ],
+                arrived.at[base + 2 * c + way], ring_send.at[base + 2 * c + way], ring_recv.at[base + 2 * c + way],
+            )
+            for c in (0, 1)
+            for way in (0, 1)
+        ]
+
+    downs, outs, ups = halves(g_down, 0), halves(g_out, 8), []
     for order in (0, 1):
         for way in (0, 1):
             relation = RELATIONS[way][order]
-            slot = 2 * way + order
-            rings.append(
-                Ring(
+            slot = 4 + 2 * order + way
+            ups.append(
+                Adding(
                     at, way,
-                    lambda which, relation=relation: g_in.at[flip(me, relation), which],
-                    local.at[slot], arrived.at[slot], loads.at[slot], ring_send.at[slot], ring_recv.at[slot],
+                    lambda which, relation=relation: g_up.at[
+                        pl.ds(pl.multiple_of((flip(me, relation) * total + which) * r_up, r_up), r_up), :
+                    ],
+                    arrived.at[slot], ring_send.at[slot], ring_recv.at[slot],
                 )
             )
-            relations.append(relation)
-
-    count = part.shape[0]
-    up_width = up.shape[-1]
-
-    def up_copy(relation):
-        return remote(
-            up.at[flip(me, relation)], up_in.at[relation - 1],
-            up_send.at[relation - 1], up_recv.at[relation - 1], at.peer(relation),
-        )
-
-    def row_copy(kind, n):
+
+    chunks = 4
+    size = rows // chunks
+    step_rows = 32
+    far = flip(me, 2)
+
+    def rows_of(c):
+        return pl.ds(c * size, size)
+
+    def copy(kind, c):
+        r = rows_of(c)
         if kind == 0:
-            src, dst, dev = part.at[n, flip(me, 3)], core_in.at[n, 0], at.peer(1)
+            src, dst, dev = part.at[flip(me, 3), r], core_in.at[0, r], core
         elif kind == 1:
-            src, dst, dev = part.at[n, flip(me, 1)], core_in.at[n, 1], at.peer(1)
+            src, dst, dev = part.at[flip(me, 1), r], core_in.at[1, r], core
+        elif kind == 2:
+            src, dst, dev = out_x.at[r], in_x.at[r], across
+        elif kind == 3:
+            src, dst, dev = low.at[r], full_branch.at[me, r], across
+        elif kind == 4:
+            src, dst, dev = low.at[r], full_branch.at[me, r], core
         else:
-            src, dst, dev = out_x.at[n], in_x.at[n], at.peer(2)
-        return remote(src, dst, row_send.at[n, kind], row_recv.at[n, kind], dev)
-
-    def row_load(n, which):
-        return pltpu.make_async_copy(
-            part.at[n, flip(me, 2) if which == 0 else me], own_part.at[n, which], row_own.at[n, which]
-        )
-
-    for n in range(count):
-        for kind in (0, 1):
-            row_copy(kind, n).start()
-            row_load(n, kind).start()
-    for relation in (1, 2, 3):
-        up_copy(relation).start()
-
-    def send_rows():
-        for n in range(count):
-            row_load(n, 0).wait()
-            row_copy(0, n).wait_recv()
-            out_x[n] = (own_part[n, 0].astype(F32) + core_in[n, 0].astype(F32)).astype(BF16)
-            row_copy(2, n).start()
-
-    def take_rows():
-        for n in range(count):
-            row_load(n, 1).wait()
-            row_copy(1, n).wait_recv()
-            row_copy(2, n).wait_recv()
-            o_part[n] = (
-                own_part[n, 1].astype(F32) + core_in[n, 1].astype(F32) + in_x[n].astype(F32)
+            src, dst, dev = full_branch.at[far, r], full_branch.at[far, r], core
+        return remote(src, dst, row_send.at[kind, c], row_recv.at[kind, c], dev)
+
+    def load(which, c):
+        r = rows_of(c)
+        source = far if which == 0 else me
+        return pltpu.make_async_copy(part.at[source, r], own_part.at[which, r], row_own.at[which, c])
+
+    def store(c):
+        r = rows_of(c)
+        return pltpu.make_async_copy(low.at[r], full_branch.at[me, r], row_own.at[2, c])
+
+    for which in (0, 1):
+        for c in range(chunks):
+            copy(which, c).start()
+            load(which, c).start()
+    for ring in downs:
+        ring.begin()
+    fetch_two = pltpu.make_async_copy(two, wide_buf, load_sem.at[0])
+    fetch_upper = pltpu.make_async_copy(d_upper, narrow_buf, load_sem.at[1])
+    fetch_out = pltpu.make_async_copy(h_out, wo, load_sem.at[2])
+    for fetch in (fetch_two, fetch_upper, fetch_out):
+        fetch.start()
+
+    def unit_loads(unit, slot):
+        h, b = unit // GROUP, lax.rem(unit, GROUP)
+        r = pl.ds(pl.multiple_of(b * rows, rows), rows)
+        pairs = ((h_query, query), (h_keys, keys), (h_values, values), (h_gate, gate), (h_mixed, mixed))
+        return [
+            pltpu.make_async_copy(src.at[h, r], dst.at[slot], unit_sem.at[slot, n])
+            for n, (src, dst) in enumerate(pairs)
+        ]
+
+    for unit in (0, 1):
+        for fetch in unit_loads(jnp.int32(unit), unit):
+            fetch.start()
+
+    def send_sums(c):
+        r = rows_of(c)
+        load(0, c).wait()
+        copy(0, c).wait_recv()
+        out_x[r, :] = (own_part[0, r, :].astype(F32) + core_in[0, r, :].astype(F32)).astype(BF16)
+        copy(2, c).start()
+
+    def norm_back(c):
+        load(1, c).wait()
+        copy(1, c).wait_recv()
+        copy(2, c).wait_recv()
+
+        def some_rows(n, carry):
+            s = pl.ds(pl.multiple_of(c * size + n * step_rows, step_rows), step_rows)
+            e = own_part[1, s, :].astype(F32) + core_in[1, s, :].astype(F32) + in_x[s, :].astype(F32)
+            normal, scale = norm_parts(hidden[s, :], EPSILON)
+            with_gain = e * gain_two[...]
+            sums[0:1, :] += jnp.sum(e * normal, axis=0, keepdims=True)
+            sums[1:2, :] += jnp.sum(e, axis=0, keepdims=True)
+            value = seed[s, :].astype(F32) + scale * (
+                with_gain
+                - jnp.mean(with_gain, axis=-1, keepdims=True)
+                - normal * jnp.mean(with_gain * normal, axis=-1, keepdims=True)
             )
-        for relation in range(4):
-            if relation:
-                up_copy(relation).wait_recv()
-            value = up_in[relation - 1] if relation else up[me]
-            start = pl.multiple_of(flip(me, relation) * up_width, 128)
-            o_up[:, pl.ds(start, up_width)] = value.astype(F32)
-        for relation in (1, 2, 3):
-            up_copy(relation).wait_send()
-
-    run_rings(rings, total, ((2, send_rows), (total - 2, take_rows)))
-    pieces = column_pieces(o_in.shape[1])
-
-    def place(other, value):
-        for base, stride, off, width in pieces:
-            start = pl.multiple_of(base + other * stride, 128)
-            o_in[:, pl.ds(start, width)] = value[:, off : off + width]
-
-    def across(relation):
+            d_hidden[s, :] = value
+            low[s, :] = value.astype(BF16)
+            return carry
+
+        lax.fori_loop(0, size // step_rows, some_rows, 0)
+        copy(3, c).start()
+        copy(4, c).start()
+        store(c).start()
+
+    sums[...] = jnp.zeros_like(sums)
+    o_group[...] = jnp.zeros_like(o_group)
+    for c in range(chunks):
+        send_sums(c)
+    plan = tick_plan(total, 6)
+    add_steps(downs, *plan[0])
+    fetch_two.wait()
+    fetch_upper.wait()
+
+    def grad_tiles(left, right, out, start, stop):
+        wide = 512
+
+        def tile(n, carry):
+            rows_n = right.shape[1] // wide
+            i, j = n // rows_n, lax.rem(n, rows_n)
+            a = pl.ds(pl.multiple_of(i * 256, 256), 256)
+            c = pl.ds(pl.multiple_of(j * wide, wide), wide)
+            out[a, c] = dot_rows(left[:, a], right[:, c]).astype(BF16)
+            return carry
+
+        lax.fori_loop(start, stop, tile, 0)
+
+    tiles = (width // 256) * (up_width // 512)
+    for quarter in range(4):
+        grad_tiles(wide_buf, narrow_buf, g_up, tiles * quarter // 4, tiles * (quarter + 1) // 4)
+        if quarter:
+            norm_back(quarter - 1)
+        add_steps(downs, *plan[1 + quarter])
+    norm_back(3)
+    add_steps(downs, *plan[5])
+    for ring in ups:
+        ring.begin()
+    fetch_gated = pltpu.make_async_copy(h_gated, narrow_buf, load_sem.at[1])
+    fetch_gated.start()
+    for n, ring in enumerate(downs):
+        c, way = n // 2, n % 2
+        o_down[pl.ds(way * half, half), pl.ds(c * side, side)] = ring.finish()
+    for c in range(chunks):
+        copy(3, c).wait_recv()
+        copy(5, c).start()
+        if c % 2:
+            add_steps(ups, *plan[c // 2])
+    for c in range(chunks):
+        copy(4, c).wait_recv()
+        copy(5, c).wait_recv()
+        store(c).wait()
+    branch = wide_buf
+    fetch_branch = [
+        pltpu.make_async_copy(full_branch.at[b], branch.at[pl.ds(b * rows, rows)], load_sem.at[3 + b])
+        for b in range(GROUP)
+    ]
+    for fetch in fetch_branch:
+        fetch.start()
+    for fetch in fetch_branch:
+        fetch.wait()
+    fetch_gated.wait()
+    fetch_out.wait()
+    tiles = (narrow_buf.shape[1] // 256) * (width // 512)
+    for quarter in range(4):
+        grad_tiles(narrow_buf, branch, g_out, tiles * quarter // 4, tiles * (quarter + 1) // 4)
+        add_steps(ups, *plan[2 + quarter])
+    for ring in outs:
+        ring.begin()
+
+    def sent_across(relation):
         return remote(
             stage.at[relation - 1], landed.at[relation - 1],
             a2a_send.at[relation - 1], a2a_recv.at[relation - 1], at.peer(relation),
         )
 
-    for ring, relation in zip(rings, relations):
+    for n, ring in enumerate(ups):
+        relation = RELATIONS[n % 2][n // 2]
         value = ring.finish()
+        if relation == 0:
+            o_up[:, pl.ds(pl.multiple_of(me * up_width, 128), up_width)] = value
+        else:
+            stage[relation - 1] = value.astype(BF16)
+            sent_across(relation).start()
+
+    units = heads * GROUP
+    qk, vv = heads * QKH, heads * VH
+
+    def unit_stores(unit, slot):
+        h, b = unit // GROUP, lax.rem(unit, GROUP)
+        r = pl.ds(pl.multiple_of(b * rows, rows), rows)
+        table = (
+            (h * QKH, 0, QKH),
+            (qk + h * QKH, QKH, QKH),
+            (2 * qk + h * VH, 2 * QKH, VH),
+            (2 * qk + vv + h * VH, 2 * QKH + VH, VH),
+        )
+        return [
+            pltpu.make_async_copy(
+                staged.at[slot, :, pl.ds(off, size)],
+                o_project.at[r, pl.ds(pl.multiple_of(start, 128), size)],
+                out_sem.at[slot, n],
+            )
+            for n, (start, off, size) in enumerate(table)
+        ]
+
+    def unrotated(value, r, scale):
+        mid = QKH // 2
+        first, second = value[:, :mid], value[:, mid:]
+        c, s = cosine[r, :], sine[r, :]
+        return jnp.concatenate(
+            [(first * c + second * s) * scale, (second * c - first * s) * scale], axis=1
+        )
+
+    def unit_body(unit, carry):
+        slot = lax.rem(unit, 2)
+        h, b = unit // GROUP, lax.rem(unit, GROUP)
+        r = pl.ds(pl.multiple_of(b * rows, rows), rows)
+        back[...] = dot_back(branch[r, :], wo[pl.ds(pl.multiple_of(h * VH, VH), VH), :])
+        for fetch in unit_loads(unit, slot):
+            fetch.wait()
+
+        @pl.when(unit >= 2)
+        def _():
+            for done in unit_stores(unit - 2, slot):
+                done.wait()
+
+        gains = gain_group[h]
+
+        def some_rows(n, carry):
+            s = pl.ds(pl.multiple_of(n * step_rows, step_rows), step_rows)
+            normal, scale = norm_parts(mixed[slot, s, :], GROUP_EPSILON)
+            z = gate[slot, s, :]
+            f = back[s, :]
+            sigmoid = 1.0 / (1.0 + jnp.exp(-z))
+            silu = z * sigmoid
+            d_silu = f * (normal * gains)
+            staged[slot, s, 2 * QKH + VH :] = (d_silu * (sigmoid + silu * (1.0 - sigmoid))).astype(BF16)
+            d_scaled = f * silu
+            o_group[h] += jnp.sum(d_scaled * normal, axis=0, keepdims=True)
+            d_normal = d_scaled * gains
+            d_mixed[s, :] = (
+                scale
+                * (
+                    d_normal
+                    - jnp.mean(d_normal, axis=-1, keepdims=True)
+                    - normal * jnp.mean(d_normal * normal, axis=-1, keepdims=True)
+                )
+            ).astype(BF16)
+            return carry
+
+        lax.fori_loop(0, rows // step_rows, some_rows, 0)
+        linked = (ident_col[b] == ident_row[b]) & (ident_col[b] >= 0)
+        decay = jnp.where(linked, powers[h], 0.0)
+        masked = (dot_back(query[slot], keys[slot]) * decay).astype(BF16)
+        staged[slot, :, 2 * QKH : 2 * QKH + VH] = dot_rows(masked, d_mixed[...]).astype(BF16)
+        d_raw = (dot_back(d_mixed[...], values[slot]) * decay).astype(BF16)
+        d_query = dot(d_raw, keys[slot]) * QKH ** (-0.5)
+        staged[slot, :, :QKH] = unrotated(d_query, r, growth[r, :]).astype(BF16)
+        d_keys = dot_rows(d_raw, query[slot])
+        staged[slot, :, QKH : 2 * QKH] = unrotated(d_keys, r, shrink[r, :]).astype(BF16)
+        for done in unit_stores(unit, slot):
+            done.start()
+
+        @pl.when(unit + 2 < units)
+        def _():
+            for fetch in unit_loads(unit + 2, slot):
+                fetch.start()
+
+        steps = total - 2
+        add_steps(outs, 1 + (steps * unit) // units, 1 + (steps * (unit + 1)) // units)
+        return carry
+
+    lax.fori_loop(0, units, unit_body, 0)
+    for relation in (1, 2, 3):
+        sent_across(relation).wait_recv()
+        o_up[:, pl.ds(pl.multiple_of(flip(me, relation) * up_width, 128), up_width)] = landed[
+            relation - 1
+        ].astype(F32)
+        sent_across(relation).wait_send()
+    for slot in (0, 1):
+        for done in unit_stores(jnp.int32(units - 2 + slot), slot):
+            done.wait()
+    for n, ring in enumerate(outs):
+        c, way = n // 2, n % 2
+        o_out[pl.ds(way * half, half), pl.ds(c * side, side)] = ring.finish()
+    for c in range(chunks):
+        for kind in range(6):
+            copy(kind, c).wait_send()
+    wait_added(downs + ups + outs, total)
+
+
+def add_steps(rings, start, stop):
+    def body(step, carry):
+        for ring in rings:
+            ring.onward(step)
+        return carry
+
+    lax.fori_loop(start, stop, body, 0)
+
+
+def backward(
+    total, g_down, two, d_upper, part, seed, hidden, gain_two, gated, full_out, query, keys, values, gate, mixed,
+    tables, powers, ident_col, ident_row, gain_group,
+):
+    rows, width = seed.shape
+    count = GROUP * rows
+    heads = HEADS // GROUP
+    up_width = d_upper.shape[1]
+    r_out, r_up = g_down.shape[0] // total, width // GROUP // total
+    half, side = r_out // 2, width // 2
+    vmem, hbm = pl.BlockSpec(memory_space=pltpu.VMEM), pl.BlockSpec(memory_space=ANY)
+    dma = pltpu.SemaphoreType.DMA
+    shapes = (
+        ((r_out, width), F32),
+        ((r_up, up_width * GROUP), F32),
+        ((r_out, width), F32),
+        ((rows, width), F32),
+        ((GROUP, rows, width), BF16),
+        ((8, width), F32),
+        ((heads, 1, VH), F32),
+        ((count, 2 * heads * (QKH + VH)), BF16),
+    )
+    return pl.pallas_call(
+        functools.partial(backward_kernel, total),
+        out_shape=[jax.ShapeDtypeStruct(s, d) for s, d in shapes],
+        in_specs=[vmem, hbm, hbm, hbm, vmem, vmem, vmem] + [hbm] * 7 + [vmem] * 8,
+        out_specs=[vmem] * 4 + [hbm, vmem, vmem, hbm],
+        scratch_shapes=[
+            pltpu.VMEM((width, up_width), BF16),
+            pltpu.VMEM(g_down.shape, BF16),
+            pltpu.VMEM((12, total - 1, half, side), BF16),
+            pltpu.VMEM((count, width), BF16),
+            pltpu.VMEM((count, up_width), BF16),
+            pltpu.VMEM(full_out.shape, BF16),
+            pltpu.VMEM((2, rows, width), BF16),
+            pltpu.VMEM((2, rows, width), BF16),
+            pltpu.VMEM((rows, width), BF16),
+            pltpu.VMEM((rows, width), BF16),
+            pltpu.VMEM((rows, width), BF16),
+            pltpu.VMEM((2, rows, QKH), BF16),
+            pltpu.VMEM((2, rows, QKH), BF16),
+            pltpu.VMEM((2, rows, VH), BF16),
+            pltpu.VMEM((2, rows, VH), F32),
+            pltpu.VMEM((2, rows, VH), F32),
+            pltpu.VMEM((rows, VH), F32),
+            pltpu.VMEM((rows, VH), BF16),
+            pltpu.VMEM((2, rows, 2 * (QKH + VH)), BF16),
+            pltpu.VMEM((3, r_up, up_width), BF16),
+            pltpu.VMEM((3, r_up, up_width), BF16),
+            dma((12, total - 1)), dma((12, total - 1)), dma((6, 4)), dma((6, 4)), dma((3, 4)), dma((7,)),
+            dma((2, 5)), dma((2, 4)), dma((3,)), dma((3,)),
+        ],
+        compiler_params=pltpu.CompilerParams(
+            collective_id=2, has_side_effects=True, vmem_limit_bytes=63 * MIB
+        ),
+        name="backward_retention",
+    )(
+        g_down, two, d_upper, part, seed, hidden, gain_two, gated, full_out, query, keys, values, gate, mixed,
+        *tables, powers, ident_col, ident_row, gain_group,
+    )
+
+
+def final_kernel(
+    total, h_project, h_in, h_turned, part_down, hidden, d_hidden, tok, gain_one, valid, sums_two, d_group,
+    o_in, output, d_tokens, o_vec, o_grp,
+    project, turned, first_term, term, arrived, win, part, own_part, core_in, out_x, in_x, stage, landed,
+    vec, grp, near_in, mid, far_in, far_grp,
+    load_sem, win_sem, ring_send, ring_recv, a2a_send, a2a_recv, row_send, row_recv, row_own,
+    near_send, near_recv, far_send, far_recv,
+):
+    at = Place(total)
+    me, inner = at.group, at.inner
+    others = [(me, lax.rem(inner + n, total)) for n in range(1, total)]
+    greet([at.peer(r) for r in (1, 2, 3)] + others)
+    rows, width = tok.shape
+    count = GROUP * rows
+    block = o_in.shape[0]
+    step_rows = 32
+
+    fetch_turned = pltpu.make_async_copy(h_turned, turned, load_sem.at[0])
+    fetch_project = pltpu.make_async_copy(h_project, project, load_sem.at[1])
+    fetch_turned.start()
+    fetch_project.start()
+
+    def source(n, b):
+        if n == 0:
+            return part_down.at[b]
+        return part.at[pl.ds(pl.multiple_of(b * rows, rows), rows), :]
+
+    def row_copy(kind, n):
+        if kind < 2:
+            return remote(
+                source(n, flip(me, 3 - 2 * kind)), core_in.at[n, kind], row_send.at[n, kind], row_recv.at[n, kind],
+                at.peer(1),
+            )
+        return remote(out_x.at[n], in_x.at[n], row_send.at[n, 2], row_recv.at[n, 2], at.peer(2))
+
+    def row_load(which):
+        return pltpu.make_async_copy(
+            source(0, flip(me, 2) if which == 0 else me), own_part.at[which], row_own.at[which]
+        )
+
+    def own_rows(n, which, r):
+        if n == 0:
+            return own_part[which, pl.ds(r, step_rows), :]
+        b = flip(me, 2) if which == 0 else me
+        return part[pl.ds(pl.multiple_of(b * rows + r, step_rows), step_rows), :]
+
+    def by_rows(body):
+        def some(k, carry):
+            body(pl.multiple_of(k * step_rows, step_rows))
+            return carry
+
+        lax.fori_loop(0, rows // step_rows, some, 0)
+
+    def send_rows(n):
+        row_copy(0, n).wait_recv()
+
+        def some(r):
+            s = pl.ds(r, step_rows)
+            out_x[n, s, :] = (own_rows(n, 0, r).astype(F32) + core_in[n, 0, s, :].astype(F32)).astype(BF16)
+
+        by_rows(some)
+        row_copy(2, n).start()
+
+    def summed_rows(n, r):
+        s = pl.ds(r, step_rows)
+        return own_rows(n, 1, r).astype(F32) + core_in[n, 1, s, :].astype(F32) + in_x[n, s, :].astype(F32)
+
+    def take_down():
+        row_copy(1, 0).wait_recv()
+        row_copy(2, 0).wait_recv()
+
+        def some(r):
+            s = pl.ds(r, step_rows)
+            output[s, :] = ((hidden[s, :] + summed_rows(0, r)) * valid[s, :]).astype(BF16)
+
+        by_rows(some)
+
+    def take_rows():
+        row_copy(1, 1).wait_recv()
+        row_copy(2, 1).wait_recv()
+        vec[...] = jnp.zeros_like(vec)
+        vec[2:4, :] = sums_two[0:2, :]
+
+        def some(r):
+            s = pl.ds(r, step_rows)
+            e = summed_rows(1, r)
+            normal, scale = norm_parts(tok[s, :].astype(F32), EPSILON)
+            with_gain = e * gain_one[...]
+            vec[0:1, :] += jnp.sum(e * normal, axis=0, keepdims=True)
+            vec[1:2, :] += jnp.sum(e, axis=0, keepdims=True)
+            value = d_hidden[s, :] + scale * (
+                with_gain
+                - jnp.mean(with_gain, axis=-1, keepdims=True)
+                - normal * jnp.mean(with_gain * normal, axis=-1, keepdims=True)
+            )
+            d_tokens[s, :] = value.astype(BF16)
+
+        by_rows(some)
+
+    quarter = width // GROUP
+    small = quarter // total
+    large = grp.shape[1] // total
+
+    def near(relation):
+        start = pl.multiple_of(flip(me, relation) * quarter, 128)
+        return remote(
+            vec.at[:, pl.ds(start, quarter)], near_in.at[relation - 1], near_send.at[relation - 1],
+            near_recv.at[relation - 1], at.peer(relation),
+        )
+
+    def tile_of(index, size):
+        return pl.ds(pl.multiple_of((index * size) // 128 * 128, 128), 128)
+
+    def distant(kind, n):
+        target = lax.rem(inner + n, total)
+        src = mid.at[:, tile_of(target, small)] if kind == 0 else grp.at[:, tile_of(target, large)]
+        dst = far_in if kind == 0 else far_grp
+        return remote(
+            src, dst.at[n - 1], far_send.at[kind, n - 1], far_recv.at[kind, n - 1], (me, target)
+        )
+
+    def vectors_near():
+        for relation in (1, 2, 3):
+            near(relation).start()
+        grp[...] = jnp.zeros_like(grp)
+        for h in range(d_group.shape[0]):
+            grp[0:1, h * VH : (h + 1) * VH] = d_group[h]
+
+    def vectors_far():
+        for relation in (1, 2, 3):
+            near(relation).wait_recv()
+        mid[...] = (
+            vec[:, pl.ds(pl.multiple_of(me * quarter, 128), quarter)] + near_in[0] + near_in[1] + near_in[2]
+        )
+        for n in range(1, total):
+            for kind in (0, 1):
+                distant(kind, n).start()
+
+    def vectors_end():
+        for n in range(1, total):
+            for kind in (0, 1):
+                distant(kind, n).wait_recv()
+        o_vec[...] = mid[:, tile_of(inner, small)] + jnp.sum(far_in[...], axis=0)
+        o_grp[...] = grp[:, tile_of(inner, large)] + jnp.sum(far_grp[...], axis=0)
+
+    wide = 512
+
+    def terms(step, out):
+        for way in (0, 1):
+            which = at.behind(way, step + 1)
+            left = jnp.concatenate(
+                [
+                    turned[
+                        pl.ds(pl.multiple_of((flip(me, relation) * total + which) * block, block), block), :
+                    ]
+                    for relation in RELATIONS[way]
+                ],
+                axis=0,
+            )
+
+            def tile(n, carry, left=left, way=way):
+                c = pl.ds(pl.multiple_of(n * wide, wide), wide)
+                value = dot(left, project[:, c]).astype(BF16)
+                out[2 * way, :, c] = value[:block]
+                out[2 * way + 1, :, c] = value[block:]
+                return carry
+
+            lax.fori_loop(0, project.shape[1] // wide, tile, 0)
+
+    def hop(slot, step, first=False):
+        src = first_term.at[slot] if first else arrived.at[slot, step - 1]
+        return remote(
+            src, arrived.at[slot, step], ring_send.at[slot, step], ring_recv.at[slot, step],
+            at.neighbour(slot // 2),
+        )
+
+    order = (0, 2, 1, 3)
+
+    def onward(step, carry):
+        terms(step, term)
+        for slot in order:
+            hop(slot, step - 1, True).wait_recv()
+            arrived[slot, step - 1] = (
+                arrived[slot, step - 1].astype(F32) + term[slot].astype(F32)
+            ).astype(BF16)
+            hop(slot, step).start()
+        return carry
+
+    def fetch_win(n):
+        return pltpu.make_async_copy(
+            h_in.at[pl.ds(n * 256, 256), :], win.at[n % 2], win_sem.at[n % 2]
+        )
+
+    columns = width // 256
+
+    def row_tiles(n):
+        fetch_win(n).wait()
+
+        def tile(m, carry):
+            r = pl.ds(pl.multiple_of(m * 512, 512), 512)
+            part[r, n * 256 : (n + 1) * 256] = dot_back(project[r, :], win[n % 2]).astype(BF16)
+            return carry
+
+        lax.fori_loop(0, count // 512, tile, 0)
+        if n + 2 < columns:
+            fetch_win(n + 2).start()
+
+    row_copy(0, 0).start()
+    row_copy(1, 0).start()
+    row_load(0).start()
+    row_load(1).start()
+    fetch_win(0).start()
+    fetch_win(1).start()
+    fetch_turned.wait()
+    fetch_project.wait()
+    terms(0, first_term)
+    for slot in order:
+        hop(slot, 0, True).start()
+    row_load(0).wait()
+    send_rows(0)
+    plan = tick_plan(total, 6)
+
+    def extra(number):
+        if number < 4:
+            for n in range(columns * number // 4, columns * (number + 1) // 4):
+                row_tiles(n)
+            if number == 3:
+                row_copy(0, 1).start()
+                row_copy(1, 1).start()
+        elif number == 4:
+            send_rows(1)
+            row_load(1).wait()
+            take_down()
+        else:
+            take_rows()
+            vectors_near()
+
+    for number in range(6):
+        extra(number)
+        lax.fori_loop(*plan[number], onward, 0)
+    vectors_far()
+    terms(total - 1, term)
+    pieces = column_pieces(o_in.shape[1])
+
+    def place(other, value):
+        for base, stride, off, size in pieces:
+            start = pl.multiple_of(base + other * stride, 128)
+            o_in[:, pl.ds(start, size)] = value[:, off : off + size]
+
+    def sent_across(relation):
+        return remote(
+            stage.at[relation - 1], landed.at[relation - 1],
+            a2a_send.at[relation - 1], a2a_recv.at[relation - 1], at.peer(relation),
+        )
+
+    for slot in order:
+        relation = RELATIONS[slot // 2][slot % 2]
+        hop(slot, total - 2, True).wait_recv()
+        value = arrived[slot, total - 2].astype(F32) + term[slot].astype(F32)
         if relation == 0:
             place(me, value)
         else:
             stage[relation - 1] = value.astype(BF16)
-            across(relation).start()
+            sent_across(relation).start()
+    vectors_end()
     for relation in (1, 2, 3):
-        across(relation).wait_recv()
+        sent_across(relation).wait_recv()
         place(flip(me, relation), landed[relation - 1].astype(F32))
     for relation in (1, 2, 3):
-        across(relation).wait_send()
-    close_rings(rings, total)
-    for n in range(count):
+        sent_across(relation).wait_send()
+        near(relation).wait_send()
+    for n in range(1, total):
+        for kind in (0, 1):
+            distant(kind, n).wait_send()
+    for n in (0, 1):
         for kind in (0, 1, 2):
             row_copy(kind, n).wait_send()
 
-
-def reduce_in(total, g_in, part, up):
-    rows, width = g_in.shape[2:]
-    count, _, tokens, features = part.shape
-    vmem = pl.BlockSpec(memory_space=pltpu.VMEM)
+    def sent(step, carry):
+        for slot in order:
+            hop(slot, step, True).wait_send()
+        return carry
+
+    lax.fori_loop(0, total - 1, sent, 0)
+
+
+def final(
+    total, d_project, full_in, turned, down, hidden, d_hidden, tok, gain_one, valid, sums_two, d_group
+):
+    rows, width = tok.shape
+    count, wide = d_project.shape
+    block = width // GROUP // total
+    vmem, hbm = pl.BlockSpec(memory_space=pltpu.VMEM), pl.BlockSpec(memory_space=ANY)
     dma = pltpu.SemaphoreType.DMA
+    group_width = d_group.shape[0] * d_group.shape[2]
+    shapes = (
+        ((block, wide * GROUP), F32),
+        ((rows, width), BF16),
+        ((rows, width), BF16),
+        ((8, 128), F32),
+        ((8, 128), F32),
+    )
     return pl.pallas_call(
-        functools.partial(reduce_in_kernel, total),
-        out_shape=[
-            jax.ShapeDtypeStruct((rows, width * GROUP), F32),
-            jax.ShapeDtypeStruct((count, tokens, features), F32),
-            jax.ShapeDtypeStruct((up.shape[1], up.shape[2] * GROUP), F32),
-        ],
-        in_specs=[pl.BlockSpec(memory_space=ANY)] * 2 + [vmem],
-        out_specs=[vmem] * 3,
+        functools.partial(final_kernel, total),
+        out_shape=[jax.ShapeDtypeStruct(s, d) for s, d in shapes],
+        in_specs=[hbm] * 4 + [vmem] * 7,
+        out_specs=[vmem] * 5,
         scratch_shapes=[
-            pltpu.VMEM((3,) + up.shape[1:], BF16),
-            pltpu.VMEM((4, total, rows, width), BF16),
-            pltpu.VMEM((4, total - 1, rows, width), BF16),
-            pltpu.VMEM((3, rows, width), BF16),
-            pltpu.VMEM((3, rows, width), BF16),
-            pltpu.VMEM((count, 2, tokens, features), BF16),
-            pltpu.VMEM((count, 2, tokens, features), BF16),
-            pltpu.VMEM((count, tokens, features), BF16),
-            pltpu.VMEM((count, tokens, features), BF16),
-            dma((4, total)), dma((4, total - 1)), dma((4, total - 1)),
-            dma((3,)), dma((3,)),
-            dma((count, 3)), dma((count, 3)), dma((count, 2)), dma((3,)), dma((3,)),
+            pltpu.VMEM((count, wide), BF16),
+            pltpu.VMEM(turned.shape, BF16),
+            pltpu.VMEM((4, block, wide), BF16),
+            pltpu.VMEM((4, block, wide), BF16),
+            pltpu.VMEM((4, total - 1, block, wide), BF16),
+            pltpu.VMEM((2, 256, wide), BF16),
+            pltpu.VMEM((count, width), BF16),
+            pltpu.VMEM((2, rows, width), BF16),
+            pltpu.VMEM((2, 2, rows, width), BF16),
+            pltpu.VMEM((2, rows, width), BF16),
+            pltpu.VMEM((2, rows, width), BF16),
+            pltpu.VMEM((3, block, wide), BF16),
+            pltpu.VMEM((3, block, wide), BF16),
+            pltpu.VMEM((8, width), F32),
+            pltpu.VMEM((8, group_width), F32),
+            pltpu.VMEM((3, 8, width // GROUP), F32),
+            pltpu.VMEM((8, width // GROUP), F32),
+            pltpu.VMEM((total - 1, 8, 128), F32),
+            pltpu.VMEM((total - 1, 8, 128), F32),
+            dma((2,)), dma((2,)), dma((4, total - 1)), dma((4, total - 1)), dma((3,)), dma((3,)),
+            dma((2, 3)), dma((2, 3)), dma((2,)), dma((3,)), dma((3,)), dma((2, total - 1)), dma((2, total - 1)),
         ],
         compiler_params=pltpu.CompilerParams(
-            collective_id=4, has_side_effects=True, vmem_limit_bytes=60 * MIB
+            collective_id=3, has_side_effects=True, vmem_limit_bytes=63 * MIB
         ),
-        name="reduce_in",
-    )(g_in, part, up)
-
-
-def reduce_vectors_kernel(total, vec, out, landed, mid, gathered, sends, recvs, far_send, far_recv):
-    at = Place(total)
-    me, inner = at.group, at.inner
-    others = [(me, lax.rem(inner + n, total)) for n in range(1, total)]
-    greet([at.peer(r) for r in (1, 2, 3)] + others)
-
-    def near(relation):
-        return remote(
-            vec.at[flip(me, relation)], landed.at[relation - 1],
-            sends.at[relation - 1], recvs.at[relation - 1], at.peer(relation),
-        )
-
-    for relation in (1, 2, 3):
-        near(relation).start()
-    for relation in (1, 2, 3):
-        near(relation).wait_recv()
-    mid[...] = vec[me] + landed[0] + landed[1] + landed[2]
-
-    def far(n):
-        target = lax.rem(inner + n, total)
-        return remote(mid.at[target], gathered.at[n - 1], far_send.at[n - 1], far_recv.at[n - 1], (me, target))
-
-    for n in range(1, total):
-        far(n).start()
-    for n in range(1, total):
-        far(n).wait_recv()
-    out[...] = mid[inner] + jnp.sum(gathered[...], axis=0)
-    for n in range(1, total):
-        far(n).wait_send()
-    for relation in (1, 2, 3):
-        near(relation).wait_send()
-
-
-def reduce_vectors(total, vec):
-    block = vec.shape[2:]
-    vmem = pl.BlockSpec(memory_space=pltpu.VMEM)
-    dma = pltpu.SemaphoreType.DMA
-    return pl.pallas_call(
-        functools.partial(reduce_vectors_kernel, total),
-        out_shape=jax.ShapeDtypeStruct(block, F32),
-        in_specs=[vmem],
-        out_specs=vmem,
-        scratch_shapes=[
-            pltpu.VMEM((3, total) + block, F32),
-            pltpu.VMEM((total,) + block, F32),
-            pltpu.VMEM((total - 1,) + block, F32),
-            dma((3,)), dma((3,)), dma((total - 1,)), dma((total - 1,)),
-        ],
-        compiler_params=pltpu.CompilerParams(collective_id=5, has_side_effects=True),
-        name="reduce_vectors",
-    )(vec)
+        name="final_sums",
+    )(d_project, full_in, turned, down, hidden, d_hidden, tok, gain_one, valid, sums_two, d_group)
 
 
 def layout(seq_lens, seq_owner, seq_offset, device_id, buffer_len):
@@ -1174,7 +1551,7 @@
     powers = jnp.exp(rates[:, None, None] * jnp.maximum(distance, 0).astype(F32)[None])
     powers = jnp.where(distance[None] >= 0, powers, 0.0)
     (
-        full_up, full_out, full_down, normed, query, keys, values, gate, mixed, gated, hidden, two,
+        full_up, full_out, full_down, turned, query, keys, values, gate, mixed, gated, hidden, two,
     ) = forward(
         total, own_up, w_out, w_down, full_in, tok, gain_one, bias_one, gain_group, tables, powers,
         ident[:, :, None], ident[:, None, :], tokens, gain_two, bias_two,
@@ -1194,83 +1571,16 @@
     slope = cdf + upper * jnp.exp(-0.5 * upper * upper) * (2.0 * jnp.pi) ** -0.5
     d_upper = (dot_back(seed, full_down) * slope).astype(BF16)
     d_two = dot_back(d_upper, full_up).astype(BF16).reshape(GROUP, rows, width)
-    d_hidden, d_branch, sums_two = exchange_rows(
-        total, True, d_two, own_seed, hidden, gain_two, bias_two
-    )
-    d_branch = d_branch.reshape(count, width)
-    def summed_over(value, dim):
-        return lax.psum_scatter(value, "fsdp", scatter_dimension=dim, tiled=True)
-
-    grad_down = summed_over(dot_rows(active, seed).astype(BF16), 0).astype(F32)
-    g_up = summed_over(dot_rows(two, d_upper).astype(BF16).reshape(GROUP, total * small, -1), 1)
-    grad_out = summed_over(dot_rows(gated, d_branch).astype(BF16), 0).astype(F32)
-
-    split = (heads, GROUP, rows)
-    query, keys, values = (v.reshape(split + v.shape[2:]) for v in (query, keys, values))
-    gate, mixed = gate.reshape(split + (VH,)), mixed.reshape(split + (VH,))
-    gains = gain_group[:, None]
-    linked = (ident[:, :, None] == ident[:, None, :]) & (ident[:, :, None] >= 0)
-    decay = jnp.where(linked[None], powers[:, None], 0.0)
-    masked = (jnp.einsum("hbtd,hbsd->hbts", query, keys, preferred_element_type=F32) * decay).astype(BF16)
-    d_gated = jnp.stack(
-        [dot_back(d_branch, full_out[h * VH : (h + 1) * VH]) for h in range(heads)]
-    ).reshape(split + (VH,))
-    group_normal, group_scale = norm_parts(mixed, GROUP_EPSILON)
-    sigmoid = jax.nn.sigmoid(gate)
-    silu = gate * sigmoid
-    d_silu = d_gated * (group_normal * gains)
-    d_gate = d_silu * (sigmoid + silu * (1.0 - sigmoid))
-    d_scaled = d_gated * silu
-    d_group = jnp.sum(d_scaled * group_normal, axis=(1, 2))
-    d_normal = d_scaled * gains
-    d_mixed = group_scale * (
-        d_normal - mean(d_normal) - group_normal * mean(d_normal * group_normal)
-    )
-    d_mixed = d_mixed.astype(BF16)
-    d_values = jnp.einsum("hbts,hbtv->hbsv", masked, d_mixed, preferred_element_type=F32)
-    d_masked = jnp.einsum("hbtv,hbsv->hbts", d_mixed, values, preferred_element_type=F32)
-    d_raw = (d_masked * decay).astype(BF16)
-    d_query = jnp.einsum("hbts,hbsd->hbtd", d_raw, keys, preferred_element_type=F32)
-    d_keys = jnp.einsum("hbts,hbtd->hbsd", d_raw, query, preferred_element_type=F32)
-    cosine, sine, growth, shrink = (t.reshape(GROUP, rows, -1) for t in tables)
-
-    def back(value, scale):
-        half = QKH // 2
-        first, second = value[..., :half], value[..., half:]
-        return jnp.concatenate(
-            [(first * cosine + second * sine) * scale, (second * cosine - first * sine) * scale], axis=-1
-        )
-
-    d_query = back(d_query * QKH ** (-0.5), growth).astype(BF16)
-    d_keys = back(d_keys, shrink).astype(BF16)
-    parts = [
-        value[h].reshape(count, -1).astype(BF16)
-        for value in (d_query, d_keys, d_values, d_gate)
-        for h in range(heads)
-    ]
-    d_project = jnp.concatenate(parts, axis=1)
-    d_normed = dot_back(d_project, full_in).astype(BF16).reshape(GROUP, rows, width)
-    g_in = dot_rows(normed, d_project).astype(BF16).reshape(GROUP, total, small, -1)
-    grad_in, own_rows, grad_up = reduce_in(total, g_in, jnp.stack([d_normed, down]), g_up)
-    output = ((hidden + own_rows[1]) * own_valid).astype(BF16)
-    e_one = own_rows[0]
-    normal_one, scale_one = norm_parts(tokens.astype(F32), EPSILON)
-    with_gain = e_one * gain_one
-    d_tokens = d_hidden + scale_one * (
-        with_gain - mean(with_gain) - normal_one * mean(with_gain * normal_one)
-    )
-    d_tokens = d_tokens.astype(BF16)
-
-    sums = jnp.stack(
-        [jnp.sum(e_one * normal_one, axis=0), jnp.sum(e_one, axis=0), sums_two[0], sums_two[1]]
-    )
-    sums = sums.reshape(4, GROUP, total, small).transpose(1, 2, 0, 3).reshape(GROUP, total, 4 * small)
-    mine = (jnp.arange(GROUP) == me).astype(F32)[:, None, None]
-    sums = jnp.concatenate([sums, mine * d_group.reshape(1, total, large)], axis=2)
-    sums = jnp.pad(sums, ((0, 0), (0, 0), (0, 1024 - sums.shape[2]))).reshape(GROUP, total, 8, 128)
-    summed = reduce_vectors(total, sums).reshape(1024)
-    grads = [summed[n * small : (n + 1) * small] for n in range(4)]
-    grad_group = summed[4 * small : 4 * small + large]
+    g_down = dot_rows(active, seed).astype(BF16)
+    grad_down, grad_up, grad_out, d_hidden, _, sums_two, d_group, d_project = backward(
+        total, g_down, two, d_upper, d_two, own_seed, hidden, gain_two, gated, full_out, query, keys, values,
+        gate, mixed, tables, powers, ident[:, :, None], ident[:, None, :], gain_group,
+    )
+    grad_in, output, d_tokens, vec_one, vec_two = final(
+        total, d_project, full_in, turned, down, hidden, d_hidden, tokens, gain_one, own_valid, sums_two, d_group
+    )
+    grads = lax.dynamic_slice(vec_one, (0, lax.rem(inner * small, 128)), (4, small))
+    grad_group = lax.dynamic_slice(vec_two, (0, lax.rem(inner * large, 128)), (1, large))[0]
     return (
         output,
         d_tokens,

time: 761 us -> 644 us (0.85)
  matrix products: 110 us -> 32.6 us
  Pallas kernels: 503 us -> 565 us
  other arithmetic: 58.8 us -> 10.3 us
  local copies, waits for them, and re-layouts: 59.7 us -> 24.5 us
  between operations: 14.8 us -> 1.13 us
    pallas_call x3 -> x2, Pallas kernels: 219 us -> 281 us  [the longest x1 150 us: final(): pl.pallas_call(functools.partial(final_kernel, total), out_shape=[jax.Sha...]
    dot_general x4 -> x1, matrix products: 41.2 us -> 6.27 us  [dot_rows(): lax.dot_general(left, right, (((0,), (0,)), ((), ())), preferred_element_...]
    dot_general x5 -> x2, matrix products: 40.3 us -> 11.9 us  [dot_back(): lax.dot_general(left, right, (((1,), (1,)), ((), ())), preferred_element_...]
    another operation x3 -> x0, other arithmetic: 19.9 us -> none
    unnamed x70 -> x26, local copies, waits for them, and re-layouts: 28.7 us -> 9.32 us
    reduce_sum x7 -> x0, other arithmetic: 16.5 us -> none  [the longest x1 6.03 us: local(): d_group = jnp.sum(d_scaled * group_normal, axis=(1, 2))]
    slice x10 -> x0, local copies, waits for them, and re-layouts: 16.1 us -> none  [the longest x6 12.9 us: local(): value[h].reshape(count, -1).astype(BF16)]
    convert_element_type x4 -> x0, other arithmetic: 9.42 us -> none  [the longest x1 5.09 us: local(): d_tokens = d_tokens.astype(BF16)]
  transfers between devices with their start and end apart: 3 -> 0, of which waited for: 0 -> 0; matrix products, arithmetic and copies ran while one was open for 23% -> 0% of each run, Pallas kernels for 29% -> 0%
where the time goes in v3:
time: 644 us; the launch traced here: 633 us
  Pallas kernels  565 us (88%)
  matrix products  32.6 us (5%)
  local copies, waits for them, and re-layouts  24.5 us (4%)
  other arithmetic  10.3 us (2%)
    pallas_call x1, Pallas kernels, final(): pl.pallas_call(functools.partial(final_kernel, total), out_shape=[jax.Sha...  150 us
    pallas_call x1, Pallas kernels, forward(): pl.pallas_call(functools.partial(forward_kernel, total), out_shape=[jax.S...  144 us
    pallas_call x1, Pallas kernels, gather_all(): pl.pallas_call(functools.partial(gather_kernel, total), out_shape=[jax.Sh...  140 us
    pallas_call x1, Pallas kernels, backward(): pl.pallas_call(functools.partial(backward_kernel, total), out_shape=[jax....  131 us
    dot_general x2, matrix products, dot(): return jnp.dot(left, right, preferred_element_type=F32)  14.4 us

profile of v3, /device:TPU:1, one launch (start us, length us, event | category | flops | bytes accessed | tf_op | source)
XLA Modules:
  0.0 633.3 jit_solution(1987446208962543564)
XLA Ops:
  1.3 0.7 compare_and_fusion
  2.7 0.7 iota_compare_fusion
  3.5 0.8 select_reduce_fusion
  4.4 2.3 broadcast_power_fusion
  6.6 3.4 concatenate.3
  10.7 139.7 %gather_weights.1 = (bf16[4,8,64,3072]{3,2,1,0:T(8,128)(2,1)}, bf16[4,64,1024]{2,1,0:T(8,128)(2,1)}, bf16[4,256,2048]{2,1,0:T(8,128)(2,1)}, bf16[4,256,2048]{2,1,0:T(8,128)(2,1)}, f32[8,4,8,128]{3,2,1,0:T(8,128)}) custom-call(bf16[64,12288]{1,0:T(8,128)(2,1)} %w_in.1, bf16[64,4096]{1,0:T(8,128)(2,1)} %w_up.1, bf16[256,2048]{1,0:T(8,128)(2,1)} %tok.3, ...), custom_call_target="tpu_custom_call" | custom-call | tf_op jit(solution)/shard_map/gather_weights/pallas_call | solution.py:247
  150.3 0.9 reshape.279
  152.0 0.7 reshape.283.gain_two
  153.4 0.7 reshape.284.bias_two
  154.1 0.7 reshape.281.bias_one
  154.8 3.0 multiply_sine_fusion
  157.8 1.0 copy.42.ident_col
  159.5 1.0 exponential_select_fusion.powers
  160.5 144.1 %forward_retention.1 = (bf16[4,8,64,1024]{3,2,1,0:T(8,128)(2,1)}, bf16[8,128,2048]{2,1,0:T(8,128)(2,1)}, bf16[8,128,2048]{2,1,0:T(8,128)(2,1)}, bf16[2048,1024]{...) custom-call(bf16[4,64,1024]{2,1,0:T(8,128)(2,1)} %get-tuple-element., ...), custom_call_target="tpu_custom_call" | custom-call | tf_op jit(solution)/shard_map/forward_retention/pallas_call | solution.py:657
  304.6 8.0 %multiply_convert_fusion.1 = (bf16[1024,1024]{1,0:T(8,128)(2,1)S(1)}, f32[1024,1024]{1,0:T(8,128)S(1)}) fusion(bf16[1024,2048]{1,0:T(8,128)(2,1)} %bitcast.57, bf16[2048,1024]{1,0:T(8,128)(2,1)} %bitcast.68), kind=kOutput, calls=%fused_computation.8 | convolution fusion | flops 4300210176 | bytes 14680064 | tf_op jit(solution)/shard_map/dot_general | solution.py:94
  312.6 6.4 %convolution_convert_fusion = bf16[1024,2048]{1,0:T(8,128)(2,1)} fusion(bf16[1024,1024]{1,0:T(8,128)(2,1)S(1)} %get-tuple-element.89, bf16[1024,2048]{1,0:T(8,128)(2,1)S(1)} %bitcast.70), kind=kOutput, calls=%fused_computation.10 | convolution fusion | flops 4297064448 | bytes 10485760 | tf_op jit(solution)/shard_map/dot_general | solution.py:94
  319.0 0.7 multiply_convert_fusion
  319.8 5.8 fusion.5.d_upper
  325.6 6.1 convolution_convert_fusion.1
  331.8 6.3 convolution_convert_fusion.2.g_down
  338.1 1.2 multiply_convert_fusion.2.seed
  339.3 130.7 %backward_retention.1 = (f32[128,2048]{1,0:T(8,128)}, f32[64,4096]{1,0:T(8,128)}, f32[128,2048]{1,0:T(8,128)}, f32[256,2048]{1,0:T(8,128)}, bf16[4,256,2048]{2,1...) custom-call(bf16[1024,2048]{1,0:T(8,128)(2,1)} %convolution_convert_fusion.2.g_down, ...), custom_call_target="tpu_custom_call" | custom-call | tf_op jit(solution)/shard_map/backward_retention/pallas_call | solution.py:1075
  470.0 0.8 copy.44.valid
  470.8 150.3 %final_sums.1 = (f32[64,12288]{1,0:T(8,128)}, bf16[256,2048]{1,0:T(8,128)(2,1)}, bf16[256,2048]{1,0:T(8,128)(2,1)}, f32[8,128]{1,0:T(8,128)}, f32[8,128]{1,0:T(8,128)}) custom-call(bf16[1024,3072]{1,0:T(8,128)(2,1)} %get-tuple-element.56.h_project, bf16[2048,3072]{1,0:T(8,128)(2,1)} %bitcast.54, bf16[2048,1024]{1,0:T(8,128)(2,1)} %get-tuple-element.57.h_turned, ...), custom_call_target="tpu_custom_call" | custom-call | tf_op jit(solution)/shard_map/final_sums/pallas_call | solution.py:1417
  621.1 0.9 constant_dynamic-slice_fusion
  622.6 1.2 slice_bitcast_fusion.2
  623.8 2.3 copy.63
  626.1 2.4 copy.64
  628.5 1.7 copy.65
  630.1 1.0 copy.66
  631.1 1.0 copy.67
  632.1 1.0 copy.68
  (44 shorter events, 4.7 us)
Async XLA Ops:
  304.6 8.0 %copy-start.8 = (bf16[8,128,2048]{2,1,0:T(8,128)(2,1)S(1)}, bf16[8,128,2048]{2,1,0:T(8,128)(2,1)}, u32[]{:S(2)}) copy-start(bf16[8,128,2048]{2,1,0:T(8,128)(2,1)} %get-tuple-element.47) | copy-start | bytes 12582916
  312.6 6.5 %copy-start.1 = (bf16[4,256,2048]{2,1,0:T(8,128)(2,1)S(1)}, bf16[4,256,2048]{2,1,0:T(8,128)(2,1)}, u32[]{:S(2)}) copy-start(bf16[4,256,2048]{2,1,0:T(8,128)(2,1)} %get-tuple-element.46) | copy-start | bytes 12582916
  319.8 5.8 copy-start.7
  325.6 6.1 copy-start.3
  331.8 6.3 copy-start
  621.1 7.3 %copy-start.2 = (f32[64,12288]{1,0:T(8,128)S(1)}, f32[64,12288]{1,0:T(8,128)}, u32[]{:S(2)}) copy-start(f32[64,12288]{1,0:T(8,128)} %get-tuple-element.110) | copy-start | bytes 9437188
  626.1 4.1 copy-start.6
  628.5 2.6 copy-start.5
  628.5 3.6 copy-start.4

commit v4 on v3

--- a/solution.py
+++ b/solution.py
@@ -2,6 +2,7 @@
 
 import jax
 import jax.numpy as jnp
+import numpy as np
 from jax import lax
 from jax.experimental import pallas as pl
 from jax.experimental.pallas import tpu as pltpu
@@ -78,16 +79,16 @@
     )
 
 
-def column_pieces(width_in):
-    key = HEADS * QKH
-    value = HEADS * VH
-    qk, vv = key // GROUP, value // GROUP
-    return (
-        (0, qk, 0, qk),
-        (key, qk, qk, qk),
-        (2 * key, vv, 2 * qk, vv),
-        (2 * key + value, vv, 2 * qk + vv, vv),
-    )
+def column_pieces():
+    heads = HEADS // GROUP
+    table = []
+    base, off = 0, 0
+    for size in (QKH, QKH, VH, VH):
+        for h in range(heads):
+            table.append((base + h * size, heads * size, h, off, size))
+        base += HEADS * size
+        off += size
+    return table
 
 
 def dot(left, right):
@@ -100,165 +101,6 @@
 
 def dot_back(left, right):
     return lax.dot_general(left, right, (((1,), (1,)), ((), ())), preferred_element_type=F32)
-
-
-def gather_kernel(
-    total,
-    w_in,
-    w_up,
-    tok,
-    cot,
-    vec,
-    full_in,
-    own_up,
-    full_tok,
-    full_cot,
-    full_vec,
-    a2a_send,
-    a2a_recv,
-    own_sem,
-    ring_send,
-    ring_recv,
-):
-    at = Place(total)
-    me, inner = at.group, at.inner
-    peers = [at.peer(r) for r in (1, 2, 3)]
-    greet(peers + [at.neighbour(0), at.neighbour(1)])
-    up_width = own_up.shape[-1]
-    pieces = column_pieces(w_in.shape[1])
-
-    def exchange(relation, slot):
-        other = flip(me, relation)
-        if slot < 4:
-            base, stride, off, width = pieces[slot]
-            start = pl.multiple_of(base + other * stride, 128)
-            src = w_in.at[:, pl.ds(start, width)]
-            dst = full_in.at[me, inner, :, pl.ds(off, width)]
-        elif slot == 4:
-            src = w_up.at[:, pl.ds(pl.multiple_of(other * up_width, 128), up_width)]
-            dst = own_up.at[me]
-        elif slot == 5:
-            src, dst = vec, full_vec.at[inner, me]
-        elif slot == 6:
-            src, dst = tok, full_tok.at[me]
-        else:
-            src, dst = cot, full_cot.at[me]
-        if relation == 0:
-            return pltpu.make_async_copy(src, dst, own_sem.at[slot])
-        return remote(
-            src,
-            dst,
-            a2a_send.at[relation - 1, slot],
-            a2a_recv.at[relation - 1, slot],
-            at.peer(relation),
-        )
-
-    for relation in (1, 0, 2, 3):
-        for slot in (0, 1, 2, 3):
-            exchange(relation, slot).start()
-    for relation in (1, 0, 2, 3):
-        for slot in (5, 4):
-            exchange(relation, slot).start()
-
-    ways = ((0, 2), (1, 3))
-
-    def block(item, way, which):
-        if item < 2:
-            return full_in.at[flip(me, ways[way][item]), which]
-        return full_vec.at[which]
-
-    def hop(item, way, step):
-        which = at.behind(way, step)
-        place = block(item, way, which)
-        return remote(
-            place, place, ring_send.at[item, way, step], ring_recv.at[item, way, step], at.neighbour(way)
-        )
-
-    def active(item, way):
-        return not (item == 2 and way == 1)
-
-    def first(item, way):
-        relations, slots = ((ways[way][item],), (0, 1, 2, 3)) if item < 2 else (range(4), (5,))
-        for relation in relations:
-            for slot in slots:
-                copy = exchange(relation, slot)
-                if relation == 0:
-                    copy.wait()
-                else:
-                    copy.wait_recv()
-        hop(item, way, 0).start()
-
-    groups = ((0, 1, 2),)
-    for number, group in enumerate(groups):
-        for item in group:
-            for way in (0, 1):
-                if active(item, way):
-                    first(item, way)
-        if number == 0:
-            for relation in (1, 0, 2, 3):
-                for slot in (6, 7):
-                    exchange(relation, slot).start()
-
-        def onward(step, carry, group=group):
-            for item in group:
-                for way in (0, 1):
-                    if active(item, way):
-                        hop(item, way, step - 1).wait_recv()
-                        hop(item, way, step).start()
-            return carry
-
-        lax.fori_loop(1, total - 1, onward, 0)
-
-    for group in groups:
-        for item in group:
-            for way in (0, 1):
-                if active(item, way):
-                    hop(item, way, total - 2).wait_recv()
-
-    def sent(step, carry):
-        for group in groups:
-            for item in group:
-                for way in (0, 1):
-                    if active(item, way):
-                        hop(item, way, step).wait_send()
-        return carry
-
-    lax.fori_loop(0, total - 1, sent, 0)
-    for relation in (1, 2, 3):
-        for slot in range(8):
-            exchange(relation, slot).wait_send()
-            if slot in (4, 6, 7):
-                exchange(relation, slot).wait_recv()
-    exchange(0, 4).wait()
-    exchange(0, 6).wait()
-    exchange(0, 7).wait()
-
-
-def gather_all(total, w_in, w_up, tok, cot, vec):
-    width = w_in.shape[1] // GROUP
-    up_width = w_up.shape[1] // GROUP
-    shapes = (
-        ((GROUP, total, w_in.shape[0], width), BF16),
-        ((GROUP, w_up.shape[0], up_width), BF16),
-        ((GROUP,) + tok.shape, BF16),
-        ((GROUP,) + cot.shape, BF16),
-        ((total, GROUP) + vec.shape, F32),
-    )
-    return pl.pallas_call(
-        functools.partial(gather_kernel, total),
-        out_shape=[jax.ShapeDtypeStruct(s, d) for s, d in shapes],
-        in_specs=[pl.BlockSpec(memory_space=ANY)] * 5,
-        out_specs=[pl.BlockSpec(memory_space=ANY)] * 5,
-        scratch_shapes=[
-            pltpu.SemaphoreType.DMA((3, 8)),
-            pltpu.SemaphoreType.DMA((3, 8)),
-            pltpu.SemaphoreType.DMA((8,)),
-            pltpu.SemaphoreType.DMA((3, 2, total - 1)),
-            pltpu.SemaphoreType.DMA((3, 2, total - 1)),
-        ],
-        compiler_params=pltpu.CompilerParams(collective_id=0, has_side_effects=True),
-        name="gather_weights",
-    )(w_in, w_up, tok, cot, vec)
 
 
 def norm_parts(values, epsilon):
@@ -319,7 +161,7 @@
     lax.fori_loop(start, stop, body, 0)
 
 
-def weight_rings(at, own_up, w_out, w_down, full_up, full_out, full_down, sends, recvs):
+def weight_rings(at, w_out, w_down, full_up, full_out, full_down, sends, recvs):
     me = at.group
     half = w_out.shape[0] // 2
     side = w_out.shape[1] // 2
@@ -343,7 +185,7 @@
             slot = 8 + 2 * order + way
             ups.append(
                 Passing(
-                    at, way, own_up.at[flip(me, relation)],
+                    at, way, full_up.at[flip(me, relation), at.inner],
                     lambda which, relation=relation: full_up.at[flip(me, relation), which],
                     sends.at[slot], recvs.at[slot],
                 )
@@ -360,71 +202,220 @@
 
 
 def forward_kernel(
-    total, own_up, w_out, w_down, full_in, tok, gain_one, bias_one, gain_group, cosine, sine, growth, shrink,
-    powers, ident_col, ident_row, own_tok, gain_two, bias_two,
-    full_up, full_out, full_down, o_turned, o_query, o_keys, o_values, o_gate, o_mixed, o_gated, hidden, full_two,
-    win, part, x, query, keys, values, gate, mixed, gated, wo, core_in, out_x, in_x, low,
-    ring_send, ring_recv, own_sem, load_sem, win_sem, store_sem, row_send, row_recv, row_own,
+    total, w_in, w_up, w_out, w_down, tok, cot, pack, rates, seq_cols, seq_rows, curves,
+    full_in, full_up, full_out, full_down, full_seed, o_turned, o_query, o_keys, o_values, o_gate, o_mixed,
+    o_gated, hidden, full_two, own_seed, cosine, sine, growth, shrink, powers, ident_col, ident_row, gains,
+    gain_group,
+    win, part, x, query, keys, values, gate, mixed, gated, wo, core_in, out_x, in_x, low, full_vec,
+    ring_send, ring_recv, own_sem, load_sem, store_sem, row_send, row_recv, row_own,
+    swap_send, swap_recv, swap_own, vec_send, vec_recv,
 ):
     at = Place(total)
     me, inner = at.group, at.inner
     core, across = at.peer(1), at.peer(2)
-    greet([core, across, at.neighbour(0), at.neighbour(1)])
-    rows, width = own_tok.shape
+    others = [(me, lax.rem(inner + n, total)) for n in range(1, total)]
+    greet([core, across, at.peer(3)] + others)
+    rows, width = tok.shape
     count = GROUP * rows
     heads = HEADS // GROUP
+    r_in = w_in.shape[0]
+    up_width = full_up.shape[-1]
+    pieces = column_pieces()
+    step_rows = 32
+
+    def rows_in(group_index, which):
+        return pl.ds(pl.multiple_of((group_index * total + which) * r_in, r_in), r_in)
+
+    last = len(pieces)
+
+    def swap(relation, slot):
+        other = flip(me, relation)
+        if slot < last:
+            base, stride, h, off, size = pieces[slot]
+            src = w_in.at[:, pl.ds(pl.multiple_of(base + other * stride, 128), size)]
+            dst = win.at[h, rows_in(me, inner), pl.ds(off, size)]
+        elif slot == last:
+            src = w_up.at[:, pl.ds(pl.multiple_of(other * up_width, 128), up_width)]
+            dst = full_up.at[me, inner]
+        elif slot == last + 1:
+            src, dst = pack, full_vec.at[inner, me]
+        elif slot == last + 2:
+            src, dst = tok, part.at[me]
+        else:
+            src, dst = own_seed, full_seed.at[me]
+        if relation == 0:
+            return pltpu.make_async_copy(src, dst, swap_own.at[slot])
+        return remote(
+            src, dst, swap_send.at[relation - 1, slot], swap_recv.at[relation - 1, slot], at.peer(relation)
+        )
+
+    def arrived(relation, slot):
+        if relation == 0:
+            swap(0, slot).wait()
+        else:
+            swap(relation, slot).wait_recv()
+
+    for relation in (1, 0, 2, 3):
+        for slot in range(last):
+            swap(relation, slot).start()
+    for relation in range(4):
+        swap(relation, last + 1).start()
+    for slot in (last + 2, last):
+        for relation in (1, 0, 2, 3):
+            swap(relation, slot).start()
+
+    def in_ring(relation, way, slot):
+        def place(which):
+            return win.at[:, rows_in(flip(me, relation), which), :]
+
+        return Passing(at, way, place(inner), place, ring_send.at[slot], ring_recv.at[slot])
+
+    near = [in_ring(0, 0, 12), in_ring(1, 1, 13)]
+    far_in = [in_ring(2, 0, 14), in_ring(3, 1, 15)]
+    for relation in (0, 1):
+        for slot in range(last):
+            arrived(relation, slot)
+        near[relation].begin()
+
+    def layout_of(b, down):
+        shape = (rows, 1) if down else (1, rows)
+        source = seq_rows if down else seq_cols
+        lens, owner, offset = source[0], source[1], source[2]
+        positions = lax.broadcasted_iota(jnp.int32, shape, 0 if down else 1)
+        inside = (
+            (owner == b * total + inner)
+            & (lens > 0)
+            & (positions >= offset)
+            & (positions < offset + lens)
+        )
+        axis = 1 if down else 0
+        number = lax.broadcasted_iota(jnp.int32, lens.shape, axis).astype(F32) + 1.0
+        ident = jnp.sum(jnp.where(inside, number, 0.0), axis=axis, keepdims=True) - 1.0
+        starts = jnp.sum(jnp.where(inside, offset.astype(F32), 0.0), axis=axis, keepdims=True)
+        places = jnp.where(ident >= 0.0, positions.astype(F32) - starts, 0.0)
+        return ident, places
+
+    for b in range(GROUP):
+        ident_col[b] = layout_of(b, True)[0]
+        ident_row[b] = layout_of(b, False)[0]
+
+    def seed_rows(n, carry):
+        s = pl.ds(pl.multiple_of(n * step_rows, step_rows), step_rows)
+        valid = jnp.where(ident_col[me, s, :] >= 0.0, 1.0, 0.0)
+        own_seed[s, :] = (cot[s, :].astype(F32) * valid).astype(BF16)
+        return carry
+
+    lax.fori_loop(0, rows // step_rows, seed_rows, 0)
+
+    for relation in range(4):
+        arrived(relation, last + 1)
+
+    def spread(n):
+        target = lax.rem(inner + n, total)
+        return remote(
+            full_vec.at[inner], full_vec.at[inner], vec_send.at[n - 1], vec_recv.at[n - 1], (me, target)
+        )
+
+    for n in range(1, total):
+        spread(n).start()
+    for ring in near:
+        ring.onward(1)
+    for relation in (2, 3):
+        for slot in range(last):
+            arrived(relation, slot)
+        far_in[relation - 2].begin()
+    for relation in (1, 0, 2, 3):
+        swap(relation, last + 3).start()
+
+    def both_in(step, carry):
+        for ring in near:
+            ring.onward(step)
+        for ring in far_in:
+            ring.onward(step - 1)
+        return carry
+
+    def take_vectors():
+        for n in range(1, total):
+            spread(n).wait_recv()
+        quarter = width // GROUP
+        small = quarter // total
+        large = heads * VH // total
+        for d in range(GROUP):
+            tiles = {}
+            for f in range(total):
+                t = f * small // 128
+                value = full_vec[f, d]
+                tiles[t] = tiles[t] + value if t in tiles else value
+            for t, value in tiles.items():
+                gains[:, d * quarter + t * 128 : d * quarter + (t + 1) * 128] = value
+        tiles = {}
+        for f in range(total):
+            t = f * large // 128
+            value = full_vec[f, me, 4:5, :]
+            tiles[t] = tiles[t] + value if t in tiles else value
+        for t, value in tiles.items():
+            h, off = t * 128 // VH, t * 128 % VH
+            gain_group[h, :, off : off + 128] = value
+
+    def make_tables():
+        distance = lax.broadcasted_iota(jnp.int32, (rows, rows), 0) - lax.broadcasted_iota(
+            jnp.int32, (rows, rows), 1
+        )
+        away = jnp.maximum(distance, 0).astype(F32)
+        for h in range(heads):
+            powers[h] = jnp.where(distance >= 0, jnp.exp(rates[h] * away), 0.0)
+        for b in range(GROUP):
+            places = layout_of(b, True)[1]
+            angles = places * curves[0:1, :]
+            r = slice(b * rows, (b + 1) * rows)
+            cosine[r, :] = jnp.cos(angles)
+            sine[r, :] = jnp.sin(angles)
+            lift = places * (1.0 / 512.0) * curves[1:2, :]
+            growth[r, :] = jnp.exp(lift)
+            shrink[r, :] = jnp.exp(-lift)
+
+    def norm_buffer(relation):
+        b = flip(me, relation)
+        arrived(relation, last + 2)
+
+        def norm_rows(n, carry):
+            r = pl.multiple_of(n * step_rows, step_rows)
+            normal, _ = norm_parts(part[b, pl.ds(r, step_rows), :].astype(F32), EPSILON)
+            at_rows = pl.ds(pl.multiple_of(b * rows + r, step_rows), step_rows)
+            x[at_rows, :] = (normal * gains[0:1, :] + gains[1:2, :]).astype(BF16)
+            return carry
+
+        lax.fori_loop(0, rows // step_rows, norm_rows, 0)
+
+    beside = [
+        make_tables,
+        take_vectors,
+        lambda: (norm_buffer(0), norm_buffer(1)),
+        lambda: norm_buffer(2),
+        lambda: norm_buffer(3),
+    ]
+    cuts = [2 + (total - 3) * n // 5 for n in range(6)]
+    for n in range(5):
+        lax.fori_loop(cuts[n], cuts[n + 1], both_in, 0)
+        beside[n]()
+    for ring in far_in:
+        ring.onward(total - 2)
     outs, ups, downs = weight_rings(
-        at, own_up, w_out, w_down, full_up, full_out, full_down, ring_send, ring_recv
+        at, w_out, w_down, full_up, full_out, full_down, ring_send, ring_recv
     )
     for ring in outs:
         ring.begin()
     own_copies = [
         pltpu.make_async_copy(w_out, full_out.at[inner], own_sem.at[0]),
         pltpu.make_async_copy(w_down, full_down.at[inner], own_sem.at[1]),
-        pltpu.make_async_copy(own_up, full_up.at[:, inner], own_sem.at[2]),
     ]
-    for b in range(GROUP):
-        pltpu.make_async_copy(tok.at[b], part.at[b], load_sem.at[b]).start()
-
-    def win_copies(h):
-        qk, vv = heads * QKH, heads * VH
-        table = (
-            (h * QKH, 0, QKH),
-            (qk + h * QKH, QKH, QKH),
-            (2 * qk + h * VH, 2 * QKH, VH),
-            (2 * qk + vv + h * VH, 2 * QKH + VH, VH),
-        )
-        return [
-            pltpu.make_async_copy(
-                full_in.at[:, pl.ds(pl.multiple_of(start, 128), size)],
-                win.at[h, :, pl.ds(off, size)],
-                win_sem.at[h, n],
-            )
-            for n, (start, off, size) in enumerate(table)
-        ]
-
-    for h in range(heads):
-        for copy in win_copies(h):
-            copy.start()
     for copy in own_copies:
         copy.start()
-
-    step_rows = 32
-
-    def norm_buffer(b, carry):
-        pltpu.make_async_copy(tok.at[b], part.at[b], load_sem.at[b]).wait()
-
-        def norm_rows(n, carry):
-            r = pl.multiple_of(n * step_rows, step_rows)
-            normal, _ = norm_parts(part[b, pl.ds(r, step_rows), :].astype(F32), EPSILON)
-            at_rows = pl.ds(pl.multiple_of(b * rows + r, step_rows), step_rows)
-            x[at_rows, :] = (normal * gain_one[...] + bias_one[...]).astype(BF16)
-            return carry
-
-        lax.fori_loop(0, rows // step_rows, norm_rows, 0)
-        return carry
-
-    lax.fori_loop(0, GROUP, norm_buffer, 0)
+    for ring in near + far_in:
+        ring.finish()
+    store_win = pltpu.make_async_copy(win, full_in, load_sem.at[1])
+    store_win.start()
+
     tile = 512
     spots = 6
     plan = tick_plan(total, spots)
@@ -445,9 +436,6 @@
         return at_tile
 
     def head(h, carry):
-        for copy in win_copies(h):
-            copy.wait()
-
         def rotate_tiles(m, carry):
             def put_query(r, value):
                 turned = rotated(value, cosine[r, :], sine[r, :], growth[r, :])
@@ -483,7 +471,7 @@
         def buffer(b, carry):
             r = pl.ds(pl.multiple_of(b * rows, rows), rows)
             raw = dot_back(query[h, r, :], keys[h, r, :])
-            linked = (ident_col[b] == ident_row[b]) & (ident_col[b] >= 0)
+            linked = (ident_col[b] == ident_row[b]) & (ident_col[b] >= 0.0)
             masked = (raw * jnp.where(linked, powers[h], 0.0)).astype(BF16)
             value = dot(masked, values[h, r, :])
             mixed[h, r, :] = value
@@ -498,10 +486,12 @@
         return carry
 
     lax.fori_loop(0, heads, head, 0)
+    for relation in range(4):
+        arrived(relation, last)
+    for ring in ups + downs:
+        ring.begin()
     for ring in outs:
         ring.finish()
-    for ring in ups + downs:
-        ring.begin()
     stores = [
         pltpu.make_async_copy(src, dst, store_sem.at[1 + n])
         for n, (src, dst) in enumerate(
@@ -512,7 +502,7 @@
         copy.start()
     own_copies[0].wait()
     block = w_out.shape[0]
-    fetch = pltpu.make_async_copy(full_out, wo, load_sem.at[GROUP])
+    fetch = pltpu.make_async_copy(full_out, wo, load_sem.at[0])
     fetch.start()
     fetch.wait()
 
@@ -582,6 +572,8 @@
         win[0, i, j] = x[j, i].T
         return carry
 
+    store_win.wait()
+    wait_sent(near + far_in, total)
     lax.fori_loop(0, (width // 256) * (count // 256), turn, 0)
     store_turned = pltpu.make_async_copy(win.at[0, :, pl.ds(0, count)], o_turned, store_sem.at[0])
     store_turned.start()
@@ -592,12 +584,12 @@
 
         def finish_rows(n, carry, c=c):
             s = pl.ds(pl.multiple_of(c * size + n * step_rows, step_rows), step_rows)
-            value = own_tok[s, :].astype(F32) + (
+            value = tok[s, :].astype(F32) + (
                 part[me, s, :].astype(F32) + core_in[1, s, :].astype(F32) + in_x[s, :].astype(F32)
             )
             hidden[s, :] = value
             normal, _ = norm_parts(value, EPSILON)
-            low[s, :] = (normal * gain_two[...] + bias_two[...]).astype(BF16)
+            low[s, :] = (normal * gains[2:3, :] + gains[3:4, :]).astype(BF16)
             return carry
 
         lax.fori_loop(0, size // step_rows, finish_rows, 0)
@@ -622,21 +614,29 @@
         ring.finish()
     wait_sent(outs + rest, total)
     own_copies[1].wait()
-    own_copies[2].wait()
+    arrived(0, last + 3)
+    for relation in (1, 2, 3):
+        arrived(relation, last + 3)
+        for slot in range(last + 4):
+            swap(relation, slot).wait_send()
+    for n in range(1, total):
+        spread(n).wait_send()
     store_turned.wait()
     for c in stores:
         c.wait()
 
 
-def forward(
-    total, own_up, w_out, w_down, full_in, tok, gain_one, bias_one, gain_group, tables, powers, ident_col, ident_row,
-    own_tok, gain_two, bias_two,
-):
-    rows, width = own_tok.shape
+def forward(total, w_in, w_up, w_out, w_down, tok, cot, pack, rates, seq_cols, seq_rows):
+    rows, width = tok.shape
     count = GROUP * rows
     heads = HEADS // GROUP
+    head_width = 2 * (QKH + VH)
     vmem, hbm = pl.BlockSpec(memory_space=pltpu.VMEM), pl.BlockSpec(memory_space=ANY)
     dma = pltpu.SemaphoreType.DMA
+    pair = np.arange(QKH // 2) / (QKH // 2)
+    curves = np.zeros((8, QKH // 2), np.float32)
+    curves[0] = 10000.0**-pair
+    curves[1] = np.log((pair + 0.4) / 1.4)
     kept = (
         ((heads, count, QKH), BF16),
         ((heads, count, QKH), BF16),
@@ -645,22 +645,35 @@
         ((heads, count, VH), F32),
         ((count, heads * VH), BF16),
     )
-    shapes = (
-        ((GROUP, total) + own_up.shape[1:], BF16),
+    in_hbm = (
+        ((heads, width, head_width), BF16),
+        ((GROUP, total, w_up.shape[0], w_up.shape[1] // GROUP), BF16),
         ((total,) + w_out.shape, BF16),
         ((total,) + w_down.shape, BF16),
+        ((GROUP, rows, width), BF16),
         ((width, count), BF16),
         *kept,
-        ((rows, width), F32),
-        ((GROUP, rows, width), BF16),
     )
+    in_vmem = (
+        ((rows, width), BF16),
+        ((count, QKH // 2), F32),
+        ((count, QKH // 2), F32),
+        ((count, QKH // 2), F32),
+        ((count, QKH // 2), F32),
+        ((heads, rows, rows), F32),
+        ((GROUP, rows, 1), F32),
+        ((GROUP, 1, rows), F32),
+        ((8, width), F32),
+        ((heads, 1, VH), F32),
+    )
+    shapes = (*in_hbm, ((rows, width), F32), ((GROUP, rows, width), BF16), *in_vmem)
     return pl.pallas_call(
         functools.partial(forward_kernel, total),
         out_shape=[jax.ShapeDtypeStruct(s, d) for s, d in shapes],
-        in_specs=[hbm] * 5 + [vmem] * 13,
-        out_specs=[hbm] * 10 + [vmem, hbm],
+        in_specs=[hbm] * 4 + [vmem] * 7,
+        out_specs=[hbm] * len(in_hbm) + [vmem, hbm] + [vmem] * len(in_vmem),
         scratch_shapes=[
-            pltpu.VMEM((heads, width, 2 * QKH + 2 * VH), BF16),
+            pltpu.VMEM((heads, width, head_width), BF16),
             pltpu.VMEM((GROUP, rows, width), BF16),
             pltpu.VMEM((count, width), BF16),
             *[pltpu.VMEM(s, d) for s, d in kept],
@@ -669,17 +682,16 @@
             pltpu.VMEM((rows, width), BF16),
             pltpu.VMEM((rows, width), BF16),
             pltpu.VMEM((rows, width), BF16),
-            dma((12, total - 1)), dma((12, total - 1)), dma((3,)), dma((GROUP + 1,)), dma((heads, 4)),
+            pltpu.VMEM((total, GROUP, 8, 128), F32),
+            dma((16, total - 1)), dma((16, total - 1)), dma((2,)), dma((2,)),
             dma((7,)), dma((6, 4)), dma((6, 4)), dma((4,)),
+            dma((3, 12)), dma((3, 12)), dma((12,)), dma((total - 1,)), dma((total - 1,)),
         ],
         compiler_params=pltpu.CompilerParams(
             collective_id=1, has_side_effects=True, vmem_limit_bytes=63 * MIB
         ),
         name="forward_retention",
-    )(
-        own_up, w_out, w_down, full_in, tok, gain_one, bias_one, gain_group, *tables, powers, ident_col,
-        ident_row, own_tok, gain_two, bias_two,
-    )
+    )(w_in, w_up, w_out, w_down, tok, cot, pack, rates, seq_cols, seq_rows, jnp.asarray(curves))
 
 
 class Adding:
@@ -718,7 +730,7 @@
 
 
 def backward_kernel(
-    total, g_down, two, d_upper, part, seed, hidden, gain_two, h_gated, h_out, h_query, h_keys, h_values, h_gate,
+    total, g_down, two, d_upper, part, seed, hidden, gains_all, h_gated, h_out, h_query, h_keys, h_values, h_gate,
     h_mixed, cosine, sine, growth, shrink, powers, ident_col, ident_row, gain_group,
     o_down, o_up, o_out, d_hidden, full_branch, sums, o_group, o_project,
     g_up, g_out, arrived, wide_buf, narrow_buf, wo, own_part, core_in, out_x, in_x, low,
@@ -838,7 +850,7 @@
             s = pl.ds(pl.multiple_of(c * size + n * step_rows, step_rows), step_rows)
             e = own_part[1, s, :].astype(F32) + core_in[1, s, :].astype(F32) + in_x[s, :].astype(F32)
             normal, scale = norm_parts(hidden[s, :], EPSILON)
-            with_gain = e * gain_two[...]
+            with_gain = e * gains_all[2:3, :]
             sums[0:1, :] += jnp.sum(e * normal, axis=0, keepdims=True)
             sums[1:2, :] += jnp.sum(e, axis=0, keepdims=True)
             value = seed[s, :].astype(F32) + scale * (
@@ -935,25 +947,14 @@
             sent_across(relation).start()
 
     units = heads * GROUP
-    qk, vv = heads * QKH, heads * VH
 
     def unit_stores(unit, slot):
         h, b = unit // GROUP, lax.rem(unit, GROUP)
         r = pl.ds(pl.multiple_of(b * rows, rows), rows)
-        table = (
-            (h * QKH, 0, QKH),
-            (qk + h * QKH, QKH, QKH),
-            (2 * qk + h * VH, 2 * QKH, VH),
-            (2 * qk + vv + h * VH, 2 * QKH + VH, VH),
-        )
-        return [
-            pltpu.make_async_copy(
-                staged.at[slot, :, pl.ds(off, size)],
-                o_project.at[r, pl.ds(pl.multiple_of(start, 128), size)],
-                out_sem.at[slot, n],
-            )
-            for n, (start, off, size) in enumerate(table)
-        ]
+        start = pl.multiple_of(h * staged.shape[2], 128)
+        return pltpu.make_async_copy(
+            staged.at[slot], o_project.at[r, pl.ds(start, staged.shape[2])], out_sem.at[slot]
+        )
 
     def unrotated(value, r, scale):
         mid = QKH // 2
@@ -973,8 +974,7 @@
 
         @pl.when(unit >= 2)
         def _():
-            for done in unit_stores(unit - 2, slot):
-                done.wait()
+            unit_stores(unit - 2, slot).wait()
 
         gains = gain_group[h]
 
@@ -1001,7 +1001,7 @@
             return carry
 
         lax.fori_loop(0, rows // step_rows, some_rows, 0)
-        linked = (ident_col[b] == ident_row[b]) & (ident_col[b] >= 0)
+        linked = (ident_col[b] == ident_row[b]) & (ident_col[b] >= 0.0)
         decay = jnp.where(linked, powers[h], 0.0)
         masked = (dot_back(query[slot], keys[slot]) * decay).astype(BF16)
         staged[slot, :, 2 * QKH : 2 * QKH + VH] = dot_rows(masked, d_mixed[...]).astype(BF16)
@@ -1010,8 +1010,7 @@
         staged[slot, :, :QKH] = unrotated(d_query, r, growth[r, :]).astype(BF16)
         d_keys = dot_rows(d_raw, query[slot])
         staged[slot, :, QKH : 2 * QKH] = unrotated(d_keys, r, shrink[r, :]).astype(BF16)
-        for done in unit_stores(unit, slot):
-            done.start()
+        unit_stores(unit, slot).start()
 
         @pl.when(unit + 2 < units)
         def _():
@@ -1030,8 +1029,7 @@
         ].astype(F32)
         sent_across(relation).wait_send()
     for slot in (0, 1):
-        for done in unit_stores(jnp.int32(units - 2 + slot), slot):
-            done.wait()
+        unit_stores(jnp.int32(units - 2 + slot), slot).wait()
     for n, ring in enumerate(outs):
         c, way = n // 2, n % 2
         o_out[pl.ds(way * half, half), pl.ds(c * side, side)] = ring.finish()
@@ -1100,7 +1098,7 @@
             pltpu.VMEM((3, r_up, up_width), BF16),
             pltpu.VMEM((3, r_up, up_width), BF16),
             dma((12, total - 1)), dma((12, total - 1)), dma((6, 4)), dma((6, 4)), dma((3, 4)), dma((7,)),
-            dma((2, 5)), dma((2, 4)), dma((3,)), dma((3,)),
+            dma((2, 5)), dma((2,)), dma((3,)), dma((3,)),
         ],
         compiler_params=pltpu.CompilerParams(
             collective_id=2, has_side_effects=True, vmem_limit_bytes=63 * MIB
@@ -1113,7 +1111,7 @@
 
 
 def final_kernel(
-    total, h_project, h_in, h_turned, part_down, hidden, d_hidden, tok, gain_one, valid, sums_two, d_group,
+    total, h_project, h_in, h_turned, part_down, hidden, d_hidden, tok, gains_all, ident_col, sums_two, d_group,
     o_in, output, d_tokens, o_vec, o_grp,
     project, turned, first_term, term, arrived, win, part, own_part, core_in, out_x, in_x, stage, landed,
     vec, grp, near_in, mid, far_in, far_grp,
@@ -1185,7 +1183,8 @@
 
         def some(r):
             s = pl.ds(r, step_rows)
-            output[s, :] = ((hidden[s, :] + summed_rows(0, r)) * valid[s, :]).astype(BF16)
+            valid = jnp.where(ident_col[me, s, :] >= 0.0, 1.0, 0.0)
+            output[s, :] = ((hidden[s, :] + summed_rows(0, r)) * valid).astype(BF16)
 
         by_rows(some)
 
@@ -1199,7 +1198,7 @@
             s = pl.ds(r, step_rows)
             e = summed_rows(1, r)
             normal, scale = norm_parts(tok[s, :].astype(F32), EPSILON)
-            with_gain = e * gain_one[...]
+            with_gain = e * gains_all[0:1, :]
             vec[0:1, :] += jnp.sum(e * normal, axis=0, keepdims=True)
             vec[1:2, :] += jnp.sum(e, axis=0, keepdims=True)
             value = d_hidden[s, :] + scale * (
@@ -1300,10 +1299,27 @@
             hop(slot, step).start()
         return carry
 
-    def fetch_win(n):
-        return pltpu.make_async_copy(
-            h_in.at[pl.ds(n * 256, 256), :], win.at[n % 2], win_sem.at[n % 2]
-        )
+    parts = h_in.shape[0]
+    part_width = h_in.shape[2]
+
+    class fetch_win:
+        def __init__(self, n):
+            self.copies = [
+                pltpu.make_async_copy(
+                    h_in.at[h, pl.ds(n * 256, 256), :],
+                    win.at[n % 2, :, pl.ds(h * part_width, part_width)],
+                    win_sem.at[n % 2, h],
+                )
+                for h in range(parts)
+            ]
+
+        def start(self):
+            for copy in self.copies:
+                copy.start()
+
+        def wait(self):
+            for copy in self.copies:
+                copy.wait()
 
     columns = width // 256
 
@@ -1354,11 +1370,12 @@
         lax.fori_loop(*plan[number], onward, 0)
     vectors_far()
     terms(total - 1, term)
-    pieces = column_pieces(o_in.shape[1])
+    pieces = column_pieces()
 
     def place(other, value):
-        for base, stride, off, size in pieces:
+        for base, stride, h, off, size in pieces:
             start = pl.multiple_of(base + other * stride, 128)
+            off = h * part_width + off
             o_in[:, pl.ds(start, size)] = value[:, off : off + size]
 
     def sent_across(relation):
@@ -1439,7 +1456,7 @@
             pltpu.VMEM((8, width // GROUP), F32),
             pltpu.VMEM((total - 1, 8, 128), F32),
             pltpu.VMEM((total - 1, 8, 128), F32),
-            dma((2,)), dma((2,)), dma((4, total - 1)), dma((4, total - 1)), dma((3,)), dma((3,)),
+            dma((2,)), dma((2, 2)), dma((4, total - 1)), dma((4, total - 1)), dma((3,)), dma((3,)),
             dma((2, 3)), dma((2, 3)), dma((2,)), dma((3,)), dma((3,)), dma((2, total - 1)), dma((2, total - 1)),
         ],
         compiler_params=pltpu.CompilerParams(
@@ -1447,54 +1464,6 @@
         ),
         name="final_sums",
     )(d_project, full_in, turned, down, hidden, d_hidden, tok, gain_one, valid, sums_two, d_group)
-
-
-def layout(seq_lens, seq_owner, seq_offset, device_id, buffer_len):
-    positions = jnp.arange(buffer_len, dtype=jnp.int32)[:, None]
-    inside = (
-        (seq_owner[None, :] == device_id)
-        & (seq_lens[None, :] > 0)
-        & (positions >= seq_offset[None, :])
-        & (positions < seq_offset[None, :] + seq_lens[None, :])
-    )
-    number = jnp.arange(seq_lens.shape[0], dtype=jnp.int32)[None, :] + 1
-    seq_ident = jnp.sum(jnp.where(inside, number, 0), axis=1) - 1
-    starts = jnp.sum(jnp.where(inside, seq_offset[None, :], 0), axis=1)
-    places = jnp.where(seq_ident >= 0, positions[:, 0] - starts, 0)
-    return seq_ident, places
-
-
-def rotation(places):
-    half_size = QKH // 2
-    pair_index = jnp.arange(half_size, dtype=F32) / half_size
-    inverse_freq = 10000.0 ** (-pair_index)
-    zeta_base = (pair_index + 0.4) / 1.4
-    offsets = places.astype(F32)[..., None]
-    angles = offsets * inverse_freq
-    growth = zeta_base ** (offsets / 512.0)
-    return jnp.cos(angles), jnp.sin(angles), growth
-
-
-def rotate_xpos(vectors, cosine, sine, scale):
-    half = QKH // 2
-    first, second = vectors[..., :half], vectors[..., half:]
-    cosine, sine, scale = cosine[..., None, :], sine[..., None, :], scale[..., None, :]
-    return jnp.concatenate(
-        [(first * cosine - second * sine) * scale, (second * cosine + first * sine) * scale], axis=-1
-    )
-
-
-def rotate_back(vectors, cosine, sine, scale):
-    return rotate_xpos(vectors, cosine, -sine, scale)
-
-
-def decay_tables(ident, heads):
-    positions = jnp.arange(ident.shape[-1], dtype=jnp.int32)
-    distance = positions[:, None] - positions[None, :]
-    linked = (distance >= 0) & (ident[:, :, None] == ident[:, None, :]) & (ident[:, :, None] >= 0)
-    rates = jnp.log1p(-(2.0 ** (-5.0 - heads.astype(F32))))
-    powers = jnp.maximum(distance, 0).astype(F32)
-    return jnp.where(linked[:, None], jnp.exp(rates[:, None, None] * powers[None])[None], 0.0)
 
 
 def mean(values):
@@ -1524,60 +1493,41 @@
     me, inner = lax.axis_index("dp"), lax.axis_index("fsdp")
     small, large = ln1_gain.shape[0], group_gain.shape[0]
 
-    pack = jnp.concatenate([ln1_gain, ln1_bias, ln2_gain, ln2_bias, group_gain]).astype(F32)
-    pack = jnp.pad(pack, (0, 1024 - pack.shape[0])).reshape(8, 128)
-    full_in, own_up, tok, cot, vec = gather_all(total, w_in, w_up, tokens, cotangent, pack)
-    full_in = full_in.reshape(width, -1)
-    vec = vec.reshape(total, GROUP, 1024)
-
-    def vector(number):
-        part = vec[:, :, number * small : (number + 1) * small]
-        return jnp.swapaxes(part, 0, 1).reshape(1, width)
-
-    gain_one, bias_one, gain_two, bias_two = (vector(n) for n in range(4))
-    gain_group = lax.dynamic_index_in_dim(vec, me, 1, keepdims=False)[:, 4 * small : 4 * small + large]
-    gain_group = gain_group.reshape(heads, 1, VH)
-
-    devices = jnp.arange(GROUP, dtype=jnp.int32) * total + inner
-    ident, places = jax.vmap(lambda d: layout(seq_lens, seq_owner, seq_offset, d, rows))(devices)
-    valid = (ident >= 0).astype(F32)[..., None]
-    own_valid = lax.dynamic_index_in_dim(valid, me, 0, keepdims=False)
     count = GROUP * rows
-
-    tables = rotation(places.reshape(count))
-    tables = (*tables, 1.0 / tables[2])
-    distance = jnp.arange(rows)[:, None] - jnp.arange(rows)[None, :]
+    vectors = jnp.stack([ln1_gain, ln1_bias, ln2_gain, ln2_bias]).astype(F32)
+    pack = jnp.zeros((8, 128), F32)
+    pack = lax.dynamic_update_slice(pack, vectors, (0, lax.rem(inner * small, 128)))
+    pack = lax.dynamic_update_slice(pack, group_gain.astype(F32)[None], (4, lax.rem(inner * large, 128)))
     rates = jnp.log1p(-(2.0 ** (-5.0 - (me * heads + jnp.arange(heads)).astype(F32))))
-    powers = jnp.exp(rates[:, None, None] * jnp.maximum(distance, 0).astype(F32)[None])
-    powers = jnp.where(distance[None] >= 0, powers, 0.0)
+    rates = jnp.broadcast_to(rates[:, None, None], (heads, 1, rows))
+    entries = jnp.stack([seq_lens, seq_owner, seq_offset])
     (
-        full_up, full_out, full_down, turned, query, keys, values, gate, mixed, gated, hidden, two,
+        full_in, full_up, full_out, full_down, seed, turned, query, keys, values, gate, mixed, gated, hidden, two,
+        own_seed, cosine, sine, growth, shrink, powers, ident_col, ident_row, gains, gain_group,
     ) = forward(
-        total, own_up, w_out, w_down, full_in, tok, gain_one, bias_one, gain_group, tables, powers,
-        ident[:, :, None], ident[:, None, :], tokens, gain_two, bias_two,
+        total, w_in, w_up, w_out, w_down, tokens, cotangent, pack, rates, entries[:, :, None], entries[:, None, :]
     )
+    tables = (cosine, sine, growth, shrink)
     full_up = full_up.reshape(width, -1)
     full_out = full_out.reshape(-1, width)
     full_down = full_down.reshape(-1, width)
     two = two.reshape(count, width)
+    seed = seed.reshape(count, width)
     upper = dot(two, full_up)
     cdf = 0.5 * (1.0 + lax.erf(upper * (0.5**0.5)))
     active = (upper * cdf).astype(BF16)
     down = dot(active, full_down).astype(BF16).reshape(GROUP, rows, width)
 
-    seed = (cot.astype(F32) * valid).astype(BF16)
-    own_seed = (cotangent.astype(F32) * own_valid).astype(BF16)
-    seed = seed.reshape(count, width)
     slope = cdf + upper * jnp.exp(-0.5 * upper * upper) * (2.0 * jnp.pi) ** -0.5
     d_upper = (dot_back(seed, full_down) * slope).astype(BF16)
     d_two = dot_back(d_upper, full_up).astype(BF16).reshape(GROUP, rows, width)
     g_down = dot_rows(active, seed).astype(BF16)
     grad_down, grad_up, grad_out, d_hidden, _, sums_two, d_group, d_project = backward(
-        total, g_down, two, d_upper, d_two, own_seed, hidden, gain_two, gated, full_out, query, keys, values,
-        gate, mixed, tables, powers, ident[:, :, None], ident[:, None, :], gain_group,
+        total, g_down, two, d_upper, d_two, own_seed, hidden, gains, gated, full_out, query, keys, values,
+        gate, mixed, tables, powers, ident_col, ident_row, gain_group,
     )
     grad_in, output, d_tokens, vec_one, vec_two = final(
-        total, d_project, full_in, turned, down, hidden, d_hidden, tokens, gain_one, own_valid, sums_two, d_group
+        total, d_project, full_in, turned, down, hidden, d_hidden, tokens, gains, ident_col, sums_two, d_group
     )
     grads = lax.dynamic_slice(vec_one, (0, lax.rem(inner * small, 128)), (4, small))
     grad_group = lax.dynamic_slice(vec_two, (0, lax.rem(inner * large, 128)), (1, large))[0]

time: 644 us -> 617 us (0.958)
  local copies, waits for them, and re-layouts: 24.5 us -> 14.2 us
  other arithmetic: 10.3 us -> 2.09 us
  Pallas kernels: 565 us -> 558 us
    pallas_call x1 -> x0, Pallas kernels: 140 us -> none  [gather_all(): pl.pallas_call(functools.partial(gather_kernel, total), out_shape=[jax.Sh...]
    pallas_call x1, Pallas kernels: 144 us -> 276 us  [forward(): pl.pallas_call(functools.partial(forward_kernel, total), out_shape=[jax.S...]
where the time goes in v4:
time: 617 us; the launch traced here: 608 us
  Pallas kernels  558 us (90%)
  matrix products  32.5 us (5%)
  local copies, waits for them, and re-layouts  14.2 us (2%)
    pallas_call x1, Pallas kernels, forward(): pl.pallas_call(functools.partial(forward_kernel, total), out_shape=[jax.S...  276 us
    pallas_call x1, Pallas kernels, final(): pl.pallas_call(functools.partial(final_kernel, total), out_shape=[jax.Sha...  150 us
    pallas_call x1, Pallas kernels, backward(): pl.pallas_call(functools.partial(backward_kernel, total), out_shape=[jax....  131 us
    dot_general x2, matrix products, dot(): return jnp.dot(left, right, preferred_element_type=F32)  14.3 us

profile of v4, /device:TPU:1, one launch (start us, length us, event | category | flops | bytes accessed | tf_op | source)
XLA Modules:
  0.0 607.6 jit_solution(9947755855804025893)
XLA Ops:
  0.7 0.7 bitcast_convert_fusion
  1.3 0.6 broadcast_in_dim.24.rates
  2.0 0.7 maximum_convert_fusion
  2.7 0.3 dynamic_update_slice.6
  3.1 0.0 copy-start.5
  3.1 0.7 pad_add_fusion
  3.8 0.6 broadcast_in_dim.26.seq_rows
  4.3 0.8 copy.26.seq_cols
  5.1 0.0 copy-done.5
  5.1 276.4 %forward_retention.1 = (bf16[2,2048,1536]{2,1,0:T(8,128)(2,1)}, bf16[4,8,64,1024]{3,2,1,0:T(8,128)(2,1)}, bf16[8,128,2048]{2,1,0:T(8,128)(2,1)}, bf16[8,128,2048...) custom-call(bf16[64,12288]{1,0:T(8,128)(2,1)} %w_in.1, ...), custom_call_target="tpu_custom_call" | custom-call | tf_op jit(solution)/shard_map/forward_retention/pallas_call | solution.py:670
  281.5 0.0 copy-start.7
  281.5 0.0 copy-start.8
  281.5 8.2 %multiply_convert_fusion = (bf16[1024,1024]{1,0:T(8,128)(2,1)S(1)}, f32[1024,1024]{1,0:T(8,128)S(1)}) fusion(bf16[1024,2048]{1,0:T(8,128)(2,1)} %bitcast.41, bf16[2048,1024]{1,0:T(8,128)(2,1)} %bitcast.51), kind=kOutput, calls=%fused_computation.7 | convolution fusion | flops 4300210176 | bytes 14680064 | tf_op jit(solution)/shard_map/dot_general | solution.py:95
  289.7 0.0 copy-done.7
  289.7 0.0 copy-done.8
  289.8 5.8 fusion.5.d_upper
  295.6 0.0 copy-start.1
  295.6 6.1 convolution_convert_fusion
  301.7 6.3 %convolution_convert_fusion.2.g_down = bf16[1024,2048]{1,0:T(8,128)(2,1)} fusion(bf16[1024,1024]{1,0:T(8,128)(2,1)S(1)} %get-tuple-element.89, bf16[1024,2048]{1,0:T(8,128)(2,1)S(1)} %bitcast.54), kind=kOutput, calls=%fused_computation.11 | convolution fusion | flops 4297064448 | bytes 10485760 | tf_op jit(solution)/shard_map/dot_general | solution.py:99
  308.0 0.0 copy-done.1
  308.0 6.1 %convolution_convert_fusion.1 = bf16[1024,2048]{1,0:T(8,128)(2,1)} fusion(bf16[1024,1024]{1,0:T(8,128)(2,1)S(1)} %fusion.5.d_upper, bf16[2048,1024]{1,0:T(8,128)(2,1)S(1)} %bitcast.52), kind=kOutput, calls=%fused_computation.10 | convolution fusion | flops 4297064448 | bytes 10485760 | tf_op jit(solution)/shard_map/dot_general | solution.py:103
  314.1 130.7 %backward_retention.1 = (f32[128,2048]{1,0:T(8,128)}, f32[64,4096]{1,0:T(8,128)}, f32[128,2048]{1,0:T(8,128)}, f32[256,2048]{1,0:T(8,128)}, bf16[4,256,2048]{2,1...) custom-call(bf16[1024,2048]{1,0:T(8,128)(2,1)} %convolution_convert_fusion.2.g_down, ...), custom_call_target="tpu_custom_call" | custom-call | tf_op jit(solution)/shard_map/backward_retention/pallas_call | solution.py:1073
  444.8 150.4 %final_sums.1 = (f32[64,12288]{1,0:T(8,128)}, bf16[256,2048]{1,0:T(8,128)(2,1)}, bf16[256,2048]{1,0:T(8,128)(2,1)}, f32[8,128]{1,0:T(8,128)}, f32[8,128]{1,0:T(8,128)}) custom-call(bf16[1024,3072]{1,0:T(8,128)(2,1)} %get-tuple-element.69.h_project, bf16[2,2048,1536]{2,1,0:T(8,128)(2,1)} %get-tuple-element.70.h_in, ...), custom_call_target="tpu_custom_call" | custom-call | tf_op jit(solution)/shard_map/final_sums/pallas_call | solution.py:1434
  595.2 1.3 slice_bitcast_fusion.2
  596.6 0.7 constant_dynamic-slice_fusion
  597.3 0.5 slice_bitcast_fusion
  597.9 2.3 copy.35
  600.2 2.4 copy.36
  602.6 1.7 copy.37
  604.2 1.0 copy.38
  605.2 1.0 copy.39
  606.2 1.0 copy.40
  (13 shorter events, 0.1 us)
Async XLA Ops:
  3.1 2.0 copy-start.5
  281.5 8.2 %copy-start.7 = (bf16[4,256,2048]{2,1,0:T(8,128)(2,1)S(1)}, bf16[4,256,2048]{2,1,0:T(8,128)(2,1)}, u32[]{:S(2)}) copy-start(bf16[4,256,2048]{2,1,0:T(8,128)(2,1)} %get-tuple-element.49) | copy-start | bytes 12582916
  281.5 8.2 %copy-start.8 = (bf16[8,128,2048]{2,1,0:T(8,128)(2,1)S(1)}, bf16[8,128,2048]{2,1,0:T(8,128)(2,1)}, u32[]{:S(2)}) copy-start(bf16[8,128,2048]{2,1,0:T(8,128)(2,1)} %get-tuple-element.50) | copy-start | bytes 12582916
  295.6 12.4 %copy-start.1 = (bf16[1024,1024]{1,0:T(8,128)(2,1)}, bf16[1024,1024]{1,0:T(8,128)(2,1)S(1)}, u32[]{:S(2)}) copy-start(bf16[1024,1024]{1,0:T(8,128)(2,1)S(1)} %fusion.5.d_upper) | copy-start | bytes 6291460
  301.6 6.3 %copy-start.6 = (bf16[4,8,64,1024]{3,2,1,0:T(8,128)(2,1)S(1)}, bf16[4,8,64,1024]{3,2,1,0:T(8,128)(2,1)}, u32[]{:S(2)}) copy-start(bf16[4,8,64,1024]{3,2,1,0:T(8,128)(2,1)} %get-tuple-element.48) | copy-start | bytes 12582916
  595.2 7.3 %copy-start = (f32[64,12288]{1,0:T(8,128)S(1)}, f32[64,12288]{1,0:T(8,128)}, u32[]{:S(2)}) copy-start(f32[64,12288]{1,0:T(8,128)} %get-tuple-element.104) | copy-start | bytes 9437188
  600.2 4.1 copy-start.4
  602.6 2.6 copy-start.3
  602.6 3.6 copy-start.2

commit v5 on v4

--- a/solution.py
+++ b/solution.py
@@ -204,10 +204,10 @@
 def forward_kernel(
     total, w_in, w_up, w_out, w_down, tok, cot, pack, rates, seq_cols, seq_rows, curves,
     full_in, full_up, full_out, full_down, full_seed, o_turned, o_query, o_keys, o_values, o_gate, o_mixed,
-    o_gated, hidden, full_two, own_seed, cosine, sine, growth, shrink, powers, ident_col, ident_row, gains,
+    o_gated, o_active, o_upper, o_g_down, hidden, full_two, own_seed, cosine, sine, growth, shrink, powers, ident_col, ident_row, gains,
     gain_group,
     win, part, x, query, keys, values, gate, mixed, gated, wo, core_in, out_x, in_x, low, full_vec,
-    ring_send, ring_recv, own_sem, load_sem, store_sem, row_send, row_recv, row_own,
+    win_up, wd, ring_send, ring_recv, own_sem, load_sem, fetch_sem, store_sem, row_send, row_recv, row_own,
     swap_send, swap_recv, swap_own, vec_send, vec_recv,
 ):
     at = Place(total)
@@ -255,26 +255,35 @@
         else:
             swap(relation, slot).wait_recv()
 
-    for relation in (1, 0, 2, 3):
-        for slot in range(last):
-            swap(relation, slot).start()
-    for relation in range(4):
-        swap(relation, last + 1).start()
+    for h in range(heads):
+        for relation in (1, 0, 2, 3):
+            for slot in range(last):
+                if pieces[slot][2] == h:
+                    swap(relation, slot).start()
+        if h == 0:
+            for relation in range(4):
+                swap(relation, last + 1).start()
     for slot in (last + 2, last):
         for relation in (1, 0, 2, 3):
             swap(relation, slot).start()
 
-    def in_ring(relation, way, slot):
+    def in_ring(h, relation):
         def place(which):
-            return win.at[:, rows_in(flip(me, relation), which), :]
-
-        return Passing(at, way, place(inner), place, ring_send.at[slot], ring_recv.at[slot])
-
-    near = [in_ring(0, 0, 12), in_ring(1, 1, 13)]
-    far_in = [in_ring(2, 0, 14), in_ring(3, 1, 15)]
+            return win.at[h, rows_in(flip(me, relation), which), :]
+
+        slot = 12 + 4 * h + relation
+        return Passing(at, relation % 2, place(inner), place, ring_send.at[slot], ring_recv.at[slot])
+
+    ins = [[in_ring(h, relation) for relation in range(4)] for h in range(heads)]
+    near, far_in = ins[0][:2], ins[0][2:]
+
+    def await_head(h, relation):
+        for slot in range(last):
+            if pieces[slot][2] == h:
+                arrived(relation, slot)
+
     for relation in (0, 1):
-        for slot in range(last):
-            arrived(relation, slot)
+        await_head(0, relation)
         near[relation].begin()
 
     def layout_of(b, down):
@@ -321,8 +330,7 @@
     for ring in near:
         ring.onward(1)
     for relation in (2, 3):
-        for slot in range(last):
-            arrived(relation, slot)
+        await_head(0, relation)
         far_in[relation - 2].begin()
     for relation in (1, 0, 2, 3):
         swap(relation, last + 3).start()
@@ -400,106 +408,104 @@
         beside[n]()
     for ring in far_in:
         ring.onward(total - 2)
+    for h in range(1, heads):
+        for relation in range(4):
+            await_head(h, relation)
+            ins[h][relation].begin()
     outs, ups, downs = weight_rings(
         at, w_out, w_down, full_up, full_out, full_down, ring_send, ring_recv
     )
-    for ring in outs:
-        ring.begin()
     own_copies = [
         pltpu.make_async_copy(w_out, full_out.at[inner], own_sem.at[0]),
         pltpu.make_async_copy(w_down, full_down.at[inner], own_sem.at[1]),
     ]
     for copy in own_copies:
         copy.start()
-    for ring in near + far_in:
-        ring.finish()
-    store_win = pltpu.make_async_copy(win, full_in, load_sem.at[1])
-    store_win.start()
-
+    plan = tick_plan(total, 6)
     tile = 512
-    spots = 6
-    plan = tick_plan(total, spots)
-    span = [stop - start for start, stop in plan]
-
-    def spot(h, number):
-        lows = [plan[k * (spots // heads) + number][0] for k in range(heads)]
-        highs = [plan[k * (spots // heads) + number][1] for k in range(heads)]
-        low_step = lows[0] + h * (lows[1] - lows[0])
-        high_step = highs[0] + h * (highs[1] - highs[0])
-        run_steps(outs, low_step, high_step)
-
-    def project(h, off):
-        def at_tile(m, use):
-            r = pl.ds(pl.multiple_of(m * tile, tile), tile)
-            use(r, dot(x[r, :], win[h, :, off : off + QKH]))
-
-        return at_tile
-
-    def head(h, carry):
-        def rotate_tiles(m, carry):
-            def put_query(r, value):
-                turned = rotated(value, cosine[r, :], sine[r, :], growth[r, :])
-                query[h, r, :] = (turned * QKH ** (-0.5)).astype(BF16)
-
-            def put_keys(r, value):
-                keys[h, r, :] = rotated(value, cosine[r, :], sine[r, :], shrink[r, :]).astype(BF16)
-
-            project(h, 0)(m, put_query)
-            project(h, QKH)(m, put_keys)
+
+    def project(h, off, m):
+        r = pl.ds(pl.multiple_of(m * tile, tile), tile)
+        return r, dot(x[r, :], win[h, :, off : off + QKH])
+
+    def turn_tile(h, m):
+        r, value = project(h, 0, m)
+        turned = rotated(value, cosine[r, :], sine[r, :], growth[r, :])
+        query[h, r, :] = (turned * QKH ** (-0.5)).astype(BF16)
+        r, value = project(h, QKH, m)
+        keys[h, r, :] = rotated(value, cosine[r, :], sine[r, :], shrink[r, :]).astype(BF16)
+
+    def plain_tile(h, c, m):
+        off = c * QKH
+        r, value = project(h, 2 * QKH + off, m)
+        values[h, r, off : off + QKH] = value.astype(BF16)
+        r, value = project(h, 2 * QKH + VH + off, m)
+        gate[h, r, off : off + QKH] = value
+
+    def retain(h, b):
+        r = pl.ds(pl.multiple_of(b * rows, rows), rows)
+        raw = dot_back(query[h, r, :], keys[h, r, :])
+        linked = (ident_col[b] == ident_row[b]) & (ident_col[b] >= 0.0)
+        masked = (raw * jnp.where(linked, powers[h], 0.0)).astype(BF16)
+        mixed[h, r, :] = dot(masked, values[h, r, :])
+
+        def some_rows(n, carry):
+            s = pl.ds(pl.multiple_of(b * rows + n * step_rows, step_rows), step_rows)
+            normal, _ = norm_parts(mixed[h, s, :], GROUP_EPSILON)
+            z = gate[h, s, :]
+            result = z / (1.0 + jnp.exp(-z)) * (normal * gain_group[h])
+            gated[s, h * VH : (h + 1) * VH] = result.astype(BF16)
             return carry
 
-        lax.fori_loop(0, count // tile, rotate_tiles, 0)
-        spot(h, 0)
-
-        def plain_tiles(m, carry):
-            for c in range(VH // QKH):
-                off = c * QKH
-
-                def put_values(r, value, off=off):
-                    values[h, r, off : off + QKH] = value.astype(BF16)
-
-                def put_gate(r, value, off=off):
-                    gate[h, r, off : off + QKH] = value
-
-                project(h, 2 * QKH + off)(m, put_values)
-                project(h, 2 * QKH + VH + off)(m, put_gate)
+        lax.fori_loop(0, rows // step_rows, some_rows, 0)
+
+    def looped(count_of, body):
+        def some(n, carry):
+            body(n)
             return carry
 
-        lax.fori_loop(0, count // tile, plain_tiles, 0)
-        spot(h, 1)
-
-        def buffer(b, carry):
-            r = pl.ds(pl.multiple_of(b * rows, rows), rows)
-            raw = dot_back(query[h, r, :], keys[h, r, :])
-            linked = (ident_col[b] == ident_row[b]) & (ident_col[b] >= 0.0)
-            masked = (raw * jnp.where(linked, powers[h], 0.0)).astype(BF16)
-            value = dot(masked, values[h, r, :])
-            mixed[h, r, :] = value
-            normal, _ = norm_parts(value, GROUP_EPSILON)
-            z = gate[h, r, :]
-            result = z / (1.0 + jnp.exp(-z)) * (normal * gain_group[h])
-            gated[r, pl.ds(pl.multiple_of(h * VH, VH), VH)] = result.astype(BF16)
-            return carry
-
-        lax.fori_loop(0, GROUP, buffer, 0)
-        spot(h, 2)
-        return carry
-
-    lax.fori_loop(0, heads, head, 0)
+        lax.fori_loop(0, count_of, some, 0)
+
+    def head_units(h):
+        return [
+            lambda: looped(count // tile, lambda m: turn_tile(h, m)),
+            lambda: looped(count // tile, lambda m: plain_tile(h, 0, m)),
+            lambda: looped(count // tile, lambda m: plain_tile(h, 1, m)),
+            lambda: looped(2, lambda b: retain(h, b)),
+            lambda: looped(2, lambda b: retain(h, 2 + b)),
+        ]
+
+    stores = []
+
+    def store_head(h):
+        for n, (src, dst) in enumerate(
+            ((win, full_in), (query, o_query), (keys, o_keys), (values, o_values), (gate, o_gate), (mixed, o_mixed))
+        ):
+            copy = pltpu.make_async_copy(src.at[h], dst.at[h], store_sem.at[h, n])
+            copy.start()
+            stores.append(copy)
+
+    for h in range(heads):
+        ring_set = ins[h + 1] if h + 1 < heads else outs
+        if h + 1 == heads:
+            for ring in outs:
+                ring.begin()
+        for ring in ins[h]:
+            ring.finish()
+        units = head_units(h)
+        for number in range(6):
+            if number < len(units):
+                units[number]()
+            run_steps(ring_set, *plan[number])
+        store_head(h)
     for relation in range(4):
         arrived(relation, last)
-    for ring in ups + downs:
+    for ring in ups:
         ring.begin()
     for ring in outs:
         ring.finish()
-    stores = [
-        pltpu.make_async_copy(src, dst, store_sem.at[1 + n])
-        for n, (src, dst) in enumerate(
-            ((query, o_query), (keys, o_keys), (values, o_values), (gate, o_gate), (mixed, o_mixed), (gated, o_gated))
-        )
-    ]
-    for copy in stores:
-        copy.start()
+    stores.append(pltpu.make_async_copy(gated, o_gated, store_sem.at[0, 6]))
+    stores[-1].start()
     own_copies[0].wait()
     block = w_out.shape[0]
     fetch = pltpu.make_async_copy(full_out, wo, load_sem.at[0])
@@ -508,8 +514,6 @@
 
     chunks = 4
     size = rows // chunks
-    rest = ups + downs
-    later = tick_plan(total, 6)
 
     def branch(relation):
         b = flip(me, relation)
@@ -555,6 +559,7 @@
     for c in range(chunks):
         copy(0, c).start()
     branch(2)
+    run_steps(ups, *plan[0])
     for c in range(chunks):
         r = rows_of(c)
         copy(0, c).wait_recv()
@@ -564,7 +569,10 @@
     for c in range(chunks):
         copy(1, c).start()
     branch(0)
-    run_steps(rest, *later[0])
+    run_steps(ups, *plan[1])
+    for copy_out in stores:
+        copy_out.wait()
+    wait_sent([ring for rings in ins for ring in rings], total)
 
     def turn(n, carry):
         i, j = n // (count // 256), lax.rem(n, count // 256)
@@ -572,11 +580,9 @@
         win[0, i, j] = x[j, i].T
         return carry
 
-    store_win.wait()
-    wait_sent(near + far_in, total)
-    lax.fori_loop(0, (width // 256) * (count // 256), turn, 0)
-    store_turned = pltpu.make_async_copy(win.at[0, :, pl.ds(0, count)], o_turned, store_sem.at[0])
-    store_turned.start()
+    blocks = (width // 256) * (count // 256)
+    lax.fori_loop(0, blocks // 2, turn, 0)
+    run_steps(ups, *plan[2])
     for c in range(chunks):
         r = rows_of(c)
         copy(1, c).wait_recv()
@@ -596,34 +602,115 @@
         copy(3, c).start()
         copy(4, c).start()
         store(c).start()
-        if c % 2:
-            run_steps(rest, *later[1 + c // 2])
+        if c:
+            run_steps(ups, *plan[2 + c])
+    for ring in downs:
+        ring.begin()
+    lax.fori_loop(blocks // 2, blocks, turn, 0)
+    store_turned = pltpu.make_async_copy(win.at[0, :, pl.ds(0, count)], o_turned, own_sem.at[0])
+    store_turned.start()
+    for relation in range(4):
+        arrived(relation, last + 3)
+    fetch_seed = [
+        pltpu.make_async_copy(full_seed.at[b], x.at[pl.ds(b * rows, rows)], fetch_sem.at[b])
+        for b in range(GROUP)
+    ]
+    for fetch in fetch_seed:
+        fetch.start()
+    for ring in ups:
+        ring.finish()
+    fetch_up = [
+        pltpu.make_async_copy(full_up.at[b], win_up.at[b], fetch_sem.at[GROUP + b]) for b in range(GROUP)
+    ]
+    for fetch in fetch_up:
+        fetch.start()
     for c in range(chunks):
         copy(3, c).wait_recv()
         copy(5, c).start()
         if c % 2:
-            run_steps(rest, *later[3 + c // 2])
+            run_steps(downs, *plan[c // 2])
     for c in range(chunks):
         copy(4, c).wait_recv()
         copy(5, c).wait_recv()
         store(c).wait()
         for kind in range(6):
             copy(kind, c).wait_send()
-    run_steps(rest, *later[5])
-    for ring in rest:
+    fetch_two = pltpu.make_async_copy(full_two, part, load_sem.at[1])
+    fetch_two.start()
+    for fetch in fetch_seed + fetch_up:
+        fetch.wait()
+    fetch_two.wait()
+
+    quarters = heads * VH // 256
+
+    def upper_tile(n, carry):
+        b, j = n // quarters, lax.rem(n, quarters)
+        c = pl.ds(pl.multiple_of(j * 256, 256), 256)
+        r = pl.ds(pl.multiple_of(b * rows, rows), rows)
+        upper = dot(part[b], win_up[:, :, :, c].reshape(width, 256))
+        cdf = 0.5 * (1.0 + lax.erf(upper * (0.5**0.5)))
+        gated[r, c] = (upper * cdf).astype(BF16)
+        half = pl.ds(pl.multiple_of(lax.rem(j, 2) * 256, 256), 256)
+        gate[j // 2, r, half] = cdf + upper * jnp.exp(-0.5 * upper * upper) * (2.0 * np.pi) ** -0.5
+        return carry
+
+    tiles = GROUP * quarters
+    lax.fori_loop(0, tiles // 2, upper_tile, 0)
+    run_steps(downs, *plan[2])
+    lax.fori_loop(tiles // 2, tiles, upper_tile, 0)
+    run_steps(downs, *plan[3])
+    store_active = pltpu.make_async_copy(gated, o_active, store_sem.at[0, 0])
+    store_active.start()
+    per_tile = 256 // block
+    wide = 512
+
+    def down_tile(n, carry):
+        i, j = n // (width // wide), lax.rem(n, width // wide)
+        a = pl.ds(pl.multiple_of(i * 256, 256), 256)
+        c = pl.ds(pl.multiple_of(j * wide, wide), wide)
+        value = dot_rows(gated[:, a], x[:, c]).astype(BF16)
+        wo[pl.ds(i * per_tile, per_tile), :, c] = value.reshape(per_tile, block, wide)
+        return carry
+
+    tiles = quarters * (width // wide)
+    lax.fori_loop(0, tiles // 2, down_tile, 0)
+    run_steps(downs, *plan[4])
+    lax.fori_loop(tiles // 2, tiles, down_tile, 0)
+    run_steps(downs, *plan[5])
+    store_down = pltpu.make_async_copy(wo, o_g_down, store_sem.at[0, 1])
+    store_down.start()
+    own_copies[1].wait()
+    for ring in downs:
         ring.finish()
-    wait_sent(outs + rest, total)
-    own_copies[1].wait()
-    arrived(0, last + 3)
+    fetch = pltpu.make_async_copy(full_down, wd, load_sem.at[0])
+    fetch.start()
+    fetch.wait()
+
+    def d_upper_tile(n, carry):
+        h, j = n // 4, lax.rem(n, 4)
+        m, side = j // 2, lax.rem(j, 2)
+        r = pl.ds(pl.multiple_of(m * tile, tile), tile)
+        c = pl.ds(pl.multiple_of(side * 256, 256), 256)
+        piece = wd[pl.ds((2 * h + side) * per_tile, per_tile)].reshape(256, width)
+        values[h, r, c] = (dot_back(x[r, :], piece) * gate[h, r, c]).astype(BF16)
+        return carry
+
+    lax.fori_loop(0, 4 * heads, d_upper_tile, 0)
+    last_stores = [store_active, store_down] + [
+        pltpu.make_async_copy(values.at[h], o_upper.at[:, pl.ds(h * VH, VH)], store_sem.at[0, 2 + h])
+        for h in range(heads)
+    ]
+    for copy_out in last_stores[2:]:
+        copy_out.start()
+    wait_sent(outs + downs + ups, total)
     for relation in (1, 2, 3):
-        arrived(relation, last + 3)
         for slot in range(last + 4):
             swap(relation, slot).wait_send()
     for n in range(1, total):
         spread(n).wait_send()
     store_turned.wait()
-    for c in stores:
-        c.wait()
+    for copy_out in last_stores:
+        copy_out.wait()
 
 
 def forward(total, w_in, w_up, w_out, w_down, tok, cot, pack, rates, seq_cols, seq_rows):
@@ -653,6 +740,9 @@
         ((GROUP, rows, width), BF16),
         ((width, count), BF16),
         *kept,
+        kept[-1],
+        kept[-1],
+        ((total,) + w_out.shape, BF16),
     )
     in_vmem = (
         ((rows, width), BF16),
@@ -683,8 +773,10 @@
             pltpu.VMEM((rows, width), BF16),
             pltpu.VMEM((rows, width), BF16),
             pltpu.VMEM((total, GROUP, 8, 128), F32),
-            dma((16, total - 1)), dma((16, total - 1)), dma((2,)), dma((2,)),
-            dma((7,)), dma((6, 4)), dma((6, 4)), dma((4,)),
+            pltpu.VMEM((GROUP, total, w_up.shape[0], w_up.shape[1] // GROUP), BF16),
+            pltpu.VMEM((total,) + w_down.shape, BF16),
+            dma((20, total - 1)), dma((20, total - 1)), dma((2,)), dma((2,)), dma((2 * GROUP,)),
+            dma((heads, 7)), dma((6, 4)), dma((6, 4)), dma((4,)),
             dma((3, 12)), dma((3, 12)), dma((12,)), dma((total - 1,)), dma((total - 1,)),
         ],
         compiler_params=pltpu.CompilerParams(
@@ -730,10 +822,10 @@
 
 
 def backward_kernel(
-    total, g_down, two, d_upper, part, seed, hidden, gains_all, h_gated, h_out, h_query, h_keys, h_values, h_gate,
+    total, g_down, two, d_upper, h_up, seed, hidden, gains_all, h_gated, h_out, h_query, h_keys, h_values, h_gate,
     h_mixed, cosine, sine, growth, shrink, powers, ident_col, ident_row, gain_group,
     o_down, o_up, o_out, d_hidden, full_branch, sums, o_group, o_project,
-    g_up, g_out, arrived, wide_buf, narrow_buf, wo, own_part, core_in, out_x, in_x, low,
+    g_up, g_out, arrived, wide_buf, narrow_buf, wo, part, core_in, out_x, in_x, low,
     query, keys, values, gate, mixed, back, d_mixed, staged, stage, landed,
     ring_send, ring_recv, row_send, row_recv, row_own, load_sem, unit_sem, out_sem, a2a_send, a2a_recv,
 ):
@@ -800,25 +892,19 @@
             src, dst, dev = full_branch.at[far, r], full_branch.at[far, r], core
         return remote(src, dst, row_send.at[kind, c], row_recv.at[kind, c], dev)
 
-    def load(which, c):
-        r = rows_of(c)
-        source = far if which == 0 else me
-        return pltpu.make_async_copy(part.at[source, r], own_part.at[which, r], row_own.at[which, c])
-
     def store(c):
         r = rows_of(c)
-        return pltpu.make_async_copy(low.at[r], full_branch.at[me, r], row_own.at[2, c])
-
-    for which in (0, 1):
-        for c in range(chunks):
-            copy(which, c).start()
-            load(which, c).start()
+        return pltpu.make_async_copy(low.at[r], full_branch.at[me, r], row_own.at[c])
+
     for ring in downs:
         ring.begin()
+    upper_columns = pl.ds(0, up_width)
+    fetch_upper = pltpu.make_async_copy(d_upper, g_out.at[:, upper_columns], load_sem.at[1])
+    fetch_up = pltpu.make_async_copy(h_up, g_up, load_sem.at[7])
     fetch_two = pltpu.make_async_copy(two, wide_buf, load_sem.at[0])
-    fetch_upper = pltpu.make_async_copy(d_upper, narrow_buf, load_sem.at[1])
+    fetch_gated = pltpu.make_async_copy(h_gated, narrow_buf, load_sem.at[8])
     fetch_out = pltpu.make_async_copy(h_out, wo, load_sem.at[2])
-    for fetch in (fetch_two, fetch_upper, fetch_out):
+    for fetch in (fetch_upper, fetch_up, fetch_two, fetch_gated, fetch_out):
         fetch.start()
 
     def unit_loads(unit, slot):
@@ -836,19 +922,17 @@
 
     def send_sums(c):
         r = rows_of(c)
-        load(0, c).wait()
         copy(0, c).wait_recv()
-        out_x[r, :] = (own_part[0, r, :].astype(F32) + core_in[0, r, :].astype(F32)).astype(BF16)
+        out_x[r, :] = (part[far, r, :].astype(F32) + core_in[0, r, :].astype(F32)).astype(BF16)
         copy(2, c).start()
 
     def norm_back(c):
-        load(1, c).wait()
         copy(1, c).wait_recv()
         copy(2, c).wait_recv()
 
         def some_rows(n, carry):
             s = pl.ds(pl.multiple_of(c * size + n * step_rows, step_rows), step_rows)
-            e = own_part[1, s, :].astype(F32) + core_in[1, s, :].astype(F32) + in_x[s, :].astype(F32)
+            e = part[me, s, :].astype(F32) + core_in[1, s, :].astype(F32) + in_x[s, :].astype(F32)
             normal, scale = norm_parts(hidden[s, :], EPSILON)
             with_gain = e * gains_all[2:3, :]
             sums[0:1, :] += jnp.sum(e * normal, axis=0, keepdims=True)
@@ -869,18 +953,38 @@
 
     sums[...] = jnp.zeros_like(sums)
     o_group[...] = jnp.zeros_like(o_group)
+    def d_two(relation):
+        b = flip(me, relation)
+        r = pl.ds(pl.multiple_of(b * rows, rows), rows)
+
+        def column(n, carry):
+            c = pl.ds(pl.multiple_of(n * 256, 256), 256)
+            part[b, :, c] = dot_back(g_out[r, :up_width], g_up[c, :]).astype(BF16)
+            return carry
+
+        lax.fori_loop(0, width // 256, column, 0)
+
+    plan = tick_plan(total, 6)
+    fetch_upper.wait()
+    fetch_up.wait()
+    d_two(3)
+    for c in range(chunks):
+        copy(0, c).start()
+    d_two(2)
     for c in range(chunks):
         send_sums(c)
-    plan = tick_plan(total, 6)
     add_steps(downs, *plan[0])
+    d_two(1)
+    for c in range(chunks):
+        copy(1, c).start()
+    d_two(0)
     fetch_two.wait()
-    fetch_upper.wait()
-
-    def grad_tiles(left, right, out, start, stop):
+
+    def grad_tiles(left, right, span, out, start, stop):
         wide = 512
 
         def tile(n, carry):
-            rows_n = right.shape[1] // wide
+            rows_n = span // wide
             i, j = n // rows_n, lax.rem(n, rows_n)
             a = pl.ds(pl.multiple_of(i * 256, 256), 256)
             c = pl.ds(pl.multiple_of(j * wide, wide), wide)
@@ -891,7 +995,7 @@
 
     tiles = (width // 256) * (up_width // 512)
     for quarter in range(4):
-        grad_tiles(wide_buf, narrow_buf, g_up, tiles * quarter // 4, tiles * (quarter + 1) // 4)
+        grad_tiles(wide_buf, g_out, up_width, g_up, tiles * quarter // 4, tiles * (quarter + 1) // 4)
         if quarter:
             norm_back(quarter - 1)
         add_steps(downs, *plan[1 + quarter])
@@ -899,8 +1003,6 @@
     add_steps(downs, *plan[5])
     for ring in ups:
         ring.begin()
-    fetch_gated = pltpu.make_async_copy(h_gated, narrow_buf, load_sem.at[1])
-    fetch_gated.start()
     for n, ring in enumerate(downs):
         c, way = n // 2, n % 2
         o_down[pl.ds(way * half, half), pl.ds(c * side, side)] = ring.finish()
@@ -926,7 +1028,7 @@
     fetch_out.wait()
     tiles = (narrow_buf.shape[1] // 256) * (width // 512)
     for quarter in range(4):
-        grad_tiles(narrow_buf, branch, g_out, tiles * quarter // 4, tiles * (quarter + 1) // 4)
+        grad_tiles(narrow_buf, branch, width, g_out, tiles * quarter // 4, tiles * (quarter + 1) // 4)
         add_steps(ups, *plan[2 + quarter])
     for ring in outs:
         ring.begin()
@@ -1049,7 +1151,7 @@
 
 
 def backward(
-    total, g_down, two, d_upper, part, seed, hidden, gain_two, gated, full_out, query, keys, values, gate, mixed,
+    total, g_down, two, d_upper, full_up, seed, hidden, gain_two, gated, full_out, query, keys, values, gate, mixed,
     tables, powers, ident_col, ident_row, gain_group,
 ):
     rows, width = seed.shape
@@ -1082,7 +1184,7 @@
             pltpu.VMEM((count, width), BF16),
             pltpu.VMEM((count, up_width), BF16),
             pltpu.VMEM(full_out.shape, BF16),
-            pltpu.VMEM((2, rows, width), BF16),
+            pltpu.VMEM((GROUP, rows, width), BF16),
             pltpu.VMEM((2, rows, width), BF16),
             pltpu.VMEM((rows, width), BF16),
             pltpu.VMEM((rows, width), BF16),
@@ -1097,7 +1199,7 @@
             pltpu.VMEM((2, rows, 2 * (QKH + VH)), BF16),
             pltpu.VMEM((3, r_up, up_width), BF16),
             pltpu.VMEM((3, r_up, up_width), BF16),
-            dma((12, total - 1)), dma((12, total - 1)), dma((6, 4)), dma((6, 4)), dma((3, 4)), dma((7,)),
+            dma((12, total - 1)), dma((12, total - 1)), dma((6, 4)), dma((6, 4)), dma((4,)), dma((9,)),
             dma((2, 5)), dma((2,)), dma((3,)), dma((3,)),
         ],
         compiler_params=pltpu.CompilerParams(
@@ -1105,17 +1207,17 @@
         ),
         name="backward_retention",
     )(
-        g_down, two, d_upper, part, seed, hidden, gain_two, gated, full_out, query, keys, values, gate, mixed,
+        g_down, two, d_upper, full_up, seed, hidden, gain_two, gated, full_out, query, keys, values, gate, mixed,
         *tables, powers, ident_col, ident_row, gain_group,
     )
 
 
 def final_kernel(
-    total, h_project, h_in, h_turned, part_down, hidden, d_hidden, tok, gains_all, ident_col, sums_two, d_group,
+    total, h_project, h_in, h_turned, h_active, h_down, hidden, d_hidden, tok, gains_all, ident_col, sums_two, d_group,
     o_in, output, d_tokens, o_vec, o_grp,
-    project, turned, first_term, term, arrived, win, part, own_part, core_in, out_x, in_x, stage, landed,
+    project, turned, first_term, term, arrived, win, part, active, wd, rows_f32, core_in, out_x, in_x, stage, landed,
     vec, grp, near_in, mid, far_in, far_grp,
-    load_sem, win_sem, ring_send, ring_recv, a2a_send, a2a_recv, row_send, row_recv, row_own,
+    load_sem, win_sem, ring_send, ring_recv, a2a_send, a2a_recv, row_send, row_recv,
     near_send, near_recv, far_send, far_recv,
 ):
     at = Place(total)
@@ -1133,8 +1235,6 @@
     fetch_project.start()
 
     def source(n, b):
-        if n == 0:
-            return part_down.at[b]
         return part.at[pl.ds(pl.multiple_of(b * rows, rows), rows), :]
 
     def row_copy(kind, n):
@@ -1145,14 +1245,7 @@
             )
         return remote(out_x.at[n], in_x.at[n], row_send.at[n, 2], row_recv.at[n, 2], at.peer(2))
 
-    def row_load(which):
-        return pltpu.make_async_copy(
-            source(0, flip(me, 2) if which == 0 else me), own_part.at[which], row_own.at[which]
-        )
-
     def own_rows(n, which, r):
-        if n == 0:
-            return own_part[which, pl.ds(r, step_rows), :]
         b = flip(me, 2) if which == 0 else me
         return part[pl.ds(pl.multiple_of(b * rows + r, step_rows), step_rows), :]
 
@@ -1178,17 +1271,22 @@
         return own_rows(n, 1, r).astype(F32) + core_in[n, 1, s, :].astype(F32) + in_x[n, s, :].astype(F32)
 
     def take_down():
+        fetch_hidden.wait()
         row_copy(1, 0).wait_recv()
         row_copy(2, 0).wait_recv()
 
         def some(r):
             s = pl.ds(r, step_rows)
             valid = jnp.where(ident_col[me, s, :] >= 0.0, 1.0, 0.0)
-            output[s, :] = ((hidden[s, :] + summed_rows(0, r)) * valid).astype(BF16)
+            output[s, :] = ((rows_f32[s, :] + summed_rows(0, r)) * valid).astype(BF16)
 
         by_rows(some)
+        row_copy(0, 0).wait_send()
+        row_copy(1, 0).wait_send()
+        fetch_d_hidden.start()
 
     def take_rows():
+        fetch_d_hidden.wait()
         row_copy(1, 1).wait_recv()
         row_copy(2, 1).wait_recv()
         vec[...] = jnp.zeros_like(vec)
@@ -1201,7 +1299,7 @@
             with_gain = e * gains_all[0:1, :]
             vec[0:1, :] += jnp.sum(e * normal, axis=0, keepdims=True)
             vec[1:2, :] += jnp.sum(e, axis=0, keepdims=True)
-            value = d_hidden[s, :] + scale * (
+            value = rows_f32[s, :] + scale * (
                 with_gain
                 - jnp.mean(with_gain, axis=-1, keepdims=True)
                 - normal * jnp.mean(with_gain * normal, axis=-1, keepdims=True)
@@ -1335,10 +1433,23 @@
         if n + 2 < columns:
             fetch_win(n + 2).start()
 
-    row_copy(0, 0).start()
-    row_copy(1, 0).start()
-    row_load(0).start()
-    row_load(1).start()
+    def down_rows(relation):
+        b = flip(me, relation)
+        r = pl.ds(pl.multiple_of(b * rows, rows), rows)
+
+        def column(n, carry):
+            c = pl.ds(pl.multiple_of(n * wide, wide), wide)
+            part[r, c] = dot(active[r, :], wd[:, c]).astype(BF16)
+            return carry
+
+        lax.fori_loop(0, width // wide, column, 0)
+
+    fetch_active = pltpu.make_async_copy(h_active, active, load_sem.at[2])
+    fetch_down = pltpu.make_async_copy(h_down, wd, load_sem.at[3])
+    fetch_hidden = pltpu.make_async_copy(hidden, rows_f32, load_sem.at[4])
+    fetch_d_hidden = pltpu.make_async_copy(d_hidden, rows_f32, load_sem.at[5])
+    for fetch in (fetch_active, fetch_down, fetch_hidden):
+        fetch.start()
     fetch_win(0).start()
     fetch_win(1).start()
     fetch_turned.wait()
@@ -1346,22 +1457,29 @@
     terms(0, first_term)
     for slot in order:
         hop(slot, 0, True).start()
-    row_load(0).wait()
+    fetch_active.wait()
+    fetch_down.wait()
+    down_rows(3)
+    row_copy(0, 0).start()
+    down_rows(2)
+    down_rows(1)
+    row_copy(1, 0).start()
+    down_rows(0)
     send_rows(0)
     plan = tick_plan(total, 6)
 
     def extra(number):
-        if number < 4:
-            for n in range(columns * number // 4, columns * (number + 1) // 4):
+        if number == 1:
+            take_down()
+        elif number in (2, 3):
+            for n in range(columns * (number - 2) // 2, columns * (number - 1) // 2):
                 row_tiles(n)
             if number == 3:
                 row_copy(0, 1).start()
                 row_copy(1, 1).start()
         elif number == 4:
             send_rows(1)
-            row_load(1).wait()
-            take_down()
-        else:
+        elif number == 5:
             take_rows()
             vectors_near()
 
@@ -1403,9 +1521,9 @@
     for n in range(1, total):
         for kind in (0, 1):
             distant(kind, n).wait_send()
-    for n in (0, 1):
-        for kind in (0, 1, 2):
-            row_copy(kind, n).wait_send()
+    row_copy(2, 0).wait_send()
+    for kind in (0, 1, 2):
+        row_copy(kind, 1).wait_send()
 
     def sent(step, carry):
         for slot in order:
@@ -1416,7 +1534,7 @@
 
 
 def final(
-    total, d_project, full_in, turned, down, hidden, d_hidden, tok, gain_one, valid, sums_two, d_group
+    total, d_project, full_in, turned, active, full_down, hidden, d_hidden, tok, gains, ident_col, sums_two, d_group
 ):
     rows, width = tok.shape
     count, wide = d_project.shape
@@ -1434,7 +1552,7 @@
     return pl.pallas_call(
         functools.partial(final_kernel, total),
         out_shape=[jax.ShapeDtypeStruct(s, d) for s, d in shapes],
-        in_specs=[hbm] * 4 + [vmem] * 7,
+        in_specs=[hbm] * 7 + [vmem] * 5,
         out_specs=[vmem] * 5,
         scratch_shapes=[
             pltpu.VMEM((count, wide), BF16),
@@ -1444,7 +1562,9 @@
             pltpu.VMEM((4, total - 1, block, wide), BF16),
             pltpu.VMEM((2, 256, wide), BF16),
             pltpu.VMEM((count, width), BF16),
-            pltpu.VMEM((2, rows, width), BF16),
+            pltpu.VMEM(active.shape, BF16),
+            pltpu.VMEM(full_down.shape, BF16),
+            pltpu.VMEM((rows, width), F32),
             pltpu.VMEM((2, 2, rows, width), BF16),
             pltpu.VMEM((2, rows, width), BF16),
             pltpu.VMEM((2, rows, width), BF16),
@@ -1456,14 +1576,14 @@
             pltpu.VMEM((8, width // GROUP), F32),
             pltpu.VMEM((total - 1, 8, 128), F32),
             pltpu.VMEM((total - 1, 8, 128), F32),
-            dma((2,)), dma((2, 2)), dma((4, total - 1)), dma((4, total - 1)), dma((3,)), dma((3,)),
-            dma((2, 3)), dma((2, 3)), dma((2,)), dma((3,)), dma((3,)), dma((2, total - 1)), dma((2, total - 1)),
+            dma((6,)), dma((2, 2)), dma((4, total - 1)), dma((4, total - 1)), dma((3,)), dma((3,)),
+            dma((2, 3)), dma((2, 3)), dma((3,)), dma((3,)), dma((2, total - 1)), dma((2, total - 1)),
         ],
         compiler_params=pltpu.CompilerParams(
             collective_id=3, has_side_effects=True, vmem_limit_bytes=63 * MIB
         ),
         name="final_sums",
-    )(d_project, full_in, turned, down, hidden, d_hidden, tok, gain_one, valid, sums_two, d_group)
+    )(d_project, full_in, turned, active, full_down, hidden, d_hidden, tok, gains, ident_col, sums_two, d_group)
 
 
 def mean(values):
@@ -1502,7 +1622,8 @@
     rates = jnp.broadcast_to(rates[:, None, None], (heads, 1, rows))
     entries = jnp.stack([seq_lens, seq_owner, seq_offset])
     (
-        full_in, full_up, full_out, full_down, seed, turned, query, keys, values, gate, mixed, gated, hidden, two,
+        full_in, full_up, full_out, full_down, _, turned, query, keys, values, gate, mixed, gated, active, d_upper,
+        g_down, hidden, two,
         own_seed, cosine, sine, growth, shrink, powers, ident_col, ident_row, gains, gain_group,
     ) = forward(
         total, w_in, w_up, w_out, w_down, tokens, cotangent, pack, rates, entries[:, :, None], entries[:, None, :]
@@ -1512,22 +1633,13 @@
     full_out = full_out.reshape(-1, width)
     full_down = full_down.reshape(-1, width)
     two = two.reshape(count, width)
-    seed = seed.reshape(count, width)
-    upper = dot(two, full_up)
-    cdf = 0.5 * (1.0 + lax.erf(upper * (0.5**0.5)))
-    active = (upper * cdf).astype(BF16)
-    down = dot(active, full_down).astype(BF16).reshape(GROUP, rows, width)
-
-    slope = cdf + upper * jnp.exp(-0.5 * upper * upper) * (2.0 * jnp.pi) ** -0.5
-    d_upper = (dot_back(seed, full_down) * slope).astype(BF16)
-    d_two = dot_back(d_upper, full_up).astype(BF16).reshape(GROUP, rows, width)
-    g_down = dot_rows(active, seed).astype(BF16)
     grad_down, grad_up, grad_out, d_hidden, _, sums_two, d_group, d_project = backward(
-        total, g_down, two, d_upper, d_two, own_seed, hidden, gains, gated, full_out, query, keys, values,
-        gate, mixed, tables, powers, ident_col, ident_row, gain_group,
+        total, g_down.reshape(-1, width), two, d_upper, full_up, own_seed, hidden, gains, gated, full_out, query,
+        keys, values, gate, mixed, tables, powers, ident_col, ident_row, gain_group,
     )
     grad_in, output, d_tokens, vec_one, vec_two = final(
-        total, d_project, full_in, turned, down, hidden, d_hidden, tokens, gains, ident_col, sums_two, d_group
+        total, d_project, full_in, turned, active, full_down, hidden, d_hidden, tokens, gains, ident_col, sums_two,
+        d_group,
     )
     grads = lax.dynamic_slice(vec_one, (0, lax.rem(inner * small, 128)), (4, small))
     grad_group = lax.dynamic_slice(vec_two, (0, lax.rem(inner * large, 128)), (1, large))[0]

time: 617 us -> 597 us (0.968)
  matrix products: 32.5 us -> 0 us
  Pallas kernels: 558 us -> 570 us
    dot_general x5 -> x0, matrix products: 32.5 us -> none  [the longest x2 14.3 us: dot(): return jnp.dot(left, right, preferred_element_type=F32)]
    pallas_call x1, Pallas kernels: 131 us -> 139 us  [backward(): pl.pallas_call(functools.partial(backward_kernel, total), out_shape=[jax....]
where the time goes in v5:
time: 597 us; the launch traced here: 588 us
  Pallas kernels  570 us (95%)
  local copies, waits for them, and re-layouts  14.2 us (2%)
    pallas_call x1, Pallas kernels, forward(): pl.pallas_call(functools.partial(forward_kernel, total), out_shape=[jax.S...  281 us
    pallas_call x1, Pallas kernels, final(): pl.pallas_call(functools.partial(final_kernel, total), out_shape=[jax.Sha...  150 us
    pallas_call x1, Pallas kernels, backward(): pl.pallas_call(functools.partial(backward_kernel, total), out_shape=[jax....  139 us

profile of v5, /device:TPU:1, one launch (start us, length us, event | category | flops | bytes accessed | tf_op | source)
XLA Modules:
  0.0 587.6 jit_solution(2674267191094089612)
XLA Ops:
  0.7 0.7 bitcast_convert_fusion
  1.3 0.6 broadcast_in_dim.24.rates
  2.0 0.7 maximum_convert_fusion
  2.7 0.3 dynamic_update_slice.6
  3.1 0.0 copy-start.4
  3.1 0.7 pad_add_fusion
  3.8 0.6 broadcast_in_dim.26.seq_rows
  4.3 0.8 copy.26.seq_cols
  5.1 0.0 copy-done.4
  5.1 281.1 %forward_retention.1 = (bf16[2,2048,1536]{2,1,0:T(8,128)(2,1)}, bf16[4,8,64,1024]{3,2,1,0:T(8,128)(2,1)}, bf16[8,128,2048]{2,1,0:T(8,128)(2,1)}, bf16[8,128,2048...) custom-call(bf16[64,12288]{1,0:T(8,128)(2,1)} %w_in.1, ...), custom_call_target="tpu_custom_call" | custom-call | tf_op jit(solution)/shard_map/forward_retention/pallas_call | solution.py:760
  286.3 139.3 %backward_retention.1 = (f32[128,2048]{1,0:T(8,128)}, f32[64,4096]{1,0:T(8,128)}, f32[128,2048]{1,0:T(8,128)}, f32[256,2048]{1,0:T(8,128)}, bf16[4,256,2048]{2,1...) custom-call(bf16[1024,2048]{1,0:T(8,128)(2,1)} %bitcast.30, ...), custom_call_target="tpu_custom_call" | custom-call | tf_op jit(solution)/shard_map/backward_retention/pallas_call | solution.py:1175
  425.6 149.7 %final_sums.1 = (f32[64,12288]{1,0:T(8,128)}, bf16[256,2048]{1,0:T(8,128)(2,1)}, bf16[256,2048]{1,0:T(8,128)(2,1)}, f32[8,128]{1,0:T(8,128)}, f32[8,128]{1,0:T(8,128)}) custom-call(bf16[1024,3072]{1,0:T(8,128)(2,1)} %get-tuple-element.71.h_project, bf16[2,2048,1536]{2,1,0:T(8,128)(2,1)} %get-tuple-element.72.h_in, ...), custom_call_target="tpu_custom_call" | custom-call | tf_op jit(solution)/shard_map/final_sums/pallas_call | solution.py:1552
  575.3 0.0 copy-start
  575.3 1.3 slice_bitcast_fusion.2
  576.6 0.8 constant_dynamic-slice_fusion
  577.4 0.5 slice_bitcast_fusion
  577.9 2.3 copy.35
  580.2 0.0 copy-start.3
  580.2 2.4 copy.36
  582.6 0.0 copy-done
  582.6 0.0 copy-start.2
  582.6 0.0 copy-start.1
  582.6 1.7 copy.37
  584.3 0.0 copy-done.3
  584.3 1.0 copy.38
  585.3 0.0 copy-done.2
  585.3 1.0 copy.39
  586.2 0.0 copy-done.1
  586.2 1.0 copy.40
  (3 shorter events, 0.0 us)
Async XLA Ops:
  3.1 2.0 copy-start.4
  575.3 7.3 %copy-start = (f32[64,12288]{1,0:T(8,128)S(1)}, f32[64,12288]{1,0:T(8,128)}, u32[]{:S(2)}) copy-start(f32[64,12288]{1,0:T(8,128)} %get-tuple-element.106) | copy-start | bytes 9437188
  580.2 4.1 copy-start.3
  582.6 2.6 copy-start.2
  582.6 3.6 copy-start.1

commit v6 on v5

--- a/solution.py
+++ b/solution.py
@@ -202,13 +202,14 @@
 
 
 def forward_kernel(
-    total, w_in, w_up, w_out, w_down, tok, cot, pack, rates, seq_cols, seq_rows, curves,
+    total, w_in, w_up, w_out, w_down, h_tok, h_cot, pack, rates, seq_cols, seq_rows, curves,
     full_in, full_up, full_out, full_down, full_seed, o_turned, o_query, o_keys, o_values, o_gate, o_mixed,
-    o_gated, o_active, o_upper, o_g_down, hidden, full_two, own_seed, cosine, sine, growth, shrink, powers, ident_col, ident_row, gains,
-    gain_group,
+    o_gated, o_active, o_upper, o_g_down, to_hidden, full_two, to_seed, to_cosine, to_sine, to_growth, to_shrink,
+    to_powers, ident_col, ident_row, gains, gain_group,
+    hidden, own_seed, cosine, sine, growth, shrink, powers, tok, cot,
     win, part, x, query, keys, values, gate, mixed, gated, wo, core_in, out_x, in_x, low, full_vec,
     win_up, wd, ring_send, ring_recv, own_sem, load_sem, fetch_sem, store_sem, row_send, row_recv, row_own,
-    swap_send, swap_recv, swap_own, vec_send, vec_recv,
+    swap_send, swap_recv, swap_own, vec_send, vec_recv, early_sem,
 ):
     at = Place(total)
     me, inner = at.group, at.inner
@@ -240,7 +241,7 @@
         elif slot == last + 1:
             src, dst = pack, full_vec.at[inner, me]
         elif slot == last + 2:
-            src, dst = tok, part.at[me]
+            src, dst = h_tok, part.at[me]
         else:
             src, dst = own_seed, full_seed.at[me]
         if relation == 0:
@@ -266,6 +267,20 @@
     for slot in (last + 2, last):
         for relation in (1, 0, 2, 3):
             swap(relation, slot).start()
+
+    fetch_cot = pltpu.make_async_copy(h_cot, cot, early_sem.at[0])
+    fetch_tok = pltpu.make_async_copy(h_tok, tok, early_sem.at[1])
+    fetch_cot.start()
+    fetch_tok.start()
+    early_stores = [
+        pltpu.make_async_copy(src, dst, early_sem.at[2 + n])
+        for n, (src, dst) in enumerate(
+            (
+                (own_seed, to_seed), (cosine, to_cosine), (sine, to_sine), (growth, to_growth),
+                (shrink, to_shrink), (powers, to_powers), (hidden, to_hidden),
+            )
+        )
+    ]
 
     def in_ring(h, relation):
         def place(which):
@@ -314,7 +329,9 @@
         own_seed[s, :] = (cot[s, :].astype(F32) * valid).astype(BF16)
         return carry
 
+    fetch_cot.wait()
     lax.fori_loop(0, rows // step_rows, seed_rows, 0)
+    early_stores[0].start()
 
     for relation in range(4):
         arrived(relation, last + 1)
@@ -381,6 +398,8 @@
             lift = places * (1.0 / 512.0) * curves[1:2, :]
             growth[r, :] = jnp.exp(lift)
             shrink[r, :] = jnp.exp(-lift)
+        for store_one in early_stores[1:6]:
+            store_one.start()
 
     def norm_buffer(relation):
         b = flip(me, relation)
@@ -413,11 +432,11 @@
             await_head(h, relation)
             ins[h][relation].begin()
     outs, ups, downs = weight_rings(
-        at, w_out, w_down, full_up, full_out, full_down, ring_send, ring_recv
+        at, w_out, w_down, full_up, full_out, wd, ring_send, ring_recv
     )
     own_copies = [
         pltpu.make_async_copy(w_out, full_out.at[inner], own_sem.at[0]),
-        pltpu.make_async_copy(w_down, full_down.at[inner], own_sem.at[1]),
+        pltpu.make_async_copy(w_down, wd.at[inner], own_sem.at[1]),
     ]
     for copy in own_copies:
         copy.start()
@@ -572,6 +591,7 @@
     run_steps(ups, *plan[1])
     for copy_out in stores:
         copy_out.wait()
+    fetch_tok.wait()
     wait_sent([ring for rings in ins for ring in rings], total)
 
     def turn(n, carry):
@@ -604,6 +624,7 @@
         store(c).start()
         if c:
             run_steps(ups, *plan[2 + c])
+    early_stores[6].start()
     for ring in downs:
         ring.begin()
     lax.fori_loop(blocks // 2, blocks, turn, 0)
@@ -682,9 +703,8 @@
     own_copies[1].wait()
     for ring in downs:
         ring.finish()
-    fetch = pltpu.make_async_copy(full_down, wd, load_sem.at[0])
-    fetch.start()
-    fetch.wait()
+    store_full = pltpu.make_async_copy(wd, full_down, load_sem.at[0])
+    store_full.start()
 
     def d_upper_tile(n, carry):
         h, j = n // 4, lax.rem(n, 4)
@@ -695,13 +715,13 @@
         values[h, r, c] = (dot_back(x[r, :], piece) * gate[h, r, c]).astype(BF16)
         return carry
 
-    lax.fori_loop(0, 4 * heads, d_upper_tile, 0)
-    last_stores = [store_active, store_down] + [
-        pltpu.make_async_copy(values.at[h], o_upper.at[:, pl.ds(h * VH, VH)], store_sem.at[0, 2 + h])
-        for h in range(heads)
-    ]
-    for copy_out in last_stores[2:]:
-        copy_out.start()
+    last_stores = [store_active, store_down, store_full]
+    for h in range(heads):
+        lax.fori_loop(4 * h, 4 * (h + 1), d_upper_tile, 0)
+        last_stores.append(
+            pltpu.make_async_copy(values.at[h], o_upper.at[:, pl.ds(h * VH, VH)], store_sem.at[0, 2 + h])
+        )
+        last_stores[-1].start()
     wait_sent(outs + downs + ups, total)
     for relation in (1, 2, 3):
         for slot in range(last + 4):
@@ -709,7 +729,7 @@
     for n in range(1, total):
         spread(n).wait_send()
     store_turned.wait()
-    for copy_out in last_stores:
+    for copy_out in last_stores + early_stores:
         copy_out.wait()
 
 
@@ -760,9 +780,13 @@
     return pl.pallas_call(
         functools.partial(forward_kernel, total),
         out_shape=[jax.ShapeDtypeStruct(s, d) for s, d in shapes],
-        in_specs=[hbm] * 4 + [vmem] * 7,
-        out_specs=[hbm] * len(in_hbm) + [vmem, hbm] + [vmem] * len(in_vmem),
+        in_specs=[hbm] * 6 + [vmem] * 5,
+        out_specs=[hbm] * (len(in_hbm) + 8) + [vmem] * 4,
         scratch_shapes=[
+            pltpu.VMEM((rows, width), F32),
+            *[pltpu.VMEM(s, d) for s, d in in_vmem[:6]],
+            pltpu.VMEM((rows, width), BF16),
+            pltpu.VMEM((rows, width), BF16),
             pltpu.VMEM((heads, width, head_width), BF16),
             pltpu.VMEM((GROUP, rows, width), BF16),
             pltpu.VMEM((count, width), BF16),
@@ -777,7 +801,7 @@
             pltpu.VMEM((total,) + w_down.shape, BF16),
             dma((20, total - 1)), dma((20, total - 1)), dma((2,)), dma((2,)), dma((2 * GROUP,)),
             dma((heads, 7)), dma((6, 4)), dma((6, 4)), dma((4,)),
-            dma((3, 12)), dma((3, 12)), dma((12,)), dma((total - 1,)), dma((total - 1,)),
+            dma((3, 12)), dma((3, 12)), dma((12,)), dma((total - 1,)), dma((total - 1,)), dma((9,)),
         ],
         compiler_params=pltpu.CompilerParams(
             collective_id=1, has_side_effects=True, vmem_limit_bytes=63 * MIB
@@ -787,12 +811,13 @@
 
 
 class Adding:
-    def __init__(self, at, way, term, arrived, sends, recvs):
+    def __init__(self, at, way, term, arrived, sends, recvs, origin=None):
         self.at, self.way, self.term, self.arrived = at, way, term, arrived
+        self.origin = term if origin is None else origin
         self.sends, self.recvs = sends, recvs
 
     def hop(self, step, first=False):
-        src = self.term(self.at.behind(self.way, 1)) if first else self.arrived.at[step - 1]
+        src = self.origin(self.at.behind(self.way, 1)) if first else self.arrived.at[step - 1]
         return remote(
             src, self.arrived.at[step], self.sends.at[step], self.recvs.at[step], self.at.neighbour(self.way)
         )
@@ -822,12 +847,12 @@
 
 
 def backward_kernel(
-    total, g_down, two, d_upper, h_up, seed, hidden, gains_all, h_gated, h_out, h_query, h_keys, h_values, h_gate,
-    h_mixed, cosine, sine, growth, shrink, powers, ident_col, ident_row, gain_group,
-    o_down, o_up, o_out, d_hidden, full_branch, sums, o_group, o_project,
-    g_up, g_out, arrived, wide_buf, narrow_buf, wo, part, core_in, out_x, in_x, low,
+    total, h_g_down, two, d_upper, h_up, h_seed, h_hidden, gains_all, h_gated, h_out, h_query, h_keys, h_values,
+    h_gate, h_mixed, h_cosine, h_sine, h_growth, h_shrink, h_powers, ident_col, ident_row, gain_group,
+    to_down, to_up, to_out, to_hidden, full_branch, sums, o_group, o_project,
+    g_down, seed, hidden, cosine, sine, growth, shrink, powers, o_down, o_up, o_out, d_hidden, g_up, g_out, arrived, wide_buf, narrow_buf, wo, part, core_in, out_x, in_x, low,
     query, keys, values, gate, mixed, back, d_mixed, staged, stage, landed,
-    ring_send, ring_recv, row_send, row_recv, row_own, load_sem, unit_sem, out_sem, a2a_send, a2a_recv,
+    ring_send, ring_recv, row_send, row_recv, row_own, load_sem, late_sem, unit_sem, out_sem, a2a_send, a2a_recv,
 ):
     at = Place(total)
     me = at.group
@@ -840,20 +865,24 @@
     up_width = o_up.shape[1] // GROUP
     half, side = r_out // 2, width // 2
 
-    def halves(source, base):
+    def halves(source, base, origin=None):
+        def chunk_of(ref, way, c):
+            return lambda which: ref.at[
+                pl.ds(pl.multiple_of(which * r_out + way * half, half), half), pl.ds(c * side, side)
+            ]
+
         return [
             Adding(
                 at, way,
-                lambda which, way=way, c=c: source.at[
-                    pl.ds(pl.multiple_of(which * r_out + way * half, half), half), pl.ds(c * side, side)
-                ],
+                chunk_of(source, way, c),
                 arrived.at[base + 2 * c + way], ring_send.at[base + 2 * c + way], ring_recv.at[base + 2 * c + way],
+                None if origin is None else chunk_of(origin, way, c),
             )
             for c in (0, 1)
             for way in (0, 1)
         ]
 
-    downs, outs, ups = halves(g_down, 0), halves(g_out, 8), []
+    downs, outs, ups = halves(g_down, 0, h_g_down), halves(g_out, 8), []
     for order in (0, 1):
         for way in (0, 1):
             relation = RELATIONS[way][order]
@@ -904,7 +933,21 @@
     fetch_two = pltpu.make_async_copy(two, wide_buf, load_sem.at[0])
     fetch_gated = pltpu.make_async_copy(h_gated, narrow_buf, load_sem.at[8])
     fetch_out = pltpu.make_async_copy(h_out, wo, load_sem.at[2])
-    for fetch in (fetch_upper, fetch_up, fetch_two, fetch_gated, fetch_out):
+    fetch_rows = [
+        pltpu.make_async_copy(src, dst, late_sem.at[n])
+        for n, (src, dst) in enumerate(((h_g_down, g_down), (h_seed, seed), (h_hidden, hidden)))
+    ]
+    fetch_tables = [
+        pltpu.make_async_copy(src, dst, late_sem.at[3 + n])
+        for n, (src, dst) in enumerate(
+            ((h_cosine, cosine), (h_sine, sine), (h_growth, growth), (h_shrink, shrink), (h_powers, powers))
+        )
+    ]
+    stores = [
+        pltpu.make_async_copy(src, dst, late_sem.at[8 + n])
+        for n, (src, dst) in enumerate(((o_down, to_down), (o_up, to_up), (o_out, to_out), (d_hidden, to_hidden)))
+    ]
+    for fetch in (fetch_upper, fetch_up, *fetch_rows, fetch_two, fetch_gated, fetch_out, *fetch_tables):
         fetch.start()
 
     def unit_loads(unit, slot):
@@ -973,6 +1016,8 @@
     d_two(2)
     for c in range(chunks):
         send_sums(c)
+    for fetch in fetch_rows:
+        fetch.wait()
     add_steps(downs, *plan[0])
     d_two(1)
     for c in range(chunks):
@@ -1006,6 +1051,8 @@
     for n, ring in enumerate(downs):
         c, way = n // 2, n % 2
         o_down[pl.ds(way * half, half), pl.ds(c * side, side)] = ring.finish()
+    stores[0].start()
+    stores[3].start()
     for c in range(chunks):
         copy(3, c).wait_recv()
         copy(5, c).start()
@@ -1027,26 +1074,11 @@
     fetch_gated.wait()
     fetch_out.wait()
     tiles = (narrow_buf.shape[1] // 256) * (width // 512)
-    for quarter in range(4):
-        grad_tiles(narrow_buf, branch, width, g_out, tiles * quarter // 4, tiles * (quarter + 1) // 4)
-        add_steps(ups, *plan[2 + quarter])
-    for ring in outs:
-        ring.begin()
-
-    def sent_across(relation):
-        return remote(
-            stage.at[relation - 1], landed.at[relation - 1],
-            a2a_send.at[relation - 1], a2a_recv.at[relation - 1], at.peer(relation),
-        )
-
-    for n, ring in enumerate(ups):
-        relation = RELATIONS[n % 2][n // 2]
-        value = ring.finish()
-        if relation == 0:
-            o_up[:, pl.ds(pl.multiple_of(me * up_width, 128), up_width)] = value
-        else:
-            stage[relation - 1] = value.astype(BF16)
-            sent_across(relation).start()
+    for part_of in range(2):
+        grad_tiles(narrow_buf, branch, width, g_out, tiles * part_of // 2, tiles * (part_of + 1) // 2)
+        add_steps(ups, *plan[2 + part_of])
+    for fetch in fetch_tables:
+        fetch.wait()
 
     units = heads * GROUP
 
@@ -1066,7 +1098,7 @@
             [(first * c + second * s) * scale, (second * c - first * s) * scale], axis=1
         )
 
-    def unit_body(unit, carry):
+    def unit_body(unit):
         slot = lax.rem(unit, 2)
         h, b = unit // GROUP, lax.rem(unit, GROUP)
         r = pl.ds(pl.multiple_of(b * rows, rows), rows)
@@ -1119,26 +1151,58 @@
             for fetch in unit_loads(unit + 2, slot):
                 fetch.start()
 
-        steps = total - 2
-        add_steps(outs, 1 + (steps * unit) // units, 1 + (steps * (unit + 1)) // units)
+    early = 2
+
+    def with_ups(unit, carry):
+        unit_body(unit)
+        (low_a, high_a), (low_b, high_b) = plan[4], plan[5]
+        add_steps(ups, low_a + unit * (low_b - low_a), high_a + unit * (high_b - high_a))
         return carry
 
-    lax.fori_loop(0, units, unit_body, 0)
+    def with_outs(unit, carry):
+        unit_body(unit)
+        steps, number = total - 2, unit - early
+        add_steps(outs, 1 + (steps * number) // (units - early), 1 + (steps * (number + 1)) // (units - early))
+        return carry
+
+    lax.fori_loop(0, early, with_ups, 0)
+    for ring in outs:
+        ring.begin()
+
+    def sent_across(relation):
+        return remote(
+            stage.at[relation - 1], landed.at[relation - 1],
+            a2a_send.at[relation - 1], a2a_recv.at[relation - 1], at.peer(relation),
+        )
+
+    for n, ring in enumerate(ups):
+        relation = RELATIONS[n % 2][n // 2]
+        value = ring.finish()
+        if relation == 0:
+            o_up[:, pl.ds(pl.multiple_of(me * up_width, 128), up_width)] = value
+        else:
+            stage[relation - 1] = value.astype(BF16)
+            sent_across(relation).start()
+    lax.fori_loop(early, units, with_outs, 0)
     for relation in (1, 2, 3):
         sent_across(relation).wait_recv()
         o_up[:, pl.ds(pl.multiple_of(flip(me, relation) * up_width, 128), up_width)] = landed[
             relation - 1
         ].astype(F32)
         sent_across(relation).wait_send()
+    stores[1].start()
     for slot in (0, 1):
         unit_stores(jnp.int32(units - 2 + slot), slot).wait()
     for n, ring in enumerate(outs):
         c, way = n // 2, n % 2
         o_out[pl.ds(way * half, half), pl.ds(c * side, side)] = ring.finish()
+    stores[2].start()
     for c in range(chunks):
         for kind in range(6):
             copy(kind, c).wait_send()
     wait_added(downs + ups + outs, total)
+    for store_one in stores:
+        store_one.wait()
 
 
 def add_steps(rings, start, stop):
@@ -1175,9 +1239,14 @@
     return pl.pallas_call(
         functools.partial(backward_kernel, total),
         out_shape=[jax.ShapeDtypeStruct(s, d) for s, d in shapes],
-        in_specs=[vmem, hbm, hbm, hbm, vmem, vmem, vmem] + [hbm] * 7 + [vmem] * 8,
-        out_specs=[vmem] * 4 + [hbm, vmem, vmem, hbm],
+        in_specs=[hbm] * 6 + [vmem] + [hbm] * 12 + [vmem] * 3,
+        out_specs=[hbm] * 5 + [vmem, vmem, hbm],
         scratch_shapes=[
+            pltpu.VMEM(g_down.shape, BF16),
+            pltpu.VMEM(seed.shape, BF16),
+            pltpu.VMEM(hidden.shape, F32),
+            *[pltpu.VMEM(v.shape, F32) for v in (*tables, powers)],
+            *[pltpu.VMEM(s, d) for s, d in shapes[:4]],
             pltpu.VMEM((width, up_width), BF16),
             pltpu.VMEM(g_down.shape, BF16),
             pltpu.VMEM((12, total - 1, half, side), BF16),
@@ -1199,7 +1268,7 @@
             pltpu.VMEM((2, rows, 2 * (QKH + VH)), BF16),
             pltpu.VMEM((3, r_up, up_width), BF16),
             pltpu.VMEM((3, r_up, up_width), BF16),
-            dma((12, total - 1)), dma((12, total - 1)), dma((6, 4)), dma((6, 4)), dma((4,)), dma((9,)),
+            dma((12, total - 1)), dma((12, total - 1)), dma((6, 4)), dma((6, 4)), dma((4,)), dma((9,)), dma((12,)),
             dma((2, 5)), dma((2,)), dma((3,)), dma((3,)),
         ],
         compiler_params=pltpu.CompilerParams(
@@ -1214,10 +1283,10 @@
 
 def final_kernel(
     total, h_project, h_in, h_turned, h_active, h_down, hidden, d_hidden, tok, gains_all, ident_col, sums_two, d_group,
-    o_in, output, d_tokens, o_vec, o_grp,
-    project, turned, first_term, term, arrived, win, part, active, wd, rows_f32, core_in, out_x, in_x, stage, landed,
+    o_in, o_output, o_tokens, o_vec, o_grp,
+    output, d_tokens, full_rows, project, turned, term, arrived, win, part, active, wd, rows_f32, core_in, out_x, in_x, stage, landed,
     vec, grp, near_in, mid, far_in, far_grp,
-    load_sem, win_sem, ring_send, ring_recv, a2a_send, a2a_recv, row_send, row_recv,
+    load_sem, win_sem, ring_send, ring_recv, a2a_send, a2a_recv, row_send, row_recv, in_sem, piece_sem,
     near_send, near_recv, far_send, far_recv,
 ):
     at = Place(total)
@@ -1229,10 +1298,19 @@
     block = o_in.shape[0]
     step_rows = 32
 
+    store_output = pltpu.make_async_copy(output, o_output, load_sem.at[6])
+    store_tokens = pltpu.make_async_copy(d_tokens, o_tokens, load_sem.at[7])
     fetch_turned = pltpu.make_async_copy(h_turned, turned, load_sem.at[0])
-    fetch_project = pltpu.make_async_copy(h_project, project, load_sem.at[1])
+    wide = 512
+    fetch_project = [
+        pltpu.make_async_copy(
+            h_project.at[:, pl.ds(n * wide, wide)], project.at[:, pl.ds(n * wide, wide)], piece_sem.at[n]
+        )
+        for n in range(project.shape[1] // wide)
+    ]
     fetch_turned.start()
-    fetch_project.start()
+    for fetch in fetch_project:
+        fetch.start()
 
     def source(n, b):
         return part.at[pl.ds(pl.multiple_of(b * rows, rows), rows), :]
@@ -1266,24 +1344,33 @@
         by_rows(some)
         row_copy(2, n).start()
 
+    def hold_down():
+        fetch_hidden.wait()
+        row_copy(1, 0).wait_recv()
+
+        def some(r):
+            s = pl.ds(r, step_rows)
+            rows_f32[s, :] += own_rows(0, 1, r).astype(F32) + core_in[0, 1, s, :].astype(F32)
+
+        by_rows(some)
+        row_copy(0, 0).wait_send()
+        row_copy(1, 0).wait_send()
+
     def summed_rows(n, r):
         s = pl.ds(r, step_rows)
         return own_rows(n, 1, r).astype(F32) + core_in[n, 1, s, :].astype(F32) + in_x[n, s, :].astype(F32)
 
     def take_down():
-        fetch_hidden.wait()
-        row_copy(1, 0).wait_recv()
         row_copy(2, 0).wait_recv()
 
         def some(r):
             s = pl.ds(r, step_rows)
             valid = jnp.where(ident_col[me, s, :] >= 0.0, 1.0, 0.0)
-            output[s, :] = ((rows_f32[s, :] + summed_rows(0, r)) * valid).astype(BF16)
+            output[s, :] = ((rows_f32[s, :] + in_x[0, s, :].astype(F32)) * valid).astype(BF16)
 
         by_rows(some)
-        row_copy(0, 0).wait_send()
-        row_copy(1, 0).wait_send()
         fetch_d_hidden.start()
+        store_output.start()
 
     def take_rows():
         fetch_d_hidden.wait()
@@ -1307,6 +1394,7 @@
             d_tokens[s, :] = value.astype(BF16)
 
         by_rows(some)
+        store_tokens.start()
 
     quarter = width // GROUP
     small = quarter // total
@@ -1354,47 +1442,75 @@
         o_vec[...] = mid[:, tile_of(inner, small)] + jnp.sum(far_in[...], axis=0)
         o_grp[...] = grp[:, tile_of(inner, large)] + jnp.sum(far_grp[...], axis=0)
 
-    wide = 512
-
-    def terms(step, out):
+
+    def terms(step, far_at, near_at, arriving=False):
+        lefts = []
         for way in (0, 1):
             which = at.behind(way, step + 1)
-            left = jnp.concatenate(
-                [
-                    turned[
-                        pl.ds(pl.multiple_of((flip(me, relation) * total + which) * block, block), block), :
-                    ]
-                    for relation in RELATIONS[way]
-                ],
-                axis=0,
+            lefts.append(
+                jnp.concatenate(
+                    [
+                        turned[
+                            pl.ds(pl.multiple_of((flip(me, relation) * total + which) * block, block), block), :
+                        ]
+                        for relation in RELATIONS[way]
+                    ],
+                    axis=0,
+                )
             )
 
-            def tile(n, carry, left=left, way=way):
-                c = pl.ds(pl.multiple_of(n * wide, wide), wide)
-                value = dot(left, project[:, c]).astype(BF16)
-                out[2 * way, :, c] = value[:block]
-                out[2 * way + 1, :, c] = value[block:]
+        def tile(n, way):
+            c = pl.ds(pl.multiple_of(n * wide, wide), wide)
+            value = dot(lefts[way], project[:, c]).astype(BF16)
+            term[far_at + way, :, c] = value[:block]
+            term[near_at + way, :, c] = value[block:]
+
+        if arriving:
+            for n, fetch in enumerate(fetch_project):
+                fetch.wait()
+                tile(n, 0)
+                tile(n, 1)
+            return
+        for way in (0, 1):
+
+            def some(n, carry, way=way):
+                tile(n, way)
                 return carry
 
-            lax.fori_loop(0, project.shape[1] // wide, tile, 0)
+            lax.fori_loop(0, project.shape[1] // wide, some, 0)
+
+    far_slots, near_slots = (0, 2), (1, 3)
+
+    def near_place(step):
+        return 6 + 2 * lax.rem(step, 2)
 
     def hop(slot, step, first=False):
-        src = first_term.at[slot] if first else arrived.at[slot, step - 1]
+        src = term.at[2 * (slot % 2) + slot // 2] if first else arrived.at[slot, step - 1]
         return remote(
             src, arrived.at[slot, step], ring_send.at[slot, step], ring_recv.at[slot, step],
             at.neighbour(slot // 2),
         )
 
-    order = (0, 2, 1, 3)
+    def sum_into(out, slot, step, base):
+        hop(slot, step, True).wait_recv()
+
+        def some(n, carry):
+            c = pl.ds(pl.multiple_of(n * wide, wide), wide)
+            value = arrived[slot, step, :, c].astype(F32) + term[base + slot // 2, :, c].astype(F32)
+            out[:, c] = value.astype(BF16)
+            return carry
+
+        lax.fori_loop(0, project.shape[1] // wide, some, 0)
+
+    def send_on(slots, step, base):
+        for slot in slots:
+            sum_into(arrived.at[slot, step - 1], slot, step - 1, base)
+            hop(slot, step).start()
 
     def onward(step, carry):
-        terms(step, term)
-        for slot in order:
-            hop(slot, step - 1, True).wait_recv()
-            arrived[slot, step - 1] = (
-                arrived[slot, step - 1].astype(F32) + term[slot].astype(F32)
-            ).astype(BF16)
-            hop(slot, step).start()
+        terms(step, 4, near_place(step))
+        send_on(far_slots, step, 4)
+        send_on(near_slots, step - 1, near_place(step - 1))
         return carry
 
     parts = h_in.shape[0]
@@ -1453,48 +1569,64 @@
     fetch_win(0).start()
     fetch_win(1).start()
     fetch_turned.wait()
-    fetch_project.wait()
-    terms(0, first_term)
-    for slot in order:
+    terms(0, 0, 2, True)
+    for slot in far_slots:
         hop(slot, 0, True).start()
     fetch_active.wait()
     fetch_down.wait()
     down_rows(3)
     row_copy(0, 0).start()
+    for slot in near_slots:
+        hop(slot, 0, True).start()
     down_rows(2)
     down_rows(1)
     row_copy(1, 0).start()
     down_rows(0)
     send_rows(0)
+    hold_down()
     plan = tick_plan(total, 6)
 
     def extra(number):
-        if number == 1:
-            take_down()
-        elif number in (2, 3):
-            for n in range(columns * (number - 2) // 2, columns * (number - 1) // 2):
+        if number < 3:
+            for n in range(columns * number // 3, columns * (number + 1) // 3):
                 row_tiles(n)
-            if number == 3:
+            if number == 2:
                 row_copy(0, 1).start()
                 row_copy(1, 1).start()
-        elif number == 4:
+        elif number == 3:
             send_rows(1)
+            take_down()
         elif number == 5:
             take_rows()
             vectors_near()
 
+    terms(1, 4, near_place(1))
+    send_on(far_slots, 1, 4)
     for number in range(6):
         extra(number)
-        lax.fori_loop(*plan[number], onward, 0)
-    vectors_far()
-    terms(total - 1, term)
+        lax.fori_loop(max(plan[number][0], 2), plan[number][1], onward, 0)
+    terms(total - 1, 4, near_place(total - 1))
     pieces = column_pieces()
 
-    def place(other, value):
+    def place(relation, columns_of):
+        other = flip(me, relation)
         for base, stride, h, off, size in pieces:
             start = pl.multiple_of(base + other * stride, 128)
             off = h * part_width + off
-            o_in[:, pl.ds(start, size)] = value[:, off : off + size]
+            full_rows[:, pl.ds(start, size)] = columns_of(off, size)
+        for copy in stored(relation):
+            copy.start()
+
+    def stored(relation):
+        other = flip(me, relation)
+        return [
+            pltpu.make_async_copy(
+                full_rows.at[:, pl.ds(pl.multiple_of(base + other * stride, 128), size)],
+                o_in.at[:, pl.ds(pl.multiple_of(base + other * stride, 128), size)],
+                in_sem.at[relation, n],
+            )
+            for n, (base, stride, h, off, size) in enumerate(pieces)
+        ]
 
     def sent_across(relation):
         return remote(
@@ -1502,19 +1634,34 @@
             a2a_send.at[relation - 1], a2a_recv.at[relation - 1], at.peer(relation),
         )
 
-    for slot in order:
-        relation = RELATIONS[slot // 2][slot % 2]
-        hop(slot, total - 2, True).wait_recv()
-        value = arrived[slot, total - 2].astype(F32) + term[slot].astype(F32)
+    for slot in far_slots:
+        relation = RELATIONS[slot // 2][0]
+        sum_into(stage.at[relation - 1], slot, total - 2, 4)
+        sent_across(relation).start()
+    send_on(near_slots, total - 2, near_place(total - 2))
+    vectors_far()
+    for slot in reversed(near_slots):
+        relation = RELATIONS[slot // 2][1]
+        base = near_place(total - 1)
         if relation == 0:
-            place(me, value)
+            hop(slot, total - 2, True).wait_recv()
+            place(
+                0,
+                lambda off, size: arrived[slot, total - 2, :, off : off + size].astype(F32)
+                + term[base + slot // 2, :, off : off + size].astype(F32),
+            )
         else:
-            stage[relation - 1] = value.astype(BF16)
+            sum_into(stage.at[relation - 1], slot, total - 2, base)
             sent_across(relation).start()
+    for relation in (2, 3, 1):
+        sent_across(relation).wait_recv()
+        place(relation, lambda off, size: landed[relation - 1, :, off : off + size].astype(F32))
     vectors_end()
-    for relation in (1, 2, 3):
-        sent_across(relation).wait_recv()
-        place(flip(me, relation), landed[relation - 1].astype(F32))
+    for relation in range(4):
+        for copy in stored(relation):
+            copy.wait()
+    for copy in (store_output, store_tokens):
+        copy.wait()
     for relation in (1, 2, 3):
         sent_across(relation).wait_send()
         near(relation).wait_send()
@@ -1526,7 +1673,7 @@
         row_copy(kind, 1).wait_send()
 
     def sent(step, carry):
-        for slot in order:
+        for slot in range(4):
             hop(slot, step, True).wait_send()
         return carry
 
@@ -1553,12 +1700,14 @@
         functools.partial(final_kernel, total),
         out_shape=[jax.ShapeDtypeStruct(s, d) for s, d in shapes],
         in_specs=[hbm] * 7 + [vmem] * 5,
-        out_specs=[vmem] * 5,
+        out_specs=[hbm] * 3 + [vmem] * 2,
         scratch_shapes=[
+            pltpu.VMEM((rows, width), BF16),
+            pltpu.VMEM((rows, width), BF16),
+            pltpu.VMEM((block, wide * GROUP), F32),
             pltpu.VMEM((count, wide), BF16),
             pltpu.VMEM(turned.shape, BF16),
-            pltpu.VMEM((4, block, wide), BF16),
-            pltpu.VMEM((4, block, wide), BF16),
+            pltpu.VMEM((10, block, wide), BF16),
             pltpu.VMEM((4, total - 1, block, wide), BF16),
             pltpu.VMEM((2, 256, wide), BF16),
             pltpu.VMEM((count, width), BF16),
@@ -1576,8 +1725,8 @@
             pltpu.VMEM((8, width // GROUP), F32),
             pltpu.VMEM((total - 1, 8, 128), F32),
             pltpu.VMEM((total - 1, 8, 128), F32),
-            dma((6,)), dma((2, 2)), dma((4, total - 1)), dma((4, total - 1)), dma((3,)), dma((3,)),
-            dma((2, 3)), dma((2, 3)), dma((3,)), dma((3,)), dma((2, total - 1)), dma((2, total - 1)),
+            dma((8,)), dma((2, 2)), dma((4, total - 1)), dma((4, total - 1)), dma((3,)), dma((3,)),
+            dma((2, 3)), dma((2, 3)), dma((GROUP, 8)), dma((6,)), dma((3,)), dma((3,)), dma((2, total - 1)), dma((2, total - 1)),
         ],
         compiler_params=pltpu.CompilerParams(
             collective_id=3, has_side_effects=True, vmem_limit_bytes=63 * MIB

time: 597 us -> 581 us (0.973)
  Pallas kernels: 570 us -> 555 us
    pallas_call x1, Pallas kernels: 150 us -> 143 us  [final(): pl.pallas_call(functools.partial(final_kernel, total), out_shape=[jax.Sha...]
where the time goes in v6:
time: 581 us; the launch traced here: 572 us
  Pallas kernels  555 us (96%)
  local copies, waits for them, and re-layouts  14.2 us (2%)
    pallas_call x1, Pallas kernels, forward(): pl.pallas_call(functools.partial(forward_kernel, total), out_shape=[jax.S...  276 us
    pallas_call x1, Pallas kernels, final(): pl.pallas_call(functools.partial(final_kernel, total), out_shape=[jax.Sha...  143 us
    pallas_call x1, Pallas kernels, backward(): pl.pallas_call(functools.partial(backward_kernel, total), out_shape=[jax....  135 us

profile of v6, /device:TPU:1, one launch (start us, length us, event | category | flops | bytes accessed | tf_op | source)
XLA Modules:
  0.0 572.0 jit_solution(18315972694040142854)
XLA Ops:
  0.7 0.7 bitcast_convert_fusion
  1.3 0.6 broadcast_in_dim.24.rates
  2.0 0.7 maximum_convert_fusion
  2.7 0.3 dynamic_update_slice.6
  3.1 0.0 copy-start.4
  3.1 0.7 pad_add_fusion
  3.8 0.6 broadcast_in_dim.26.seq_rows
  4.3 0.8 copy.26.seq_cols
  5.1 0.0 copy-done.4
  5.1 276.3 %forward_retention.1 = (bf16[2,2048,1536]{2,1,0:T(8,128)(2,1)}, bf16[4,8,64,1024]{3,2,1,0:T(8,128)(2,1)}, bf16[8,128,2048]{2,1,0:T(8,128)(2,1)}, bf16[8,128,2048...) custom-call(bf16[64,12288]{1,0:T(8,128)(2,1)} %w_in.1, ...), custom_call_target="tpu_custom_call" | custom-call | tf_op jit(solution)/shard_map/forward_retention/pallas_call | solution.py:780
  281.4 134.8 %backward_retention.1 = (f32[128,2048]{1,0:T(8,128)}, f32[64,4096]{1,0:T(8,128)}, f32[128,2048]{1,0:T(8,128)}, f32[256,2048]{1,0:T(8,128)}, bf16[4,256,2048]{2,1...) custom-call(bf16[1024,2048]{1,0:T(8,128)(2,1)} %bitcast.30, ...), custom_call_target="tpu_custom_call" | custom-call | tf_op jit(solution)/shard_map/backward_retention/pallas_call | solution.py:1239
  416.3 143.4 %final_sums.1 = (f32[64,12288]{1,0:T(8,128)}, bf16[256,2048]{1,0:T(8,128)(2,1)}, bf16[256,2048]{1,0:T(8,128)(2,1)}, f32[8,128]{1,0:T(8,128)}, f32[8,128]{1,0:T(8,128)}) custom-call(bf16[1024,3072]{1,0:T(8,128)(2,1)} %get-tuple-element.71.h_project, bf16[2,2048,1536]{2,1,0:T(8,128)(2,1)} %get-tuple-element.72.h_in, ...), custom_call_target="tpu_custom_call" | custom-call | tf_op jit(solution)/shard_map/final_sums/pallas_call | solution.py:1699
  559.7 0.0 copy-start
  559.7 1.3 slice_bitcast_fusion.2
  561.0 0.8 constant_dynamic-slice_fusion
  561.8 0.5 slice_bitcast_fusion
  562.3 2.3 copy.35
  564.6 0.0 copy-start.3
  564.6 2.4 copy.36
  567.0 0.0 copy-done
  567.0 0.0 copy-start.2
  567.0 0.0 copy-start.1
  567.0 1.7 copy.37
  568.7 0.0 copy-done.3
  568.7 1.0 copy.38
  569.6 0.0 copy-done.2
  569.6 1.0 copy.39
  570.6 0.0 copy-done.1
  570.6 1.0 copy.40
  (3 shorter events, 0.0 us)
Async XLA Ops:
  3.1 2.0 copy-start.4
  559.7 7.3 %copy-start = (f32[64,12288]{1,0:T(8,128)S(1)}, f32[64,12288]{1,0:T(8,128)}, u32[]{:S(2)}) copy-start(f32[64,12288]{1,0:T(8,128)} %get-tuple-element.106) | copy-start | bytes 9437188
  564.6 4.1 copy-start.3
  567.0 2.6 copy-start.2
  567.0 3.6 copy-start.1

commit v7 on v6

--- a/solution.py
+++ b/solution.py
@@ -256,22 +256,16 @@
         else:
             swap(relation, slot).wait_recv()
 
-    for h in range(heads):
-        for relation in (1, 0, 2, 3):
+    def start_head(h):
+        for relation in (0, 1, 2, 3):
             for slot in range(last):
                 if pieces[slot][2] == h:
                     swap(relation, slot).start()
-        if h == 0:
-            for relation in range(4):
-                swap(relation, last + 1).start()
-    for slot in (last + 2, last):
-        for relation in (1, 0, 2, 3):
-            swap(relation, slot).start()
+
+    start_head(0)
 
     fetch_cot = pltpu.make_async_copy(h_cot, cot, early_sem.at[0])
     fetch_tok = pltpu.make_async_copy(h_tok, tok, early_sem.at[1])
-    fetch_cot.start()
-    fetch_tok.start()
     early_stores = [
         pltpu.make_async_copy(src, dst, early_sem.at[2 + n])
         for n, (src, dst) in enumerate(
@@ -300,6 +294,15 @@
     for relation in (0, 1):
         await_head(0, relation)
         near[relation].begin()
+    fetch_cot.start()
+    fetch_tok.start()
+    for relation in (2, 3, 1, 0):
+        swap(relation, last + 1).start()
+    for slot in (last + 2, last):
+        for relation in (2, 3, 1, 0):
+            swap(relation, slot).start()
+    for h in range(1, heads):
+        start_head(h)
 
     def layout_of(b, down):
         shape = (rows, 1) if down else (1, rows)
@@ -1444,40 +1447,35 @@
 
 
     def terms(step, far_at, near_at, arriving=False):
-        lefts = []
-        for way in (0, 1):
-            which = at.behind(way, step + 1)
-            lefts.append(
-                jnp.concatenate(
-                    [
-                        turned[
-                            pl.ds(pl.multiple_of((flip(me, relation) * total + which) * block, block), block), :
-                        ]
-                        for relation in RELATIONS[way]
-                    ],
-                    axis=0,
-                )
-            )
-
-        def tile(n, way):
+        left = jnp.concatenate(
+            [
+                turned[
+                    pl.ds(
+                        pl.multiple_of((flip(me, relation) * total + at.behind(way, step + 1)) * block, block), block
+                    ),
+                    :,
+                ]
+                for way in (0, 1)
+                for relation in RELATIONS[way]
+            ],
+            axis=0,
+        )
+
+        def tile(n, carry):
             c = pl.ds(pl.multiple_of(n * wide, wide), wide)
-            value = dot(lefts[way], project[:, c]).astype(BF16)
-            term[far_at + way, :, c] = value[:block]
-            term[near_at + way, :, c] = value[block:]
+            value = dot(left, project[:, c]).astype(BF16)
+            for way in (0, 1):
+                first = 2 * way * block
+                term[far_at + way, :, c] = value[first : first + block]
+                term[near_at + way, :, c] = value[first + block : first + 2 * block]
+            return carry
 
         if arriving:
             for n, fetch in enumerate(fetch_project):
                 fetch.wait()
                 tile(n, 0)
-                tile(n, 1)
-            return
-        for way in (0, 1):
-
-            def some(n, carry, way=way):
-                tile(n, way)
-                return carry
-
-            lax.fori_loop(0, project.shape[1] // wide, some, 0)
+        else:
+            lax.fori_loop(0, project.shape[1] // wide, tile, 0)
 
     far_slots, near_slots = (0, 2), (1, 3)
 

time: 581 us -> 578 us (level)
  no operation moved by 1% of the time
where the time goes in v7:
time: 578 us; the launch traced here: 568 us
  Pallas kernels  550 us (95%)
  local copies, waits for them, and re-layouts  14.2 us (2%)
    pallas_call x1, Pallas kernels, forward(): pl.pallas_call(functools.partial(forward_kernel, total), out_shape=[jax.S...  276 us
    pallas_call x1, Pallas kernels, final(): pl.pallas_call(functools.partial(final_kernel, total), out_shape=[jax.Sha...  139 us
    pallas_call x1, Pallas kernels, backward(): pl.pallas_call(functools.partial(backward_kernel, total), out_shape=[jax....  135 us

profile of v7, /device:TPU:1, one launch (start us, length us, event | category | flops | bytes accessed | tf_op | source)
XLA Modules:
  0.0 567.7 jit_solution(16020613894446780109)
XLA Ops:
  0.7 0.7 bitcast_convert_fusion
  1.3 0.6 broadcast_in_dim.24.rates
  2.0 0.7 maximum_convert_fusion
  2.7 0.3 dynamic_update_slice.6
  3.1 0.0 copy-start.4
  3.1 0.7 pad_add_fusion
  3.8 0.6 broadcast_in_dim.26.seq_rows
  4.3 0.8 copy.26.seq_cols
  5.1 0.0 copy-done.4
  5.1 276.1 %forward_retention.1 = (bf16[2,2048,1536]{2,1,0:T(8,128)(2,1)}, bf16[4,8,64,1024]{3,2,1,0:T(8,128)(2,1)}, bf16[8,128,2048]{2,1,0:T(8,128)(2,1)}, bf16[8,128,2048...) custom-call(bf16[64,12288]{1,0:T(8,128)(2,1)} %w_in.1, ...), custom_call_target="tpu_custom_call" | custom-call | tf_op jit(solution)/shard_map/forward_retention/pallas_call | solution.py:783
  281.2 134.9 %backward_retention.1 = (f32[128,2048]{1,0:T(8,128)}, f32[64,4096]{1,0:T(8,128)}, f32[128,2048]{1,0:T(8,128)}, f32[256,2048]{1,0:T(8,128)}, bf16[4,256,2048]{2,1...) custom-call(bf16[1024,2048]{1,0:T(8,128)(2,1)} %bitcast.30, ...), custom_call_target="tpu_custom_call" | custom-call | tf_op jit(solution)/shard_map/backward_retention/pallas_call | solution.py:1242
  416.1 139.2 %final_sums.1 = (f32[64,12288]{1,0:T(8,128)}, bf16[256,2048]{1,0:T(8,128)(2,1)}, bf16[256,2048]{1,0:T(8,128)(2,1)}, f32[8,128]{1,0:T(8,128)}, f32[8,128]{1,0:T(8,128)}) custom-call(bf16[1024,3072]{1,0:T(8,128)(2,1)} %get-tuple-element.71.h_project, bf16[2,2048,1536]{2,1,0:T(8,128)(2,1)} %get-tuple-element.72.h_in, ...), custom_call_target="tpu_custom_call" | custom-call | tf_op jit(solution)/shard_map/final_sums/pallas_call | solution.py:1697
  555.3 0.0 copy-start
  555.3 1.3 slice_bitcast_fusion.2
  556.7 0.8 constant_dynamic-slice_fusion
  557.4 0.5 slice_bitcast_fusion
  558.0 2.3 copy.35
  560.3 0.0 copy-start.3
  560.3 2.4 copy.36
  562.7 0.0 copy-done
  562.7 0.0 copy-start.2
  562.7 0.0 copy-start.1
  562.7 1.7 copy.37
  564.3 0.0 copy-done.3
  564.3 1.0 copy.38
  565.3 0.0 copy-done.2
  565.3 1.0 copy.39
  566.3 0.0 copy-done.1
  566.3 1.0 copy.40
  (3 shorter events, 0.0 us)
Async XLA Ops:
  3.1 2.0 copy-start.4
  555.3 7.3 %copy-start = (f32[64,12288]{1,0:T(8,128)S(1)}, f32[64,12288]{1,0:T(8,128)}, u32[]{:S(2)}) copy-start(f32[64,12288]{1,0:T(8,128)} %get-tuple-element.106) | copy-start | bytes 9437188
  560.3 4.1 copy-start.3
  562.7 2.6 copy-start.2
  562.7 3.6 copy-start.1

commit v8 on v7

--- a/solution.py
+++ b/solution.py
@@ -1611,7 +1611,7 @@
         for base, stride, h, off, size in pieces:
             start = pl.multiple_of(base + other * stride, 128)
             off = h * part_width + off
-            full_rows[:, pl.ds(start, size)] = columns_of(off, size)
+            full_rows[:, pl.ds(start, size)] = columns_of(off, size).astype(BF16)
         for copy in stored(relation):
             copy.start()
 
@@ -1653,7 +1653,7 @@
             sent_across(relation).start()
     for relation in (2, 3, 1):
         sent_across(relation).wait_recv()
-        place(relation, lambda off, size: landed[relation - 1, :, off : off + size].astype(F32))
+        place(relation, lambda off, size: landed[relation - 1, :, off : off + size])
     vectors_end()
     for relation in range(4):
         for copy in stored(relation):
@@ -1688,7 +1688,7 @@
     dma = pltpu.SemaphoreType.DMA
     group_width = d_group.shape[0] * d_group.shape[2]
     shapes = (
-        ((block, wide * GROUP), F32),
+        ((block, wide * GROUP), BF16),
         ((rows, width), BF16),
         ((rows, width), BF16),
         ((8, 128), F32),
@@ -1702,7 +1702,7 @@
         scratch_shapes=[
             pltpu.VMEM((rows, width), BF16),
             pltpu.VMEM((rows, width), BF16),
-            pltpu.VMEM((block, wide * GROUP), F32),
+            pltpu.VMEM((block, wide * GROUP), BF16),
             pltpu.VMEM((count, wide), BF16),
             pltpu.VMEM(turned.shape, BF16),
             pltpu.VMEM((10, block, wide), BF16),
@@ -1793,7 +1793,7 @@
     return (
         output,
         d_tokens,
-        grad_in,
+        grad_in.astype(F32),
         grad_out,
         grad_up,
         grad_down,

time: 578 us -> 577 us (level)
  no operation moved by 1% of the time
where the time goes in v8:
time: 577 us; the launch traced here: 566 us
  Pallas kernels  550 us (95%)
  local copies, waits for them, and re-layouts  9.8 us (2%)
    pallas_call x1, Pallas kernels, forward(): pl.pallas_call(functools.partial(forward_kernel, total), out_shape=[jax.S...  276 us
    pallas_call x1, Pallas kernels, final(): pl.pallas_call(functools.partial(final_kernel, total), out_shape=[jax.Sha...  139 us
    pallas_call x1, Pallas kernels, backward(): pl.pallas_call(functools.partial(backward_kernel, total), out_shape=[jax....  135 us

profile of v8, /device:TPU:1, one launch (start us, length us, event | category | flops | bytes accessed | tf_op | source)
XLA Modules:
  0.0 566.4 jit_solution(15589421609439222240)
XLA Ops:
  0.7 0.7 bitcast_convert_fusion
  1.3 0.6 broadcast_in_dim.24.rates
  2.0 0.7 maximum_convert_fusion
  2.7 0.3 dynamic_update_slice.6
  3.1 0.0 copy-start.5
  3.1 0.7 pad_add_fusion
  3.8 0.6 broadcast_in_dim.26.seq_rows
  4.3 0.8 copy.26.seq_cols
  5.1 0.0 copy-done.5
  5.1 276.1 %forward_retention.1 = (bf16[2,2048,1536]{2,1,0:T(8,128)(2,1)}, bf16[4,8,64,1024]{3,2,1,0:T(8,128)(2,1)}, bf16[8,128,2048]{2,1,0:T(8,128)(2,1)}, bf16[8,128,2048...) custom-call(bf16[64,12288]{1,0:T(8,128)(2,1)} %w_in.1, ...), custom_call_target="tpu_custom_call" | custom-call | tf_op jit(solution)/shard_map/forward_retention/pallas_call | solution.py:783
  281.2 134.9 %backward_retention.1 = (f32[128,2048]{1,0:T(8,128)}, f32[64,4096]{1,0:T(8,128)}, f32[128,2048]{1,0:T(8,128)}, f32[256,2048]{1,0:T(8,128)}, bf16[4,256,2048]{2,1...) custom-call(bf16[1024,2048]{1,0:T(8,128)(2,1)} %bitcast.30, ...), custom_call_target="tpu_custom_call" | custom-call | tf_op jit(solution)/shard_map/backward_retention/pallas_call | solution.py:1242
  416.1 139.0 %final_sums.1 = (bf16[64,12288]{1,0:T(8,128)(2,1)}, bf16[256,2048]{1,0:T(8,128)(2,1)}, bf16[256,2048]{1,0:T(8,128)(2,1)}, f32[8,128]{1,0:T(8,128)}, f32[8,128]{1,0:T(8,128)}) custom-call(bf16[1024,3072]{1,0:T(8,128)(2,1)} %get-tuple-element.71.h_project, bf16[2,2048,1536]{2,1,0:T(8,128)(2,1)} %get-tuple-element.72.h_in, ...), custom_call_target="tpu_custom_call" | custom-call | tf_op jit(solution)/shard_map/final_sums/pallas_call | solution.py:1697
  555.1 0.0 copy-start.4
  555.1 0.0 copy-start.3
  555.2 1.3 slice_bitcast_fusion.2
  556.5 0.7 constant_dynamic-slice_fusion
  557.2 0.5 slice_bitcast_fusion
  557.8 0.0 copy-start.2
  557.8 3.4 convert_element_type.16
  561.1 0.0 copy-done.4
  561.1 0.0 copy-start.1
  561.1 0.0 copy-start
  561.1 1.0 copy.34
  562.1 0.0 copy-done.3
  562.1 1.0 copy.35
  563.1 0.0 copy-done.2
  563.1 1.0 copy.36
  564.0 0.0 copy-done.1
  564.0 1.0 copy.37
  565.0 0.0 copy-done
  565.0 1.0 copy.38
  (3 shorter events, 0.0 us)
Async XLA Ops:
  3.1 2.0 copy-start.5
  555.1 6.0 %copy-start.4 = (bf16[256,2048]{1,0:T(8,128)(2,1)S(1)}, bf16[256,2048]{1,0:T(8,128)(2,1)}, u32[]{:S(2)}) copy-start(bf16[256,2048]{1,0:T(8,128)(2,1)} %get-tuple-element.104) | copy-start | bytes 3145732
  555.1 7.0 %copy-start.3 = (bf16[256,2048]{1,0:T(8,128)(2,1)S(1)}, bf16[256,2048]{1,0:T(8,128)(2,1)}, u32[]{:S(2)}) copy-start(bf16[256,2048]{1,0:T(8,128)(2,1)} %get-tuple-element.105) | copy-start | bytes 3145732
  557.8 5.3 copy-start.2
  561.1 2.9 copy-start.1
  561.1 3.9 copy-start
